TPU v7x, 128 devices: a whole 4x4x4 slice. The times are simulated.
128 devices in a mesh: reader: 8 (over x_hi, y), blk: 16 (over z, x_lo, core).
Axes of the slice: x: 4 (x_hi: 2, x_lo: 2; x = x_hi * 2 + x_lo), y: 4, z: 4, core: 2. Of those that a mesh axis runs over, the one named last changes fastest.
Arguments:
- features: bfloat16 [16384, 512], P(('reader', 'blk')), may hold values from -40 to 40
- cotangent: bfloat16 [16384, 512], P(('reader', 'blk')), may hold values from -6 to 6
- w_query: bfloat16 [512, 512], replicated, may hold values from -0.25 to 0.25
- w_key: bfloat16 [512, 512], replicated, may hold values from -0.25 to 0.25
- w_value: bfloat16 [512, 512], replicated, may hold values from -0.25 to 0.25
- tile_coords: int32 [8, 16, 32, 3], P('reader', 'blk'), may hold values from 0 to 239, as said below
- tile_count: int32 [8, 16], P('reader', 'blk'), may hold values from 4 to 32, as said below
- mask_table: int32 [240, 128, 4], replicated, may hold values from -2147483648 to 2147483647, as said below
Outputs:
- attn_out: bfloat16 [16384, 512], P(('reader', 'blk'))
- grad_features: bfloat16 [16384, 512], P(('reader', 'blk'))
Inputs may be any that keep to these rules, and one draw needn't show every extreme that they name: `tile_coords`: for every r and b the 32 slots name distinct (qb, kb) pairs with qb < 16, kb < 8, p < 240; the first 1 slots are the tiles in which the nodes of segment r * 16 + b meet themselves. `tile_count`: some pair (r, b) uses all 32 slots, and some pair uses the fewest. `mask_table`: each word packs 32 edge bits as a signed int32; each bit is set with probability 1/32.
All inputs are finite; a program needn't handle non-finite values.
Results may differ from a plain program's by a relative error of at most 0.01265.
The roundings to bfloat16 on the way count: a program that leaves them out, or rounds other values in their place, can miss the bound.
Values may be sent and summed in bfloat16 or wider, within the bound.
A program may use at most 128 MiB of HBM per device.

v0:
```python
import jax
import jax.numpy as jnp
from jax import lax
from jax.sharding import PartitionSpec as P

HEADS = 8


NEG_FILL = -1e30


def unpack(mask_words):
    shifts = jnp.arange(32, dtype=jnp.int32)
    mask_bits = jnp.right_shift(mask_words[..., None], shifts) & 1
    return mask_bits.reshape(mask_words.shape[:-1] + (mask_words.shape[-1] * 32,)) > 0


def project(rows, weight):
    return jnp.dot(rows, weight, preferred_element_type=jnp.float32).astype(jnp.bfloat16)


def local(features, cotangent, w_query, w_key, w_value, tile_coords, tile_count, mask_table):
    rows_own, model_width = features.shape
    block_size = mask_table.shape[1]
    head_dim = model_width // HEADS
    scale = float(head_dim) ** (-0.5)
    seg_count = rows_own // block_size
    query_count = lax.axis_size("blk") * seg_count
    key_count = lax.axis_size("reader") * seg_count
    blk_index = lax.axis_index("blk")
    reader_index = lax.axis_index("reader")
    queries = project(features, w_query)
    query_rows, grad_rows = (
        lax.all_gather(queries, "blk", axis=0, tiled=True),
        lax.all_gather(cotangent, "blk", axis=0, tiled=True),
    )
    key_rows, value_rows = (
        lax.all_gather(project(features, w_key), "reader", axis=0, tiled=True),
        lax.all_gather(project(features, w_value), "reader", axis=0, tiled=True),
    )
    query_tiles = query_rows.reshape(query_count, block_size, HEADS, head_dim)
    grad_tiles = grad_rows.reshape(query_count, block_size, HEADS, head_dim)
    key_tiles = key_rows.reshape(key_count, block_size, HEADS, head_dim)
    value_tiles = value_rows.reshape(key_count, block_size, HEADS, head_dim)
    coords = tile_coords.reshape(-1, 3)
    tile_total = tile_count.reshape(-1)[0]
    batch_size = 8
    turns = (tile_total + batch_size - 1) // batch_size
    diagonal_cells = jnp.eye(block_size, dtype=bool)

    def tile_scores(turn_index):
        picked = lax.dynamic_slice_in_dim(coords, turn_index * batch_size, batch_size, 0)
        query_blk = picked[:, 0]
        key_blk = picked[:, 1]
        usable = turn_index * batch_size + jnp.arange(batch_size, dtype=jnp.int32) < tile_total
        on_diag = (
            (query_blk // seg_count == blk_index)
            & (key_blk // seg_count == reader_index)
            & (query_blk % seg_count == key_blk % seg_count)
        )
        allowed = (
            unpack(mask_table[picked[:, 2]]) | on_diag[:, None, None] & diagonal_cells
        ) & usable[:, None, None]
        scores = (
            jnp.einsum(
                "gqhd,gkhd->ghqk",
                query_tiles[query_blk],
                key_tiles[key_blk],
                preferred_element_type=jnp.float32,
            )
            * scale
        )
        return (query_blk, key_blk, allowed[:, None], scores)

    def max_turn(turn_index, local_max):
        query_blk, key_blk, allowed, scores = tile_scores(turn_index)
        tile_max = jnp.max(jnp.where(allowed, scores, NEG_FILL), axis=-1)
        return local_max.at[query_blk].max(tile_max)

    local_max = lax.fori_loop(
        0, turns, max_turn, jnp.full((query_count, HEADS, block_size), NEG_FILL, jnp.float32)
    )
    row_max = lax.pmax(local_max, "blk")

    def sum_turn(turn_index, state_now):
        totals, weighted = state_now
        query_blk, key_blk, allowed, scores = tile_scores(turn_index)
        expo = jnp.exp(jnp.where(allowed, scores - row_max[query_blk][..., None], NEG_FILL))
        totals = totals.at[query_blk].add(jnp.sum(expo, axis=-1))
        products = jnp.einsum(
            "ghqk,gkhd->gqhd",
            expo.astype(jnp.bfloat16),
            value_tiles[key_blk],
            preferred_element_type=jnp.float32,
        )
        return (totals, weighted.at[query_blk].add(products))

    start_sums = (
        jnp.zeros((query_count, HEADS, block_size), jnp.float32),
        jnp.zeros((query_count, block_size, HEADS, head_dim), jnp.float32),
    )
    totals, weighted = lax.fori_loop(0, turns, sum_turn, start_sums)
    weighted_all, totals_all = lax.psum((weighted, totals), "blk")
    outputs = weighted_all / totals_all.transpose(0, 2, 1)[..., None]
    delta_all = jnp.sum(grad_tiles.astype(jnp.float32) * outputs, axis=-1).transpose(0, 2, 1)
    outputs_own = lax.dynamic_slice_in_dim(
        outputs.reshape(query_count * block_size, model_width), blk_index * rows_own, rows_own, 0
    )
    attn_out = outputs_own.astype(jnp.bfloat16)

    def grad_turn(turn_index, state_now):
        grad_query, grad_key, grad_value = state_now
        query_blk, key_blk, allowed, scores = tile_scores(turn_index)
        probs = (
            jnp.exp(jnp.where(allowed, scores - row_max[query_blk][..., None], NEG_FILL))
            / totals_all[query_blk][..., None]
        )
        d_rows = grad_tiles[query_blk]
        grad_value = grad_value.at[key_blk].add(
            jnp.einsum(
                "ghqk,gqhd->gkhd",
                probs.astype(jnp.bfloat16),
                d_rows,
                preferred_element_type=jnp.float32,
            )
        )
        d_probs = jnp.einsum(
            "gqhd,gkhd->ghqk", d_rows, value_tiles[key_blk], preferred_element_type=jnp.float32
        )
        d_scores = (probs * (d_probs - delta_all[query_blk][..., None]) * scale).astype(
            jnp.bfloat16
        )
        grad_query = grad_query.at[query_blk].add(
            jnp.einsum(
                "ghqk,gkhd->gqhd", d_scores, key_tiles[key_blk], preferred_element_type=jnp.float32
            )
        )
        grad_key = grad_key.at[key_blk].add(
            jnp.einsum(
                "ghqk,gqhd->gkhd",
                d_scores,
                query_tiles[query_blk],
                preferred_element_type=jnp.float32,
            )
        )
        return (grad_query, grad_key, grad_value)

    start_grads = (
        jnp.zeros((query_count, block_size, HEADS, head_dim), jnp.float32),
        jnp.zeros((key_count, block_size, HEADS, head_dim), jnp.float32),
        jnp.zeros((key_count, block_size, HEADS, head_dim), jnp.float32),
    )
    grad_query, grad_key, grad_value = lax.fori_loop(0, turns, grad_turn, start_grads)
    query_own = lax.psum_scatter(
        grad_query.reshape(query_count * block_size, model_width),
        "blk",
        scatter_dimension=0,
        tiled=True,
    )
    key_own, value_own = (
        lax.psum_scatter(
            grad_key.reshape(key_count * block_size, model_width),
            "reader",
            scatter_dimension=0,
            tiled=True,
        ),
        lax.psum_scatter(
            grad_value.reshape(key_count * block_size, model_width),
            "reader",
            scatter_dimension=0,
            tiled=True,
        ),
    )
    grad_total = jnp.dot(
        query_own.astype(jnp.bfloat16), w_query.T, preferred_element_type=jnp.float32
    )
    grad_total = grad_total + jnp.dot(
        key_own.astype(jnp.bfloat16), w_key.T, preferred_element_type=jnp.float32
    )
    grad_total = grad_total + jnp.dot(
        value_own.astype(jnp.bfloat16), w_value.T, preferred_element_type=jnp.float32
    )
    return (attn_out, grad_total.astype(jnp.bfloat16))


def solution(mesh):
    return jax.shard_map(
        local,
        mesh=mesh,
        in_specs=(
            P(("reader", "blk"), None),
            P(("reader", "blk"), None),
            P(),
            P(),
            P(),
            P("reader", "blk", None, None),
            P("reader", "blk"),
            P(),
        ),
        out_specs=(P(("reader", "blk"), None), P(("reader", "blk"), None)),
        check_vma=False,
    )
```

profile of v0, /device:TPU:0, one launch (start us, length us, event | category | flops | bytes accessed | tf_op | source)
XLA Modules:
  0.0 994.2 jit_solution(10596690257573810664)
XLA Ops:
  14.0 45.7 %all-gather.7.cloned.1.call-done = bf16[1024,512]{1,0:T(8,128)(2,1)} async-done(((bf16[128,512]{1,0:T(8,128)(2,1)}), bf16[1024,512]{1,0:T(8,128)(2,1)}) %all-gather.7.cloned.1.call-update) | async-done | bytes 1048592 | tf_op jit(solution)/shard_map/all_gather | solution.py:38
  62.5 32.6 %all-gather.5.cloned.1.call-done = bf16[2048,512]{1,0:T(8,128)(2,1)} async-done(((bf16[128,512]{1,0:T(8,128)(2,1)}), bf16[2048,512]{1,0:T(8,128)(2,1)}) %all-gather.5.cloned.1.call-update) | async-done | bytes 2097168 | tf_op jit(solution)/shard_map/all_gather | solution.py:34
  95.1 6.2 reshape.610
  101.2 25.9 %while.48 = (s32[]{:T(128)}, f32[16,8,128]{2,1,0:T(8,128)S(1)}, s32[]{:T(128)}, s32[32,3]{0,1:T(4,128)S(1)}, s32[240,128,4]{1,2,0:T(4,128)S(1)}, /*index=5*/s32[...) while((s32[]{:T(128)}, f32[16,8,128]{2,1,0:T(8,128)S(1)}, ...), condition=%wide.region_3.4_spmd.clone, body=%wide.region_0.3_spmd.clone.sunk | while | flops 138169456 | bytes 6781831 | solution.py:80
  128.4 15.0 %all-gather.9.cloned.1.call-done = bf16[1024,512]{1,0:T(8,128)(2,1)} async-done(((bf16[128,512]{1,0:T(8,128)(2,1)}), bf16[1024,512]{1,0:T(8,128)(2,1)}) %all-gather.9.cloned.1.call-update) | async-done | bytes 1048592 | tf_op jit(solution)/shard_map/all_gather | solution.py:39
  147.4 109.5 %all-reduce.4.cloned.1.call-done = f32[16,8,128]{2,1,0:T(8,128)} async-done(((f32[16,8,128]{2,1,0:T(8,128)}), f32[16,8,128]{2,1,0:T(8,128)}) %all-reduce.4.cloned.1.call-update) | async-done | bytes 65552 | tf_op jit(solution)/shard_map/pmax | solution.py:83
  259.4 50.4 %while.49 = (s32[]{:T(128)}, f32[16,8,128]{2,1,0:T(8,128)S(1)}, f32[16,128,8,64]{1,3,2,0:T(8,128)}, s32[]{:T(128)}, s32[32,3]{0,1:T(4,128)S(1)}, /*index=5*/s32[...) while((s32[]{:T(128)}, f32[16,8,128]{2,1,0:T(8,128)S(1)}, ...), condition=%wide.region_9.10_spmd.clone, body=%wide.region_5.9_spmd.clone.sunk | while | flops 278154368 | bytes 31161372 | solution.py:102
  279.4 5.0 scatter_fusion.2
  304.5 5.0 scatter_fusion.2
  309.8 6.5 copy.81
  324.0 5.3 copy.86
  329.2 169.5 %all-reduce.6.cloned.1.call-done = (f32[16,128,8,64]{1,0,3,2:T(8,128)}, f32[16,8,128]{2,1,0:T(8,128)}) async-done(((f32[16,128,8,64]{1,0,3,2:T(8,128)}, f32[16,8,128]{2,1,0:T(8,128)}), (f32[16,128,8,64]{1,0,3,2:T(8,128)}, f32[16,8,128]{2,1,0:T(8,128)})) %all-reduce.6.cloned.1.call-update) | async-done | bytes 4259856 | tf_op jit(solution)/shard_map/psum | solution.py:103
  499.6 4.8 multiply_reduce_fusion
  510.1 122.0 %while.50 = (s32[]{:T(128)}, f32[16,128,8,64]{1,3,2,0:T(8,128)}, f32[8,128,8,64]{1,3,2,0:T(8,128)}, f32[8,128,8,64]{1,3,2,0:T(8,128)}, s32[]{:T(128)}, /*index=5...) while((s32[]{:T(128)}, f32[16,128,8,64]{1,3,2,0:T(8,128)}, ...), condition=%wide.region_17.18_spmd.clone, body=%wide.region_13.17_spmd.clone.sunk | while | flops 682904704 | bytes 88493080 | solution.py:153
  539.3 4.7 exponential_divide_fusion.2
  549.3 4.9 scatter_fusion.5
  561.2 4.9 scatter_fusion.4
  566.0 4.9 scatter_fusion.3
  610.2 4.9 scatter_fusion.5
  622.1 4.9 scatter_fusion.4
  627.1 4.9 scatter_fusion.3
  652.8 176.6 %reduce-scatter.4.cloned.1.call-done = f32[128,512]{0,1:T(8,128)} async-done(((f32[2048,512]{0,1:T(8,128)}), f32[128,512]{0,1:T(8,128)}) %reduce-scatter.4.cloned.1.call-update) | async-done | bytes 262160 | tf_op jit(solution)/shard_map/reduce_scatter | solution.py:154
  830.6 77.1 %reduce-scatter.6.cloned.1.call-done = f32[128,512]{0,1:T(8,128)} async-done(((f32[1024,512]{0,1:T(8,128)}), f32[128,512]{0,1:T(8,128)}) %reduce-scatter.6.cloned.1.call-update) | async-done | bytes 262160 | tf_op jit(solution)/shard_map/reduce_scatter | solution.py:161
  909.0 76.6 %reduce-scatter.8.cloned.1.call-done = f32[128,512]{0,1:T(8,128)} async-done(((f32[1024,512]{0,1:T(8,128)}), f32[128,512]{0,1:T(8,128)}) %reduce-scatter.8.cloned.1.call-update) | async-done | bytes 262160 | tf_op jit(solution)/shard_map/reduce_scatter | solution.py:167
  (244 shorter events, 208.9 us)
Async XLA Ops:
  7.2 6.8 copy-start.24
  7.2 52.5 %all-gather.7.cloned.1.call-start = ((), (), s32[]{:S(2)}) async-start(), calls=%async_computation.4 | async-start | bytes 1179648 | tf_op jit(solution)/shard_map/all_gather | solution.py:38
  9.3 85.7 %all-gather.5.cloned.1.call-start = ((), (), s32[]{:S(2)}) async-start(), calls=%async_computation.3 | async-start | bytes 2228224 | tf_op jit(solution)/shard_map/all_gather | solution.py:34
  11.2 132.3 %all-gather.9.cloned.1.call-start = ((), (), s32[]{:S(2)}) async-start(), calls=%async_computation.6 | async-start | bytes 1179648 | tf_op jit(solution)/shard_map/all_gather | solution.py:39
  13.3 243.6 %all-reduce.4.cloned.1.call-start = ((), (), s32[]{:S(2)}) async-start(), calls=%async_computation.5 | async-start | bytes 131072 | tf_op jit(solution)/shard_map/pmax | solution.py:83
  62.5 38.7 %copy-start.5 = (s32[240,128,4]{1,2,0:T(4,128)S(1)}, s32[240,128,4]{1,2,0:T(4,128)}, u32[]{:S(2)}) copy-start(s32[240,128,4]{1,2,0:T(4,128)} %param.21) | copy-start | bytes 1474564
  127.8 188.7 %all-gather.11.cloned.1.call-start = ((), (), s32[]{:S(2)}) async-start(), calls=%async_computation.7 | async-start | bytes 2228224 | tf_op jit(solution)/shard_map/all_gather | solution.py:35
  128.4 370.3 %all-reduce.6.cloned.1.call-start = ((), (), s32[]{:S(2)}) async-start(), calls=%async_computation.11 | async-start | bytes 8519680 | tf_op jit(solution)/shard_map/psum | solution.py:103
  309.8 6.5 copy-start.13
  316.4 513.0 %reduce-scatter.4.cloned.1.call-start = ((), (), s32[]{:S(2)}) async-start(), calls=%async_computation.8 | async-start | bytes 4456448 | tf_op jit(solution)/shard_map/reduce_scatter | solution.py:154
  539.3 4.7 copy-start.2
  539.3 4.7 copy-start.4
  561.2 4.9 copy-start.23
  566.0 4.9 copy-start.16
  566.0 4.9 copy-start.18
  600.2 4.7 copy-start.2
  600.2 4.7 copy-start.4
  622.1 4.9 copy-start.23
  627.1 4.9 copy-start.16
  627.1 4.9 copy-start.18
  640.6 267.1 %reduce-scatter.6.cloned.1.call-start = ((), (), s32[]{:S(2)}) async-start(), calls=%async_computation.9 | async-start | bytes 2359296 | tf_op jit(solution)/shard_map/reduce_scatter | solution.py:161
  645.2 340.4 %reduce-scatter.8.cloned.1.call-start = ((), (), s32[]{:S(2)}) async-start(), calls=%async_computation.10 | async-start | bytes 2359296 | tf_op jit(solution)/shard_map/reduce_scatter | solution.py:167
  651.4 256.3 %copy-start.10 = (bf16[512,512]{1,0:T(8,128)(2,1)S(1)}, bf16[512,512]{1,0:T(8,128)(2,1)}, u32[]{:S(2)}) copy-start(bf16[512,512]{1,0:T(8,128)(2,1)} %param.17) | copy-start | bytes 1572868
  652.0 333.6 %copy-start.11 = (bf16[512,512]{1,0:T(8,128)(2,1)S(1)}, bf16[512,512]{1,0:T(8,128)(2,1)}, u32[]{:S(2)}) copy-start(bf16[512,512]{1,0:T(8,128)(2,1)} %param.18) | copy-start | bytes 1572868
  (24 other events, 73.1 us)
Sparse Core Ops, SparseCore 0:
  11.0 48.6 all-gather.6
  62.0 33.0 all-gather.4
  97.4 46.0 all-gather.8
  146.4 110.4 all-reduce.3
  258.5 32.9 all-gather.10
  316.5 182.1 all-reduce.5
  640.7 188.5 reduce-scatter.3
  833.5 74.1 reduce-scatter.5
  911.9 73.6 reduce-scatter.7
where the time goes:
time: 1010 us; the launch traced here: 994 us
  waiting for transfers between devices  703 us (70%)
  local copies, waits for them, and re-layouts  155 us (15%)
  matrix products  64.9 us (6%)
  other arithmetic  54.5 us (5%)
  between operations  14.9 us (1%)
    reduce_scatter x1, waiting for transfers between devices, local(): lax.psum_scatter(grad_query.reshape(query_count * block_size, model_width...  177 us
    psum x1, waiting for transfers between devices, local(): weighted_all, totals_all = lax.psum((weighted, totals), 'blk')  169 us
    pmax x1, waiting for transfers between devices, local(): row_max = lax.pmax(local_max, 'blk')  109 us
    reduce_scatter x1, waiting for transfers between devices, local(): lax.psum_scatter(grad_key.reshape(key_count * block_size, model_width), '...  77.1 us
    reduce_scatter x1, waiting for transfers between devices, local(): lax.psum_scatter(grad_value.reshape(key_count * block_size, model_width),...  76.6 us
    all_gather x1, waiting for transfers between devices, local(): lax.all_gather(project(features, w_key), 'reader', axis=0, tiled=True)  45.7 us
    all_gather x1, waiting for transfers between devices, local(): lax.all_gather(queries, 'blk', axis=0, tiled=True)  32.6 us
    gather x8, local copies, waits for them, and re-layouts, tile_scores(): query_tiles[query_blk]  32.4 us
  transfers between devices with their start and end apart: 9, of which 8 were waited for; matrix products, arithmetic and copies ran while one was open for 12% of the time, Pallas kernels for 0%

commit v1 on v0

v1 whole, which is shorter than its diff:
```python
import functools

import jax
import jax.numpy as jnp
from jax import lax
from jax.experimental import pallas as pl
from jax.experimental.pallas import tpu as pltpu
from jax.sharding import PartitionSpec as P

HEADS = 8
HEAD_DIM = 64
D = 512
BLOCK = 128
SCALE = 0.125
FLOOR = -1e20
NEG_FILL = -1e30
MESH = pl.DeviceIdType.MESH
F32 = jnp.float32
BF16 = jnp.bfloat16
VMEM = pltpu.VMEM


def dot(a, b):
    return jnp.dot(a, b, preferred_element_type=F32)


def dot_nt(a, b):
    return lax.dot_general(a, b, (((1,), (1,)), ((), ())), preferred_element_type=F32)


def greet(devices):
    barrier = pltpu.get_barrier_semaphore()
    for device in devices:
        pl.semaphore_signal(barrier, inc=1, device_id=device, device_id_type=MESH)
    pl.semaphore_wait(barrier, len(devices))


def gather_kernel(
    nb, nr, x_ref, g_ref, wq_ref, wk_ref, wv_ref,
    qg_ref, k_ref, v_ref, kt_ref, vt_ref,
    own, xs, psend, precv, rsend, rrecv, ssend, srecv, lsem,
):
    reader, blk = lax.axis_index("reader"), lax.axis_index("blk")
    sib = blk + 1 - 2 * lax.rem(blk, 2)
    half = nb // 2
    peer = lambda d: lax.rem(blk + 2 * d, nb)
    source = lambda d: lax.rem(blk + nb - 2 * d, nb)
    rpeer = lambda d: lax.rem(reader + d, nr)
    rsource = lambda d: lax.rem(reader + nr - d, nr)

    greet(
        [(reader, peer(d)) for d in range(1, half)]
        + [(rpeer(d), blk) for d in range(1, nr)]
        + [(reader, sib)]
    )

    def feature_copy(d):
        return pltpu.make_async_remote_copy(
            src_ref=x_ref, dst_ref=xs.at[d], send_sem=rsend.at[d], recv_sem=rrecv.at[d],
            device_id=(rpeer(d), blk), device_id_type=MESH,
        )

    def peer_copy(d):
        return pltpu.make_async_remote_copy(
            src_ref=own, dst_ref=qg_ref.at[blk], send_sem=psend.at[d], recv_sem=precv.at[d],
            device_id=(reader, peer(d)), device_id_type=MESH,
        )

    def arrival(d):
        return pltpu.make_async_remote_copy(
            src_ref=own, dst_ref=qg_ref.at[source(d)], send_sem=psend.at[d], recv_sem=precv.at[d],
            device_id=(reader, peer(d)), device_id_type=MESH,
        )

    def relay(d, src=None):
        at = source(d)
        return pltpu.make_async_remote_copy(
            src_ref=qg_ref.at[at] if src is None else src, dst_ref=qg_ref.at[at],
            send_sem=ssend.at[d], recv_sem=srecv.at[d],
            device_id=(reader, sib), device_id_type=MESH,
        )

    def relay_arrival(d):
        at = lax.rem(sib + nb - 2 * d, nb)
        return pltpu.make_async_remote_copy(
            src_ref=own, dst_ref=qg_ref.at[at],
            send_sem=ssend.at[d], recv_sem=srecv.at[d],
            device_id=(reader, sib), device_id_type=MESH,
        )

    for d in range(1, nr):
        feature_copy(d).start()
    own[D:] = g_ref[...].astype(F32).T.astype(BF16)
    q = dot(x_ref[...], wq_ref[...]).astype(BF16).astype(F32) * SCALE
    own[:D] = q.T.astype(BF16)
    for d in range(1, half):
        peer_copy(d).start()
    relay(0, own).start()
    keep = pltpu.make_async_copy(own, qg_ref.at[blk], lsem)
    keep.start()

    def project(at, rows):
        k = dot(rows, wk_ref[...])
        k_ref[at] = k.astype(BF16)
        kt_ref[at] = k.T.astype(BF16)
        v = dot(rows, wv_ref[...])
        v_ref[at] = v.astype(BF16)
        vt_ref[at] = v.T.astype(BF16)

    project(reader, x_ref[...])

    def reader_step(d, carry):
        feature_copy(d).wait_recv()
        project(rsource(d), xs[d])
        return carry

    lax.fori_loop(1, nr, reader_step, 0)

    def relay_step(d, carry):
        arrival(d).wait_recv()
        relay(d).start()
        return carry

    lax.fori_loop(1, half, relay_step, 0)

    def relay_done(d, carry):
        relay_arrival(d).wait_recv()
        relay(d).wait_send()
        return carry

    lax.fori_loop(1, half, relay_done, 0)
    relay_arrival(0).wait_recv()
    relay(0, own).wait_send()
    keep.wait()
    for d in range(1, nr):
        feature_copy(d).wait_send()
    for d in range(1, half):
        peer_copy(d).wait_send()


def gather(features, cotangent, w_query, w_key, w_value):
    nb, nr = lax.axis_size("blk"), lax.axis_size("reader")
    rows = pl.BlockSpec(memory_space=VMEM)
    sems = [pltpu.SemaphoreType.DMA((n,)) for n in (nb // 2, nb // 2, nr, nr, nb // 2, nb // 2)]
    return pl.pallas_call(
        functools.partial(gather_kernel, nb, nr),
        out_shape=[
            jax.ShapeDtypeStruct((nb, 2 * D, BLOCK), BF16),
            jax.ShapeDtypeStruct((nr, BLOCK, D), BF16),
            jax.ShapeDtypeStruct((nr, BLOCK, D), BF16),
            jax.ShapeDtypeStruct((nr, D, BLOCK), BF16),
            jax.ShapeDtypeStruct((nr, D, BLOCK), BF16),
        ],
        in_specs=[rows] * 5,
        out_specs=[pl.BlockSpec(memory_space=pl.ANY)] + [rows] * 4,
        scratch_shapes=[
            VMEM((2 * D, BLOCK), BF16),
            VMEM((nr, BLOCK, D), BF16),
            *sems,
            pltpu.SemaphoreType.DMA,
        ],
        compiler_params=pltpu.CompilerParams(
            collective_id=0, has_side_effects=True, vmem_limit_bytes=48 * 2**20
        ),
        name="gather",
    )(features, cotangent, w_query, w_key, w_value)


def tile_bias(words, first):
    spread = jnp.concatenate(
        [jnp.broadcast_to(words[w : w + 1], (32, BLOCK)) for w in range(BLOCK // 32)], axis=0
    )
    key = lax.broadcasted_iota(jnp.int32, (BLOCK, BLOCK), 0)
    query = lax.broadcasted_iota(jnp.int32, (BLOCK, BLOCK), 1)
    bits = lax.shift_right_logical(spread, key & 31) & 1
    own = jnp.where(key == query, first, 0)
    return jnp.where((bits | own) > 0, 0.0, NEG_FILL).astype(F32)


def pair_product(left, right):
    zero = jnp.zeros((HEAD_DIM, BLOCK), right.dtype)
    top = jnp.concatenate([right[:HEAD_DIM], zero], axis=1)
    bottom = jnp.concatenate([zero, right[HEAD_DIM:]], axis=1)
    return dot(left, jnp.concatenate([top, bottom], axis=0))


def stats_kernel(count_ref, coords_ref, qg_ref, k_ref, v_ref, mask_ref, out_ref):
    nb = out_ref.shape[0]
    row = lax.broadcasted_iota(jnp.int32, (nb, 3 * HEADS, BLOCK), 1)
    out_ref[...] = jnp.where(row < HEADS, FLOOR, 0.0).astype(F32)

    def tile(t, carry):
        qb, kb, p = (coords_ref[0, 0, t, c] for c in range(3))
        bias = tile_bias(mask_ref[p], jnp.where(t == 0, 1, 0))
        for pair in range(HEADS // 2):
            at = pair * 2 * HEAD_DIM
            s2 = pair_product(k_ref[kb, :, at : at + 128], qg_ref[qb, at : at + 128])
            d2 = pair_product(v_ref[kb, :, at : at + 128], qg_ref[qb, D + at : D + at + 128])
            for half in range(2):
                h = pair * 2 + half
                s = s2[:, half * BLOCK : (half + 1) * BLOCK] + bias
                m_old = out_ref[qb, h : h + 1]
                m = jnp.maximum(m_old, jnp.max(s, axis=0, keepdims=True))
                e = jnp.exp(s - m)
                drop = jnp.exp(m_old - m)
                out_ref[qb, h : h + 1] = m
                l_at, d_at = HEADS + h, 2 * HEADS + h
                out_ref[qb, l_at : l_at + 1] = out_ref[qb, l_at : l_at + 1] * drop + jnp.sum(
                    e, axis=0, keepdims=True
                )
                out_ref[qb, d_at : d_at + 1] = out_ref[qb, d_at : d_at + 1] * drop + jnp.sum(
                    e * d2[:, half * BLOCK : (half + 1) * BLOCK], axis=0, keepdims=True
                )
        return carry

    lax.fori_loop(0, count_ref[0, 0], tile, 0)


def stats(count, coords, qg, keys, values, masks):
    nb = qg.shape[0]
    smem, vmem = pl.BlockSpec(memory_space=pltpu.SMEM), pl.BlockSpec(memory_space=VMEM)
    return pl.pallas_call(
        stats_kernel,
        out_shape=jax.ShapeDtypeStruct((nb, 3 * HEADS, BLOCK), F32),
        in_specs=[smem, smem, vmem, vmem, vmem, vmem],
        out_specs=vmem,
        compiler_params=pltpu.CompilerParams(vmem_limit_bytes=48 * 2**20),
        name="stats",
    )(count, coords, qg, keys, values, masks)


def merge_kernel(nb, st_ref, out_ref, land, fin, send, recv, fsend, frecv):
    reader, blk = lax.axis_index("reader"), lax.axis_index("blk")
    peer = lambda d: lax.rem(blk + d, nb)
    source = lambda d: lax.rem(blk + nb - d, nb)
    greet([(reader, peer(d)) for d in range(1, nb)])

    def part(d):
        return pltpu.make_async_remote_copy(
            src_ref=st_ref.at[peer(d)], dst_ref=land.at[d], send_sem=send.at[d], recv_sem=recv.at[d],
            device_id=(reader, peer(d)), device_id_type=MESH,
        )

    def whole(d):
        return pltpu.make_async_remote_copy(
            src_ref=fin.at[0], dst_ref=fin.at[d], send_sem=fsend.at[d], recv_sem=frecv.at[d],
            device_id=(reader, peer(d)), device_id_type=MESH,
        )

    for d in range(1, nb):
        part(d).start()
    land[0] = st_ref[blk]
    for d in range(1, nb):
        part(d).wait()
    m = land[0, :HEADS]
    for d in range(1, nb):
        m = jnp.maximum(m, land[d, :HEADS])
    total = jnp.zeros_like(m)
    dots = jnp.zeros_like(m)
    for d in range(nb):
        weight = jnp.exp(land[d, :HEADS] - m)
        total += land[d, HEADS : 2 * HEADS] * weight
        dots += land[d, 2 * HEADS :] * weight
    fin[0, :HEADS] = m + jnp.log(total)
    fin[0, HEADS:] = dots / total
    for d in range(1, nb):
        whole(d).start()
    out_ref[blk] = fin[0]
    for d in range(1, nb):
        whole(d).wait()
        out_ref[source(d)] = fin[d]


def merge(partial):
    nb = partial.shape[0]
    vmem = pl.BlockSpec(memory_space=VMEM)
    return pl.pallas_call(
        functools.partial(merge_kernel, nb),
        out_shape=jax.ShapeDtypeStruct((nb, 2 * HEADS, BLOCK), F32),
        in_specs=[vmem],
        out_specs=vmem,
        scratch_shapes=[
            VMEM((nb, 3 * HEADS, BLOCK), F32),
            VMEM((nb, 2 * HEADS, BLOCK), F32),
            *[pltpu.SemaphoreType.DMA((nb,))] * 4,
        ],
        compiler_params=pltpu.CompilerParams(collective_id=1, has_side_effects=True),
        name="merge",
    )(partial)


def grad_kernel(
    count_ref, coords_ref, qg_ref, k_ref, v_ref, kt_ref, vt_ref, mask_ref, fin_ref, wk_ref, wv_ref,
    out_ref, kv_ref, acc, kacc, vacc,
):
    nb, nr = out_ref.shape[0], kv_ref.shape[0]

    def clear(at, carry):
        acc[at] = jnp.zeros(acc.shape[1:], F32)
        return carry

    def clear_keys(at, carry):
        kacc[at] = jnp.zeros(kacc.shape[1:], F32)
        vacc[at] = jnp.zeros(vacc.shape[1:], F32)
        return carry

    lax.fori_loop(0, nb, clear, 0)
    lax.fori_loop(0, nr, clear_keys, 0)

    def tile(t, carry):
        qb, kb, p = (coords_ref[0, 0, t, c] for c in range(3))
        bias = tile_bias(mask_ref[p], jnp.where(t == 0, 1, 0))
        for pair in range(HEADS // 2):
            at = pair * 2 * HEAD_DIM
            s2 = pair_product(k_ref[kb, :, at : at + 128], qg_ref[qb, at : at + 128])
            d2 = pair_product(v_ref[kb, :, at : at + 128], qg_ref[qb, D + at : D + at + 128])
            for half in range(2):
                h = pair * 2 + half
                lanes = slice(half * BLOCK, (half + 1) * BLOCK)
                head = slice(h * HEAD_DIM, (h + 1) * HEAD_DIM)
                ghead = slice(D + h * HEAD_DIM, D + (h + 1) * HEAD_DIM)
                prob = jnp.exp(s2[:, lanes] + bias - fin_ref[qb, h : h + 1])
                low = prob.astype(BF16)
                ds = (prob * (d2[:, lanes] - fin_ref[qb, HEADS + h : HEADS + h + 1])).astype(BF16)
                acc[qb, head] += dot(vt_ref[kb, head], low)
                acc[qb, ghead] += dot(kt_ref[kb, head], ds)
                kacc[kb, head] += dot_nt(qg_ref[qb, head], ds)
                vacc[kb, head] += dot_nt(qg_ref[qb, ghead], low)
        return carry

    lax.fori_loop(0, count_ref[0, 0], tile, 0)

    def finish(at, carry):
        out_ref[at] = acc[at].astype(BF16)
        return carry

    def finish_keys(at, carry):
        low = dot(wk_ref[...], kacc[at].astype(BF16)) + dot(wv_ref[...], vacc[at].astype(BF16))
        kv_ref[at] = low.astype(BF16)
        return carry

    lax.fori_loop(0, nb, finish, 0)
    lax.fori_loop(0, nr, finish_keys, 0)


def grads(count, coords, qg, keys, values, keys_t, values_t, masks, fin, w_key, w_value):
    nb, nr = qg.shape[0], keys.shape[0]
    smem, vmem = pl.BlockSpec(memory_space=pltpu.SMEM), pl.BlockSpec(memory_space=VMEM)
    return pl.pallas_call(
        grad_kernel,
        out_shape=[
            jax.ShapeDtypeStruct((nb, 2 * D, BLOCK), BF16),
            jax.ShapeDtypeStruct((nr, D, BLOCK), BF16),
        ],
        in_specs=[smem, smem] + [vmem] * 9,
        out_specs=[vmem, vmem],
        scratch_shapes=[
            VMEM((nb, 2 * D, BLOCK), F32),
            VMEM((nr, D, BLOCK), F32),
            VMEM((nr, D, BLOCK), F32),
        ],
        compiler_params=pltpu.CompilerParams(vmem_limit_bytes=56 * 2**20),
        name="grads",
    )(count, coords, qg, keys, values, keys_t, values_t, masks, fin, w_key, w_value)


def reduce_kernel(
    nb, nr, p_ref, kv_ref, wq_ref, attn_ref, grad_ref,
    sland, sums, land, rland, ssend, srecv, psend, precv, rsend, rrecv,
):
    reader, blk = lax.axis_index("reader"), lax.axis_index("blk")
    core = lax.rem(blk, 2)
    sib = blk + 1 - 2 * core
    half = nb // 2
    peer = lambda d: lax.rem(blk + 2 * d, nb)
    rpeer = lambda d: lax.rem(reader + d, nr)

    greet(
        [(reader, peer(d)) for d in range(1, half)]
        + [(rpeer(d), blk) for d in range(1, nr)]
        + [(reader, sib)]
    )

    def to_sibling(d):
        at = lax.rem(sib + 2 * d, nb)
        return pltpu.make_async_remote_copy(
            src_ref=p_ref.at[at], dst_ref=sland.at[d], send_sem=ssend.at[d], recv_sem=srecv.at[d],
            device_id=(reader, sib), device_id_type=MESH,
        )

    def to_reader(d):
        return pltpu.make_async_remote_copy(
            src_ref=kv_ref.at[rpeer(d)], dst_ref=rland.at[d], send_sem=rsend.at[d], recv_sem=rrecv.at[d],
            device_id=(rpeer(d), blk), device_id_type=MESH,
        )

    def to_peer(d):
        return pltpu.make_async_remote_copy(
            src_ref=sums.at[d], dst_ref=land.at[d], send_sem=psend.at[d], recv_sem=precv.at[d],
            device_id=(reader, peer(d)), device_id_type=MESH,
        )

    for d in range(1, half):
        to_sibling(d).start()
    to_sibling(0).start()
    for d in range(1, nr):
        to_reader(d).start()

    def pass_on(d, carry):
        to_sibling(d).wait_recv()
        both = p_ref[peer(d)].astype(F32) + sland[d].astype(F32)
        sums[d] = both.astype(BF16)
        to_peer(d).start()
        return carry

    lax.fori_loop(1, half, pass_on, 0)
    to_sibling(0).wait_recv()
    total = p_ref[blk].astype(F32) + sland[0].astype(F32)
    nodes = kv_ref[reader].astype(F32)
    for d in range(1, nr):
        to_reader(d).wait()
        nodes += rland[d].astype(F32)
    for d in range(1, half):
        to_peer(d).wait()
        total += land[d].astype(F32)
    attn_ref[...] = total[:D].T.astype(BF16)
    nodes += dot(wq_ref[...], (total[D:] * SCALE).astype(BF16))
    grad_ref[...] = nodes.T.astype(BF16)
    for d in range(half):
        to_sibling(d).wait_send()


def reduce(parts, key_parts, w_query):
    nb, nr = parts.shape[0], key_parts.shape[0]
    vmem = pl.BlockSpec(memory_space=VMEM)
    half = nb // 2
    return pl.pallas_call(
        functools.partial(reduce_kernel, nb, nr),
        out_shape=[jax.ShapeDtypeStruct((BLOCK, D), BF16)] * 2,
        in_specs=[vmem] * 3,
        out_specs=[vmem] * 2,
        scratch_shapes=[
            VMEM((half, 2 * D, BLOCK), BF16),
            VMEM((half, 2 * D, BLOCK), BF16),
            VMEM((half, 2 * D, BLOCK), BF16),
            VMEM((nr, D, BLOCK), BF16),
            *[pltpu.SemaphoreType.DMA((n,)) for n in (half, half, half, half, nr, nr)],
        ],
        compiler_params=pltpu.CompilerParams(
            collective_id=2, has_side_effects=True, vmem_limit_bytes=48 * 2**20
        ),
        name="reduce",
    )(parts, key_parts, w_query)


def local(features, cotangent, w_query, w_key, w_value, tile_coords, tile_count, mask_table):
    masks = mask_table.transpose(0, 2, 1)
    qg, keys, values, keys_t, values_t = gather(features, cotangent, w_query, w_key, w_value)
    partial = stats(tile_count, tile_coords, qg, keys, values, masks)
    fin = merge(partial)
    parts, key_parts = grads(
        tile_count, tile_coords, qg, keys, values, keys_t, values_t, masks, fin, w_key, w_value
    )
    return tuple(reduce(parts, key_parts, w_query))


def solution(mesh):
    return jax.shard_map(
        local,
        mesh=mesh,
        in_specs=(
            P(("reader", "blk"), None),
            P(("reader", "blk"), None),
            P(),
            P(),
            P(),
            P("reader", "blk", None, None),
            P("reader", "blk"),
            P(),
        ),
        out_specs=(P(("reader", "blk"), None), P(("reader", "blk"), None)),
        check_vma=False,
    )
```

time: 1010 us -> 176 us (0.17)
  the two profiles are of different devices: /device:TPU:0 before, /device:TPU:50 now
where the time goes in v1:
time: 176 us
  Pallas kernels  160 us (91%)
  local copies, waits for them, and re-layouts  14.4 us (8%)
    pallas_call x1, Pallas kernels, reduce(): pl.pallas_call(functools.partial(reduce_kernel, nb, nr), out_shape=[jax.S...  64 us
    pallas_call x1, Pallas kernels, gather(): pl.pallas_call(functools.partial(gather_kernel, nb, nr), out_shape=[jax.S...  42.9 us
    pallas_call x1, Pallas kernels, grads(): pl.pallas_call(grad_kernel, out_shape=[jax.ShapeDtypeStruct((nb, 2 * D, B...  26.7 us
    pallas_call x1, Pallas kernels, merge(): pl.pallas_call(functools.partial(merge_kernel, nb), out_shape=jax.ShapeDt...  19.8 us
    unnamed x33, local copies, waits for them, and re-layouts  14.4 us
    pallas_call x1, Pallas kernels, stats(): pl.pallas_call(stats_kernel, out_shape=jax.ShapeDtypeStruct((nb, 3 * HEAD...  6.53 us

profile of v1, /device:TPU:50, one launch (start us, length us, event | category | flops | bytes accessed | tf_op | source)
XLA Modules:
  0.0 175.8 jit_solution(5717030232659059282)
XLA Ops:
  1.3 0.8 copy.11.coords_ref
  2.0 1.0 copy-done.3
  3.1 1.0 copy-done.4
  4.1 1.0 copy-done.5
  5.2 0.9 copy-done.13
  6.1 0.9 copy-done.14
  7.0 42.9 %gather.1 = (bf16[16,1024,128]{2,1,0:T(8,128)(2,1)}, bf16[8,128,512]{2,1,0:T(8,128)(2,1)S(1)}, bf16[8,128,512]{2,1,0:T(8,128)(2,1)S(1)}, bf16[8,512,128]{2,1,0:T(8,128)(2,1)S(1)}, bf16[8,512,128]{2,1,0:T(8,128)(2,1)S(1)}) custom-call(bf16[128,512]{1,0:T(8,128)(2,1)S(1)} %copy-done.13, bf16[128,512]{1,0:T(8,128)(2,1)S(1)} %copy-done.14, ...), custom_call_target="tpu_custom_call" | custom-call | tf_op jit(solution)/shard_map/gather/pallas_call | solution.py:145
  49.9 0.0 copy-start.8
  49.9 1.0 copy-done.8
  50.8 1.0 copy-done.9
  51.9 1.4 copy-done.7
  53.2 6.5 %stats.1.st_ref = f32[16,24,128]{2,1,0:T(8,128)S(1)} custom-call(s32[1,1]{1,0:T(1,128)S(6)} %copy.14.count_ref, s32[1,1,32,3]{3,2,1,0:T(8,128)S(1)} %copy.11.coords_ref, bf16[16,1024,128]{2,1,0:T(8,128)(2,1)} %get-tuple-element.9.qg_ref, bf16[8,128,512]{2,1,0:T(8,128)(2,1)S(1)} %get-tuple-element.10.k_ref, bf16[8,128,512]{2,1,0:T(8,128)(2,1)S(1)} %get-tuple-element.11.v_ref, ...), custom_call_target="tpu_custom_call" | custom-call | tf_op jit(solution)/shard_map/stats/pallas_call | solution.py:222
  59.8 0.0 copy-done.12
  59.8 0.7 copy-done.11
  60.4 19.8 %merge.1.fin_ref = f32[16,16,128]{2,1,0:T(8,128)} custom-call(f32[16,24,128]{2,1,0:T(8,128)} %copy-done.11), custom_call_target="tpu_custom_call" | custom-call | tf_op jit(solution)/shard_map/merge/pallas_call | solution.py:277
  80.3 0.0 copy-done.1
  80.3 0.0 copy-done.2
  80.3 0.0 copy-start.6
  80.3 26.7 %grads.1 = (bf16[16,1024,128]{2,1,0:T(8,128)(2,1)}, bf16[8,512,128]{2,1,0:T(8,128)(2,1)}) custom-call(s32[1,1]{1,0:T(1,128)S(6)} %copy.14.count_ref, s32[1,1,32,3]{3,2,1,0:T(8,128)} %copy-done.12, bf16[16,1024,128]{2,1,0:T(8,128)(2,1)} %get-tuple-element.9.qg_ref, bf16[8,128,512]{2,1,0:T(8,128)(2,1)} %copy-done.1, bf16[8,128,512]{2,1,0:T(8,128)(2,1)} %copy-done.2, ...), custom_call_target="tpu_custom_call" | custom-call | tf_op jit(solution)/shard_map/grads/pallas_call | solution.py:349
  107.0 2.2 %copy-done = bf16[16,1024,128]{2,1,0:T(8,128)(2,1)S(1)} copy-done((bf16[16,1024,128]{2,1,0:T(8,128)(2,1)S(1)}, bf16[16,1024,128]{2,1,0:T(8,128)(2,1)}, u32[]{:S(2)}) %copy-start) | copy-done | bytes 4194328
  109.2 1.2 copy-done.10
  110.4 64.0 %reduce.1 = (bf16[128,512]{1,0:T(8,128)(2,1)S(1)}, bf16[128,512]{1,0:T(8,128)(2,1)S(1)}) custom-call(bf16[16,1024,128]{2,1,0:T(8,128)(2,1)S(1)} %copy-done, bf16[8,512,128]{2,1,0:T(8,128)(2,1)S(1)} %copy-done.10, bf16[512,512]{1,0:T(8,128)(2,1)S(1)} %copy-done.6), custom_call_target="tpu_custom_call" | custom-call | tf_op jit(solution)/shard_map/reduce/pallas_call | solution.py:437
  174.5 0.7 copy.15
  175.1 0.7 copy.16
  (14 shorter events, 0.0 us)
Async XLA Ops:
  2.0 1.0 copy-start.3
  3.1 1.0 copy-start.4
  4.1 1.0 copy-start.5
  5.2 0.9 copy-start.13
  6.1 0.9 copy-start.14
  7.0 52.8 %copy-start.12 = (s32[1,1,32,3]{3,2,1,0:T(8,128)}, s32[1,1,32,3]{3,2,1,0:T(8,128)S(1)}, u32[]{:S(2)}) copy-start(s32[1,1,32,3]{3,2,1,0:T(8,128)S(1)} %copy.11.coords_ref) | copy-start | bytes 1156
  49.9 1.0 copy-start.8
  50.8 1.0 copy-start.9
  51.9 28.4 %copy-start.1 = (bf16[8,128,512]{2,1,0:T(8,128)(2,1)}, bf16[8,128,512]{2,1,0:T(8,128)(2,1)S(1)}, u32[]{:S(2)}) copy-start(bf16[8,128,512]{2,1,0:T(8,128)(2,1)S(1)} %get-tuple-element.10.k_ref) | copy-start | bytes 3145732
  51.9 28.4 %copy-start.2 = (bf16[8,128,512]{2,1,0:T(8,128)(2,1)}, bf16[8,128,512]{2,1,0:T(8,128)(2,1)S(1)}, u32[]{:S(2)}) copy-start(bf16[8,128,512]{2,1,0:T(8,128)(2,1)S(1)} %get-tuple-element.11.v_ref) | copy-start | bytes 3145732
  51.9 1.4 copy-start.7
  59.8 0.7 copy-start.11
  80.3 26.7 %copy-start.6 = (bf16[512,512]{1,0:T(8,128)(2,1)S(1)}, bf16[512,512]{1,0:T(8,128)(2,1)}, u32[]{:S(2)}) copy-start(bf16[512,512]{1,0:T(8,128)(2,1)} %wq_ref.3) | copy-start | bytes 1572868
  107.0 2.2 %copy-start = (bf16[16,1024,128]{2,1,0:T(8,128)(2,1)S(1)}, bf16[16,1024,128]{2,1,0:T(8,128)(2,1)}, u32[]{:S(2)}) copy-start(bf16[16,1024,128]{2,1,0:T(8,128)(2,1)} %get-tuple-element.14.p_ref) | copy-start | bytes 12582916
  109.2 1.2 copy-start.10

commit v2 on v1

v2 whole, which is shorter than its diff:
```python
import functools

import jax
import jax.numpy as jnp
from jax import lax
from jax.experimental import pallas as pl
from jax.experimental.pallas import tpu as pltpu
from jax.sharding import PartitionSpec as P

HEADS = 8
HEAD_DIM = 64
D = 512
BLOCK = 128
SCALE = 0.125
FLOOR = -1e20
NEG_FILL = -1e30
MESH = pl.DeviceIdType.MESH
F32 = jnp.float32
BF16 = jnp.bfloat16
VMEM = pltpu.VMEM


def dot(a, b):
    return jnp.dot(a, b, preferred_element_type=F32)


def dot_nt(a, b):
    return lax.dot_general(a, b, (((1,), (1,)), ((), ())), preferred_element_type=F32)


def greet(devices):
    barrier = pltpu.get_barrier_semaphore()
    for device in devices:
        pl.semaphore_signal(barrier, inc=1, device_id=device, device_id_type=MESH)
    pl.semaphore_wait(barrier, len(devices))


def remote(src, dst, send, recv, device):
    return pltpu.make_async_remote_copy(
        src_ref=src, dst_ref=dst, send_sem=send, recv_sem=recv, device_id=device, device_id_type=MESH
    )


class Links:
    def __init__(self, send, recv, self_device):
        self.send, self.recv, self.anyone, self.started = send, recv, self_device, {}

    def start(self, i, src, dst, device):
        copy = remote(src, dst, self.send.at[i], self.recv.at[i], device)
        self.started[i] = copy
        copy.start()

    def arrive(self, i, dst):
        remote(dst, dst, self.send.at[i], self.recv.at[i], self.anyone).wait_recv()

    def finish(self):
        for copy in self.started.values():
            copy.wait_send()


def place():
    reader, blk = lax.axis_index("reader"), lax.axis_index("blk")
    return reader, blk, blk // 4, lax.rem(blk // 2, 2), lax.rem(blk, 2), reader // 4, lax.rem(reader, 4)


def neighbours():
    reader, blk, z, x, core, xh, y = place()
    on_blk = lambda z, x, core: (reader, z * 4 + x * 2 + core)
    on_reader = lambda xh, y: (xh * 4 + y, blk)
    return (
        on_blk(lax.rem(z + 1, 4), x, core),
        on_blk(lax.rem(z + 3, 4), x, core),
        on_blk(z, 1 - x, core),
        on_blk(z, x, 1 - core),
        on_reader(xh, lax.rem(y + 1, 4)),
        on_reader(xh, lax.rem(y + 3, 4)),
        on_reader(1 - xh, y),
    )


def gather_kernel(
    x_hbm, g_hbm, wq_hbm, wk_hbm, wv_hbm, mask_hbm,
    qg_ref, qn_ref, k_ref, v_ref, kt_ref, vt_ref, mask_ref, wq_ref, wkt_ref, wvt_ref,
    g_buf, wk_buf, wv_buf, xs, send, recv, local,
):
    reader, blk, z, x, core, xh, y = place()
    zp, zm, xn, sib, yp, ym, xp = neighbours()
    links = Links(send, recv, sib)
    at = lambda dz, side, other=0: (
        lax.rem(z + dz, 4) * 4 + (x if side == 0 else 1 - x) * 2 + (core if other == 0 else 1 - core)
    )
    half = pl.ds(0, D), pl.ds(D, D)
    own = xs.at[y, xh]

    loads = [
        pltpu.make_async_copy(src, dst, local.at[i])
        for i, (src, dst) in enumerate(
            [
                (x_hbm, own), (g_hbm, g_buf), (wq_hbm, wq_ref),
                (wk_hbm, wk_buf), (wv_hbm, wv_buf), (mask_hbm, mask_ref),
            ]
        )
    ]
    for load in loads:
        load.start()
    barrier = pltpu.get_barrier_semaphore()
    for device in (zp, zm, xn, sib, yp, ym, xp):
        pl.semaphore_signal(barrier, inc=1, device_id=device, device_id_type=MESH)

    def natural(b):
        qn_ref[b] = qg_ref[b].T

    loads[1].wait()
    qg_ref[blk, D:] = g_buf[...].astype(F32).T.astype(BF16)
    loads[0].wait()
    loads[2].wait()
    q = dot(xs[y, xh], wq_ref[...]).astype(BF16).astype(F32) * SCALE
    qg_ref[blk, :D] = q.T.astype(BF16)

    pl.semaphore_wait(barrier, 7)
    links.start(0, own, own, xp)
    mine = qg_ref.at[blk]
    links.start(10, mine, mine, zp)
    links.start(11, mine, mine, zm)
    links.start(12, mine, mine, xn)
    links.start(20, mine, mine, sib)

    loads[3].wait()
    loads[4].wait()

    def project(ring, side):
        b = side * 4 + ring
        rows = xs[ring, side]
        k = dot(rows, wk_buf[...])
        k_ref[b] = k.astype(BF16)
        kt_ref[b] = k.T.astype(BF16)
        v = dot(rows, wv_buf[...])
        v_ref[b] = v.astype(BF16)
        vt_ref[b] = v.T.astype(BF16)

    links.arrive(0, xs.at[y, 1 - xh])
    pair = xs.at[y]
    links.start(1, pair, pair, yp)
    links.start(2, pair, pair, ym)
    project(y, xh)
    project(y, 1 - xh)

    def relay(i, block, device):
        links.start(i, qg_ref.at[block], qg_ref.at[block], device)

    b_zm, b_zp, b_xn = at(3, 0), at(1, 0), at(0, 1)
    links.arrive(10, qg_ref.at[b_zm])
    ref = qg_ref.at[b_zm, half[0]]
    links.start(13, ref, ref, zp)
    relay(21, b_zm, sib)
    links.arrive(11, qg_ref.at[b_zp])
    ref = qg_ref.at[b_zp, half[1]]
    links.start(14, ref, ref, zm)
    relay(22, b_zp, sib)
    links.arrive(12, qg_ref.at[b_xn])
    relay(15, b_xn, zp)
    relay(16, b_xn, zm)
    relay(23, b_xn, sib)

    y_m, y_p, y_2 = lax.rem(y + 3, 4), lax.rem(y + 1, 4), lax.rem(y + 2, 4)
    links.arrive(1, xs.at[y_m])
    ref = xs.at[y_m, 0]
    links.start(3, ref, ref, yp)
    links.arrive(2, xs.at[y_p])
    ref = xs.at[y_p, 1]
    links.start(4, ref, ref, ym)
    natural(blk)
    natural(b_zm)
    natural(b_zp)
    project(y_m, 0)

    b_z2 = at(2, 0)
    links.arrive(13, qg_ref.at[b_z2, half[0]])
    links.arrive(14, qg_ref.at[b_z2, half[1]])
    relay(17, b_z2, xn)
    relay(24, b_z2, sib)
    natural(b_xn)
    project(y_m, 1)
    project(y_p, 0)
    project(y_p, 1)
    links.arrive(3, xs.at[y_2, 0])
    links.arrive(4, xs.at[y_2, 1])
    project(y_2, 0)
    project(y_2, 1)
    natural(b_z2)
    wkt_ref[...] = wk_buf[...].T
    wvt_ref[...] = wv_buf[...].T

    others = [at(0, 0, 1), at(3, 0, 1), at(1, 0, 1), at(0, 1, 1), at(2, 0, 1)]
    for i in range(4):
        links.arrive(20 + i, qg_ref.at[others[i]])
        natural(others[i])
    b_zmx, b_zpx, b_z2x = at(3, 1), at(1, 1), at(2, 1)
    links.arrive(15, qg_ref.at[b_zmx])
    relay(25, b_zmx, sib)
    links.arrive(16, qg_ref.at[b_zpx])
    relay(26, b_zpx, sib)
    natural(b_zmx)
    natural(b_zpx)
    links.arrive(24, qg_ref.at[others[4]])
    natural(others[4])
    links.arrive(17, qg_ref.at[b_z2x])
    relay(27, b_z2x, sib)
    natural(b_z2x)
    for i, block in enumerate([at(3, 1, 1), at(1, 1, 1), at(2, 1, 1)]):
        links.arrive(25 + i, qg_ref.at[block])
        natural(block)
    loads[5].wait()
    links.finish()


def gather(features, cotangent, w_query, w_key, w_value, masks):
    nb, nr = lax.axis_size("blk"), lax.axis_size("reader")
    hbm, vmem = pl.BlockSpec(memory_space=pltpu.HBM), pl.BlockSpec(memory_space=VMEM)
    return pl.pallas_call(
        gather_kernel,
        out_shape=[
            VMEM((nb, 2 * D, BLOCK), BF16),
            VMEM((nb, BLOCK, 2 * D), BF16),
            VMEM((nr, BLOCK, D), BF16),
            VMEM((nr, BLOCK, D), BF16),
            VMEM((nr, D, BLOCK), BF16),
            VMEM((nr, D, BLOCK), BF16),
            VMEM(masks.shape, jnp.int32),
            VMEM((D, D), BF16),
            VMEM((D, D), BF16),
            VMEM((D, D), BF16),
        ],
        in_specs=[hbm] * 6,
        out_specs=[vmem] * 10,
        scratch_shapes=[
            VMEM((BLOCK, D), BF16),
            VMEM((D, D), BF16),
            VMEM((D, D), BF16),
            VMEM((4, 2, BLOCK, D), BF16),
            pltpu.SemaphoreType.DMA((28,)),
            pltpu.SemaphoreType.DMA((28,)),
            pltpu.SemaphoreType.DMA((6,)),
        ],
        compiler_params=pltpu.CompilerParams(
            collective_id=0, has_side_effects=True, vmem_limit_bytes=16 * 2**20
        ),
        name="gather",
    )(*(pltpu.with_memory_space_constraint(a, pltpu.HBM) for a in (features, cotangent, w_query, w_key, w_value, masks)))


def tile_bias(words, first):
    spread = jnp.concatenate(
        [jnp.broadcast_to(words[w : w + 1], (32, BLOCK)) for w in range(BLOCK // 32)], axis=0
    )
    key = lax.broadcasted_iota(jnp.int32, (BLOCK, BLOCK), 0)
    query = lax.broadcasted_iota(jnp.int32, (BLOCK, BLOCK), 1)
    bits = lax.shift_right_logical(spread, key & 31) & 1
    own = jnp.where(key == query, first, 0)
    return jnp.where((bits | own) > 0, 0.0, NEG_FILL).astype(F32)


def pair_product(left, right):
    zero = jnp.zeros((HEAD_DIM, BLOCK), right.dtype)
    top = jnp.concatenate([right[:HEAD_DIM], zero], axis=1)
    bottom = jnp.concatenate([zero, right[HEAD_DIM:]], axis=1)
    return dot(left, jnp.concatenate([top, bottom], axis=0))


def stats_kernel(count_ref, coords_ref, qg_ref, k_ref, v_ref, mask_ref, out_ref):
    nb = out_ref.shape[0]
    row = lax.broadcasted_iota(jnp.int32, (nb, 3 * HEADS, BLOCK), 1)
    out_ref[...] = jnp.where(row < HEADS, FLOOR, 0.0).astype(F32)

    def tile(t, carry):
        qb, kb, p = (coords_ref[0, c, 0, t] for c in range(3))
        bias = tile_bias(mask_ref[p], jnp.where(t == 0, 1, 0))
        for pair in range(HEADS // 2):
            at = pair * 2 * HEAD_DIM
            s2 = pair_product(k_ref[kb, :, at : at + 128], qg_ref[qb, at : at + 128])
            d2 = pair_product(v_ref[kb, :, at : at + 128], qg_ref[qb, D + at : D + at + 128])
            for half in range(2):
                h = pair * 2 + half
                s = s2[:, half * BLOCK : (half + 1) * BLOCK] + bias
                m_old = out_ref[qb, h : h + 1]
                m = jnp.maximum(m_old, jnp.max(s, axis=0, keepdims=True))
                e = jnp.exp(s - m)
                drop = jnp.exp(m_old - m)
                out_ref[qb, h : h + 1] = m
                l_at, d_at = HEADS + h, 2 * HEADS + h
                out_ref[qb, l_at : l_at + 1] = out_ref[qb, l_at : l_at + 1] * drop + jnp.sum(
                    e, axis=0, keepdims=True
                )
                out_ref[qb, d_at : d_at + 1] = out_ref[qb, d_at : d_at + 1] * drop + jnp.sum(
                    e * d2[:, half * BLOCK : (half + 1) * BLOCK], axis=0, keepdims=True
                )
        return carry

    lax.fori_loop(0, count_ref[0, 0], tile, 0)


def stats(count, coords, qg, keys, values, masks):
    nb = qg.shape[0]
    smem, vmem = pl.BlockSpec(memory_space=pltpu.SMEM), pl.BlockSpec(memory_space=VMEM)
    return pl.pallas_call(
        stats_kernel,
        out_shape=VMEM((nb, 3 * HEADS, BLOCK), F32),
        in_specs=[smem, smem, vmem, vmem, vmem, vmem],
        out_specs=vmem,
        compiler_params=pltpu.CompilerParams(vmem_limit_bytes=8 * 2**20),
        name="stats",
    )(count, coords, qg, keys, values, masks)


def merge_kernel(nb, st_ref, out_ref, land, fin, send, recv, fsend, frecv):
    reader, blk = lax.axis_index("reader"), lax.axis_index("blk")
    peer = lambda d: lax.rem(blk + d, nb)
    source = lambda d: lax.rem(blk + nb - d, nb)
    greet([(reader, peer(d)) for d in range(1, nb)])

    def part(d):
        return pltpu.make_async_remote_copy(
            src_ref=st_ref.at[peer(d)], dst_ref=land.at[d], send_sem=send.at[d], recv_sem=recv.at[d],
            device_id=(reader, peer(d)), device_id_type=MESH,
        )

    def whole(d):
        return pltpu.make_async_remote_copy(
            src_ref=fin.at[0], dst_ref=fin.at[d], send_sem=fsend.at[d], recv_sem=frecv.at[d],
            device_id=(reader, peer(d)), device_id_type=MESH,
        )

    for d in range(1, nb):
        part(d).start()
    land[0] = st_ref[blk]
    for d in range(1, nb):
        part(d).wait()
    m = land[0, :HEADS]
    for d in range(1, nb):
        m = jnp.maximum(m, land[d, :HEADS])
    total = jnp.zeros_like(m)
    dots = jnp.zeros_like(m)
    for d in range(nb):
        weight = jnp.exp(land[d, :HEADS] - m)
        total += land[d, HEADS : 2 * HEADS] * weight
        dots += land[d, 2 * HEADS :] * weight
    fin[0, :HEADS] = m + jnp.log(total)
    fin[0, HEADS:] = dots / total
    for d in range(1, nb):
        whole(d).start()
    out_ref[blk] = fin[0]
    for d in range(1, nb):
        whole(d).wait()
        out_ref[source(d)] = fin[d]


def merge(partial):
    nb = partial.shape[0]
    vmem = pl.BlockSpec(memory_space=VMEM)
    return pl.pallas_call(
        functools.partial(merge_kernel, nb),
        out_shape=VMEM((nb, 2 * HEADS, BLOCK), F32),
        in_specs=[vmem],
        out_specs=vmem,
        scratch_shapes=[
            VMEM((nb, 3 * HEADS, BLOCK), F32),
            VMEM((nb, 2 * HEADS, BLOCK), F32),
            *[pltpu.SemaphoreType.DMA((nb,))] * 4,
        ],
        compiler_params=pltpu.CompilerParams(
            collective_id=1, has_side_effects=True, vmem_limit_bytes=4 * 2**20
        ),
        name="merge",
    )(partial)


def lane_split(block):
    lane = lax.broadcasted_iota(jnp.int32, block.shape, 1)
    zero = jnp.zeros_like(block)
    return jnp.concatenate(
        [jnp.where(lane < HEAD_DIM, block, zero), jnp.where(lane >= HEAD_DIM, block, zero)], axis=0
    )


def grad_kernel(
    count_ref, coords_ref, qg_ref, qn_ref, k_ref, v_ref, kt_ref, vt_ref, mask_ref, fin_ref, wkt_ref, wvt_ref,
    acc, kv_ref, kacc, vacc, probs, dscores,
):
    nb, nr = acc.shape[0], kacc.shape[0]

    def clear(at, carry):
        acc[at] = jnp.zeros(acc.shape[1:], F32)
        return carry

    def clear_keys(at, carry):
        kacc[at] = jnp.zeros(kacc.shape[1:], F32)
        vacc[at] = jnp.zeros(vacc.shape[1:], F32)
        return carry

    lax.fori_loop(0, nb, clear, 0)
    lax.fori_loop(0, nr, clear_keys, 0)

    def scores(t):
        qb, kb, p = (coords_ref[0, c, 0, t] for c in range(3))
        bias = tile_bias(mask_ref[p], jnp.where(t == 0, 1, 0))
        for pair in range(HEADS // 2):
            at = pair * 2 * HEAD_DIM
            s2 = pair_product(k_ref[kb, :, at : at + 128], qg_ref[qb, at : at + 128])
            d2 = pair_product(v_ref[kb, :, at : at + 128], qg_ref[qb, D + at : D + at + 128])
            for half in range(2):
                h = pair * 2 + half
                lanes = slice(half * BLOCK, (half + 1) * BLOCK)
                prob = jnp.exp(s2[:, lanes] + bias - fin_ref[qb, h : h + 1])
                probs[h] = prob.astype(BF16)
                delta = fin_ref[qb, HEADS + h : HEADS + h + 1]
                dscores[h] = (prob * (d2[:, lanes] - delta)).astype(BF16)

    def products(t):
        qb, kb = coords_ref[0, 0, 0, t], coords_ref[0, 1, 0, t]
        for pair in range(HEADS // 2):
            for h in (2 * pair, 2 * pair + 1):
                head = slice(h * HEAD_DIM, (h + 1) * HEAD_DIM)
                ghead = slice(D + h * HEAD_DIM, D + (h + 1) * HEAD_DIM)
                acc[qb, head] += dot(vt_ref[kb, head], probs[h])
                acc[qb, ghead] += dot(kt_ref[kb, head], dscores[h])
            two = slice(pair * 128, pair * 128 + 128)
            gtwo = slice(D + pair * 128, D + pair * 128 + 128)
            low = jnp.concatenate([probs[2 * pair], probs[2 * pair + 1]], axis=1)
            ds = jnp.concatenate([dscores[2 * pair], dscores[2 * pair + 1]], axis=1)
            kacc[kb, :, two] += dot(ds, lane_split(qn_ref[qb, :, two]))
            vacc[kb, :, two] += dot(low, lane_split(qn_ref[qb, :, gtwo]))

    def step(t, carry):
        products(t - 1)
        scores(t)
        return carry

    count = count_ref[0, 0]
    scores(0)
    lax.fori_loop(1, count, step, 0)
    products(count - 1)

    for ring in range(4):
        for side in range(2):
            at = side * 4 + ring
            total = dot(kacc[at].astype(BF16), wkt_ref[...]) + dot(vacc[at].astype(BF16), wvt_ref[...])
            kv_ref[ring, side] = total.astype(BF16)


def grads(count, coords, qg, qn, keys, values, keys_t, values_t, masks, fin, wkt, wvt):
    nb, nr = qg.shape[0], keys.shape[0]
    smem, vmem = pl.BlockSpec(memory_space=pltpu.SMEM), pl.BlockSpec(memory_space=VMEM)
    return pl.pallas_call(
        grad_kernel,
        out_shape=[VMEM((nb, 2 * D, BLOCK), F32), VMEM((4, 2, BLOCK, D), BF16)],
        in_specs=[smem, smem] + [vmem] * 10,
        out_specs=[vmem, vmem],
        scratch_shapes=[
            VMEM((nr, BLOCK, D), F32),
            VMEM((nr, BLOCK, D), F32),
            VMEM((HEADS, BLOCK, BLOCK), BF16),
            VMEM((HEADS, BLOCK, BLOCK), BF16),
        ],
        compiler_params=pltpu.CompilerParams(vmem_limit_bytes=16 * 2**20),
        name="grads",
    )(count, coords, qg, qn, keys, values, keys_t, values_t, masks, fin, wkt, wvt)


def reduce_kernel(
    p_ref, kv_ref, wq_ref, attn_ref, grad_ref,
    to_sib, from_sib, sums, land, halves, kland, khalves, ksum, send, recv,
):
    reader, blk, z, x, core, xh, y = place()
    zp, zm, xn, sib, yp, ym, xp = neighbours()
    links = Links(send, recv, sib)
    at = lambda dz, side, other=0: (
        lax.rem(z + dz, 4) * 4 + (x if side == 0 else 1 - x) * 2 + (core if other == 0 else 1 - core)
    )
    order = [(2, 1), (1, 1), (3, 1), (2, 0), (0, 1), (1, 0), (3, 0), (0, 0)]
    barrier = pltpu.get_barrier_semaphore()
    for device in (zp, zm, xn, sib, yp, ym, xp):
        pl.semaphore_signal(barrier, inc=1, device_id=device, device_id_type=MESH)
    for i in range(2):
        to_sib[i] = p_ref[at(*order[i], 1)].astype(BF16)
    pl.semaphore_wait(barrier, 7)

    y_m, y_p, y_2 = lax.rem(y + 3, 4), lax.rem(y + 1, 4), lax.rem(y + 2, 4)
    links.start(0, kv_ref.at[y_2, 0], khalves.at[0], yp)
    links.start(1, kv_ref.at[y_2, 1], khalves.at[1], ym)
    for i in range(8):
        if i >= 2:
            to_sib[i] = p_ref[at(*order[i], 1)].astype(BF16)
        links.start(20 + i, to_sib.at[i], from_sib.at[i], sib)

    def both(i):
        links.arrive(20 + i, from_sib.at[i])
        return p_ref[at(*order[i])] + from_sib[i].astype(F32)

    sums[0] = both(0).astype(BF16)
    links.start(10, sums.at[0], land.at[0], xn)
    sums[1] = both(1).astype(BF16)
    links.start(11, sums.at[1], land.at[1], zp)
    sums[2] = both(2).astype(BF16)
    links.start(12, sums.at[2], land.at[2], zm)

    links.arrive(0, khalves.at[0])
    ksum[0, 0] = (kv_ref[y_p, 0].astype(F32) + khalves[0].astype(F32)).astype(BF16)
    ksum[0, 1] = kv_ref[y_p, 1]
    links.start(2, ksum.at[0], kland.at[0], yp)
    links.arrive(1, khalves.at[1])
    ksum[1, 0] = kv_ref[y_m, 0]
    ksum[1, 1] = (kv_ref[y_m, 1].astype(F32) + khalves[1].astype(F32)).astype(BF16)
    links.start(3, ksum.at[1], kland.at[1], ym)

    far = both(3)
    links.arrive(10, land.at[0])
    sums[3] = (far + land[0].astype(F32)).astype(BF16)
    links.start(13, sums.at[3, pl.ds(0, D)], halves.at[0], zp)
    links.start(14, sums.at[3, pl.ds(D, D)], halves.at[1], zm)
    across = both(4)
    links.arrive(11, land.at[1])
    links.arrive(12, land.at[2])
    sums[4] = (across + land[1].astype(F32) + land[2].astype(F32)).astype(BF16)
    links.start(15, sums.at[4], land.at[3], xn)

    up = both(5)
    links.arrive(13, halves.at[0])
    sums[5, :D] = (up[:D] + halves[0].astype(F32)).astype(BF16)
    sums[5, D:] = up[D:].astype(BF16)
    links.start(16, sums.at[5], land.at[4], zp)
    down = both(6)
    links.arrive(14, halves.at[1])
    sums[6, :D] = down[:D].astype(BF16)
    sums[6, D:] = (down[D:] + halves[1].astype(F32)).astype(BF16)
    links.start(17, sums.at[6], land.at[5], zm)

    links.arrive(2, kland.at[0])
    links.arrive(3, kland.at[1])
    ksum[2, 0] = (
        kv_ref[y, 1 - xh].astype(F32) + kland[0, 1 - xh].astype(F32) + kland[1, 1 - xh].astype(F32)
    ).astype(BF16)
    links.start(4, ksum.at[2, 0], ksum.at[2, 1], xp)
    nodes = kv_ref[y, xh].astype(F32) + kland[0, xh].astype(F32) + kland[1, xh].astype(F32)

    total = both(7)
    links.arrive(15, land.at[3])
    total += land[3].astype(F32)
    links.arrive(4, ksum.at[2, 1])
    nodes += ksum[2, 1].astype(F32)
    links.arrive(16, land.at[4])
    links.arrive(17, land.at[5])
    total += land[4].astype(F32) + land[5].astype(F32)
    attn_ref[...] = total[:D].T.astype(BF16)
    nodes += dot(wq_ref[...], (total[D:] * SCALE).astype(BF16)).T
    grad_ref[...] = nodes.astype(BF16)
    links.finish()


def reduce(parts, key_parts, w_query):
    vmem = pl.BlockSpec(memory_space=VMEM)
    block = (2 * D, BLOCK)
    return pl.pallas_call(
        reduce_kernel,
        out_shape=[jax.ShapeDtypeStruct((BLOCK, D), BF16)] * 2,
        in_specs=[vmem] * 3,
        out_specs=[vmem] * 2,
        scratch_shapes=[
            VMEM((8, *block), BF16),
            VMEM((8, *block), BF16),
            VMEM((7, *block), BF16),
            VMEM((6, *block), BF16),
            VMEM((2, D, BLOCK), BF16),
            VMEM((2, 2, BLOCK, D), BF16),
            VMEM((2, BLOCK, D), BF16),
            VMEM((3, 2, BLOCK, D), BF16),
            pltpu.SemaphoreType.DMA((28,)),
            pltpu.SemaphoreType.DMA((28,)),
        ],
        compiler_params=pltpu.CompilerParams(
            collective_id=2, has_side_effects=True, vmem_limit_bytes=24 * 2**20
        ),
        name="reduce",
    )(parts, key_parts, w_query)


def local(features, cotangent, w_query, w_key, w_value, tile_coords, tile_count, mask_table):
    masks = mask_table.transpose(0, 2, 1)
    coords = tile_coords.transpose(0, 3, 1, 2)
    qg, qn, keys, values, keys_t, values_t, masks, wq, wkt, wvt = gather(
        features, cotangent, w_query, w_key, w_value, masks
    )
    partial = stats(tile_count, coords, qg, keys, values, masks)
    fin = merge(partial)
    parts, key_parts = grads(
        tile_count, coords, qg, qn, keys, values, keys_t, values_t, masks, fin, wkt, wvt
    )
    return tuple(reduce(parts, key_parts, wq))


def solution(mesh):
    return jax.shard_map(
        local,
        mesh=mesh,
        in_specs=(
            P(("reader", "blk"), None),
            P(("reader", "blk"), None),
            P(),
            P(),
            P(),
            P("reader", "blk", None, None),
            P("reader", "blk"),
            P(),
        ),
        out_specs=(P(("reader", "blk"), None), P(("reader", "blk"), None)),
        check_vma=False,
    )
```

time: 176 us -> 100 us (0.57)
  the two profiles are of different devices: /device:TPU:50 before, /device:TPU:0 now
where the time goes in v2:
time: 100 us; the launch traced here: 99.8 us
  Pallas kernels  96.4 us (96%)
  local copies, waits for them, and re-layouts  2.06 us (2%)
  between operations  1.34 us (1%)
    pallas_call x1, Pallas kernels, reduce(): pl.pallas_call(reduce_kernel, out_shape=[jax.ShapeDtypeStruct((BLOCK, D),...  38.3 us
    pallas_call x1, Pallas kernels, gather(): pl.pallas_call(gather_kernel, out_shape=[VMEM((nb, 2 * D, BLOCK), BF16),...  27.7 us
    pallas_call x1, Pallas kernels, merge(): pl.pallas_call(functools.partial(merge_kernel, nb), out_shape=VMEM((nb, 2...  21.2 us
    pallas_call x1, Pallas kernels, grads(): pl.pallas_call(grad_kernel, out_shape=[VMEM((nb, 2 * D, BLOCK), F32), VME...  6.36 us
    pallas_call x1, Pallas kernels, stats(): pl.pallas_call(stats_kernel, out_shape=VMEM((nb, 3 * HEADS, BLOCK), F32),...  2.77 us
    unnamed x6, local copies, waits for them, and re-layouts  2.06 us

profile of v2, /device:TPU:0, one launch (start us, length us, event | category | flops | bytes accessed | tf_op | source)
XLA Modules:
  0.0 99.8 jit_solution(7617090949356252734)
XLA Ops:
  1.3 27.7 %gather.1 = (bf16[16,1024,128]{2,1,0:T(8,128)(2,1)S(1)}, bf16[16,128,1024]{2,1,0:T(8,128)(2,1)S(1)}, bf16[8,128,512]{2,1,0:T(8,128)(2,1)S(1)}, bf16[8,128,512]{2...) custom-call(bf16[128,512]{1,0:T(8,128)(2,1)} %x_hbm.1, ...), custom_call_target="tpu_custom_call" | custom-call | tf_op jit(solution)/shard_map/gather/pallas_call | solution.py:220
  29.0 0.0 copy-start.1
  29.0 0.0 copy-start
  29.0 0.7 copy-done
  29.8 2.8 %stats.1.st_ref = f32[16,24,128]{2,1,0:T(8,128)S(1)} custom-call(s32[1,1]{1,0:T(1,128)S(6)} %copy.12.count_ref, s32[1,3,1,32]{3,2,1,0:T(1,128)S(1)} %bitcast.2, bf16[16,1024,128]{2,1,0:T(8,128)(2,1)S(1)} %get-tuple-element.14.qg_ref, bf16[8,128,512]{2,1,0:T(8,128)(2,1)S(1)} %get-tuple-element.16.k_ref, bf16[8,128,512]{2,1,0:T(8,128)(2,1)S(1)} %get-tuple-element.17.v_ref, ...), custom_call_target="tpu_custom_call" | custom-call | tf_op jit(solution)/shard_map/stats/pallas_call | solution.py:305
  32.5 21.2 %merge.1.fin_ref = f32[16,16,128]{2,1,0:T(8,128)S(1)} custom-call(f32[16,24,128]{2,1,0:T(8,128)S(1)} %stats.1.st_ref), custom_call_target="tpu_custom_call" | custom-call | tf_op jit(solution)/shard_map/merge/pallas_call | solution.py:360
  53.8 0.0 copy-done.1
  53.8 6.4 %grads.1 = (f32[16,1024,128]{2,1,0:T(8,128)S(1)}, bf16[4,2,128,512]{3,2,1,0:T(8,128)(2,1)S(1)}) custom-call(s32[1,1]{1,0:T(1,128)S(6)} %copy.12.count_ref, s32[1,3,1,32]{3,2,1,0:T(1,128)S(1)} %bitcast.3, bf16[16,1024,128]{2,1,0:T(8,128)(2,1)S(1)} %get-tuple-element.14.qg_ref, bf16[16,128,1024]{2,1,0:T(8,128)(2,1)S(1)} %get-tuple-element.15.qn_ref, ...), custom_call_target="tpu_custom_call" | custom-call | tf_op jit(solution)/shard_map/grads/pallas_call | solution.py:453
  60.1 38.3 %reduce.1 = (bf16[128,512]{1,0:T(8,128)(2,1)S(1)}, bf16[128,512]{1,0:T(8,128)(2,1)S(1)}) custom-call(f32[16,1024,128]{2,1,0:T(8,128)S(1)} %get-tuple-element.23.p_ref, bf16[4,2,128,512]{3,2,1,0:T(8,128)(2,1)S(1)} %get-tuple-element.24.kv_ref, bf16[512,512]{1,0:T(8,128)(2,1)S(1)} %get-tuple-element.25.wq_ref), custom_call_target="tpu_custom_call" | custom-call | tf_op jit(solution)/shard_map/reduce/pallas_call | solution.py:562
  98.4 0.7 copy.13
  99.1 0.7 copy.14
Async XLA Ops:
  29.0 24.8 %copy-start.1 = (s32[1,1,32,3]{2,1,3,0:T(1,128)S(1)}, s32[1,1,32,3]{2,1,3,0:T(1,128)}, u32[]{:S(2)}) copy-start(s32[1,1,32,3]{2,1,3,0:T(1,128)} %param.13) | copy-start | bytes 1156
  29.0 0.7 copy-start

commit v3 on v2

v3 whole, which is shorter than its diff:
```python
import functools

import jax
import jax.numpy as jnp
from jax import lax
from jax.experimental import pallas as pl
from jax.experimental.pallas import tpu as pltpu
from jax.sharding import PartitionSpec as P

HEADS = 8
HEAD_DIM = 64
D = 512
BLOCK = 128
SCALE = 0.125
FLOOR = -1e20
NEG_FILL = -1e30
MESH = pl.DeviceIdType.MESH
F32 = jnp.float32
BF16 = jnp.bfloat16
VMEM = pltpu.VMEM


def dot(a, b):
    return jnp.dot(a, b, preferred_element_type=F32)


def remote(src, dst, send, recv, device):
    return pltpu.make_async_remote_copy(
        src_ref=src, dst_ref=dst, send_sem=send, recv_sem=recv, device_id=device, device_id_type=MESH
    )


class Links:
    def __init__(self, send, recv, self_device):
        self.send, self.recv, self.anyone, self.started = send, recv, self_device, {}

    def start(self, i, src, dst, device):
        copy = remote(src, dst, self.send.at[i], self.recv.at[i], device)
        self.started[i] = copy
        copy.start()

    def arrive(self, i, dst):
        remote(dst, dst, self.send.at[i], self.recv.at[i], self.anyone).wait_recv()

    def finish(self):
        for copy in self.started.values():
            copy.wait_send()


def place():
    reader, blk = lax.axis_index("reader"), lax.axis_index("blk")
    return reader, blk, blk // 4, lax.rem(blk // 2, 2), lax.rem(blk, 2), reader // 4, lax.rem(reader, 4)


def neighbours():
    reader, blk, z, x, core, xh, y = place()
    on_blk = lambda z, x, core: (reader, z * 4 + x * 2 + core)
    on_reader = lambda xh, y: (xh * 4 + y, blk)
    return (
        on_blk(lax.rem(z + 1, 4), x, core),
        on_blk(lax.rem(z + 3, 4), x, core),
        on_blk(z, 1 - x, core),
        on_blk(z, x, 1 - core),
        on_reader(xh, lax.rem(y + 1, 4)),
        on_reader(xh, lax.rem(y + 3, 4)),
        on_reader(1 - xh, y),
    )


def blocks():
    _, _, z, x, core, _, _ = place()
    return lambda dz, side, other=0: (
        lax.rem(z + dz, 4) * 4 + (x if side == 0 else 1 - x) * 2 + (core if other == 0 else 1 - core)
    )


def gather_kernel(
    x_hbm, g_hbm, wq_hbm, wk_hbm, wv_hbm, mask_hbm,
    qt_ref, gt_ref, qn_ref, gn_ref, k_ref, v_ref, kt_ref, vt_ref, mask_ref, wq_ref, wkt_ref, wvt_ref,
    wk_buf, wv_buf, xb, xs, send, recv, local,
):
    reader, blk, z, x, core, xh, y = place()
    zp, zm, xn, sib, yp, ym, xp = neighbours()
    links = Links(send, recv, sib)
    at = blocks()

    barrier = pltpu.get_barrier_semaphore()
    for device in (zp, zm, xn, sib, yp, ym, xp):
        pl.semaphore_signal(barrier, inc=1, device_id=device, device_id_type=MESH)
    loads = [
        pltpu.make_async_copy(src, dst, local.at[i])
        for i, (src, dst) in enumerate(
            [
                (x_hbm, xs.at[y, xh]), (x_hbm, xb.at[blk]), (g_hbm, gn_ref.at[blk]), (wk_hbm, wk_buf),
                (wv_hbm, wv_buf), (wq_hbm, wq_ref), (mask_hbm, mask_ref),
            ]
        )
    ]
    for load in loads:
        load.start()
    pl.semaphore_wait(barrier, 7)

    links.start(10, x_hbm, xb.at[blk], zp)
    links.start(12, x_hbm, xb.at[blk], zm)
    links.start(14, x_hbm, xb.at[blk], xn)
    links.start(1, x_hbm, xs.at[y, xh], yp)
    links.start(2, x_hbm, xs.at[y, xh], ym)
    links.start(0, x_hbm, xs.at[y, xh], xp)
    links.start(11, g_hbm, gn_ref.at[blk], zp)
    links.start(13, g_hbm, gn_ref.at[blk], zm)
    links.start(15, g_hbm, gn_ref.at[blk], xn)
    links.start(30, x_hbm, xb.at[blk], sib)
    links.start(31, g_hbm, gn_ref.at[blk], sib)

    def arrive_x(i, b):
        links.arrive(i, xb.at[b])

    def arrive_g(i, b):
        links.arrive(i, gn_ref.at[b])

    def pass_x(i, b, device):
        links.start(i, xb.at[b], xb.at[b], device)

    def pass_g(i, b, device):
        links.start(i, gn_ref.at[b], gn_ref.at[b], device)

    def arrive_s(i, ring, side):
        links.arrive(i, xs.at[ring, side])

    def pass_s(i, ring, side, device):
        links.start(i, xs.at[ring, side], xs.at[ring, side], device)

    def prepare(b):
        q = (dot(xb[b], wq_ref[...]).astype(BF16).astype(F32) * SCALE).astype(BF16)
        qn_ref[b] = q
        qt_ref[b] = q.T
        gt_ref[b] = gn_ref[b].T

    def project(ring, side):
        b = side * 4 + ring
        rows = xs[ring, side]
        k = dot(rows, wk_buf[...]).astype(BF16)
        k_ref[b] = k
        kt_ref[b] = k.T
        v = dot(rows, wv_buf[...]).astype(BF16)
        v_ref[b] = v
        vt_ref[b] = v.T

    b_zm, b_zp, b_xn, b_z2 = at(3, 0), at(1, 0), at(0, 1), at(2, 0)
    b_zmx, b_zpx, b_z2x = at(3, 1), at(1, 1), at(2, 1)
    y_m, y_p, y_2 = lax.rem(y + 3, 4), lax.rem(y + 1, 4), lax.rem(y + 2, 4)

    for i in range(6):
        loads[i].wait()
    project(y, xh)
    prepare(blk)

    arrive_x(10, b_zm)
    pass_x(18, b_zm, zp)
    arrive_x(14, b_xn)
    pass_x(20, b_xn, zp)
    pass_x(22, b_xn, zm)
    arrive_x(12, b_zp)
    arrive_s(1, y_m, xh)
    pass_s(5, y_m, xh, yp)
    pass_x(32, b_zm, sib)
    pass_x(34, b_zp, sib)
    pass_x(36, b_xn, sib)
    arrive_s(2, y_p, xh)
    project(y_m, xh)

    arrive_g(13, b_zp)
    pass_g(19, b_zp, zm)
    arrive_g(15, b_xn)
    pass_g(21, b_xn, zp)
    pass_g(23, b_xn, zm)
    arrive_s(0, y, 1 - xh)
    pass_s(3, y, 1 - xh, yp)
    pass_s(4, y, 1 - xh, ym)
    arrive_g(11, b_zm)
    pass_g(33, b_zm, sib)
    pass_g(35, b_zp, sib)
    pass_g(37, b_xn, sib)
    project(y_p, xh)
    project(y, 1 - xh)

    arrive_x(18, b_z2)
    pass_x(24, b_z2, xn)
    pass_x(38, b_z2, sib)
    prepare(b_zm)
    prepare(b_zp)
    arrive_s(4, y_p, 1 - xh)
    pass_s(6, y_p, 1 - xh, ym)
    arrive_g(19, b_z2)
    pass_g(25, b_z2, xn)
    pass_g(39, b_z2, sib)
    prepare(b_xn)
    project(y_p, 1 - xh)
    arrive_s(3, y_m, 1 - xh)
    project(y_m, 1 - xh)
    arrive_s(5, y_2, xh)
    project(y_2, xh)
    wkt_ref[...] = wk_buf[...].T
    wvt_ref[...] = wv_buf[...].T

    o_own, o_zm, o_zp, o_xn, o_z2 = at(0, 0, 1), at(3, 0, 1), at(1, 0, 1), at(0, 1, 1), at(2, 0, 1)
    for i, b in ((30, o_own), (32, o_zm), (34, o_zp), (36, o_xn)):
        arrive_x(i, b)
        arrive_g(i + 1, b)
        prepare(b)
    arrive_x(20, b_zmx)
    pass_x(40, b_zmx, sib)
    arrive_x(22, b_zpx)
    pass_x(42, b_zpx, sib)
    arrive_s(6, y_2, 1 - xh)
    project(y_2, 1 - xh)
    prepare(b_z2)
    arrive_g(23, b_zpx)
    pass_g(43, b_zpx, sib)
    arrive_g(21, b_zmx)
    pass_g(41, b_zmx, sib)
    arrive_x(24, b_z2x)
    pass_x(44, b_z2x, sib)
    arrive_x(38, o_z2)
    arrive_g(39, o_z2)
    prepare(o_z2)
    prepare(b_zmx)
    prepare(b_zpx)
    arrive_g(25, b_z2x)
    pass_g(45, b_z2x, sib)
    prepare(b_z2x)
    for i, b in ((40, at(3, 1, 1)), (42, at(1, 1, 1)), (44, at(2, 1, 1))):
        arrive_x(i, b)
        arrive_g(i + 1, b)
        prepare(b)
    loads[6].wait()
    links.finish()


def gather(features, cotangent, w_query, w_key, w_value, masks):
    nb, nr = lax.axis_size("blk"), lax.axis_size("reader")
    hbm, vmem = pl.BlockSpec(memory_space=pltpu.HBM), pl.BlockSpec(memory_space=VMEM)
    operands = (features, cotangent, w_query, w_key, w_value, masks)
    return pl.pallas_call(
        gather_kernel,
        out_shape=[
            VMEM((nb, D, BLOCK), BF16),
            VMEM((nb, D, BLOCK), BF16),
            VMEM((nb, BLOCK, D), BF16),
            VMEM((nb, BLOCK, D), BF16),
            VMEM((nr, BLOCK, D), BF16),
            VMEM((nr, BLOCK, D), BF16),
            VMEM((nr, D, BLOCK), BF16),
            VMEM((nr, D, BLOCK), BF16),
            VMEM(masks.shape, jnp.int32),
            VMEM((D, D), BF16),
            VMEM((D, D), BF16),
            VMEM((D, D), BF16),
        ],
        in_specs=[hbm] * 6,
        out_specs=[vmem] * 12,
        scratch_shapes=[
            VMEM((D, D), BF16),
            VMEM((D, D), BF16),
            VMEM((nb, BLOCK, D), BF16),
            VMEM((4, 2, BLOCK, D), BF16),
            pltpu.SemaphoreType.DMA((46,)),
            pltpu.SemaphoreType.DMA((46,)),
            pltpu.SemaphoreType.DMA((7,)),
        ],
        compiler_params=pltpu.CompilerParams(
            collective_id=0, has_side_effects=True, vmem_limit_bytes=16 * 2**20
        ),
        name="gather",
    )(*(pltpu.with_memory_space_constraint(a, pltpu.HBM) for a in operands))


def tile_bias(words, t, count):
    spread = jnp.concatenate(
        [jnp.broadcast_to(words[w : w + 1], (32, BLOCK)) for w in range(BLOCK // 32)], axis=0
    )
    key = lax.broadcasted_iota(jnp.int32, (BLOCK, BLOCK), 0)
    query = lax.broadcasted_iota(jnp.int32, (BLOCK, BLOCK), 1)
    own = jnp.where(key == query, jnp.where(t == 0, 1, 0), 0)
    bits = (lax.shift_right_logical(spread, key & 31) | own) & jnp.where(t < count, 1, 0)
    return jnp.where(bits > 0, 0.0, NEG_FILL).astype(F32)


def pair_product(left, right):
    zero = jnp.zeros((HEAD_DIM, BLOCK), right.dtype)
    top = jnp.concatenate([right[:HEAD_DIM], zero], axis=1)
    bottom = jnp.concatenate([zero, right[HEAD_DIM:]], axis=1)
    return dot(left, jnp.concatenate([top, bottom], axis=0))


UNROLL = 4


def stats_kernel(count_ref, coords_ref, qt_ref, gt_ref, k_ref, v_ref, mask_ref, out_ref, run):
    nb = out_ref.shape[0]
    row = lax.broadcasted_iota(jnp.int32, run.shape, 1)
    run[...] = jnp.where(row < HEADS, FLOOR, 0.0).astype(F32)
    count = count_ref[0, 0]

    def tile(t):
        qb, kb, p = (coords_ref[0, c, 0, t] for c in range(3))
        bias = tile_bias(mask_ref[p], t, count)
        peaks, totals, dots = [], [], []
        for pair in range(HEADS // 2):
            two = slice(pair * 128, pair * 128 + 128)
            s2 = pair_product(k_ref[kb, :, two], qt_ref[qb, two])
            d2 = pair_product(v_ref[kb, :, two], gt_ref[qb, two])
            for half in range(2):
                lanes = slice(half * BLOCK, (half + 1) * BLOCK)
                s = s2[:, lanes] + bias
                peak = jnp.max(s, axis=0, keepdims=True)
                e = jnp.exp(s - peak)
                peaks.append(peak)
                totals.append(jnp.sum(e, axis=0, keepdims=True))
                dots.append(jnp.sum(e * d2[:, lanes], axis=0, keepdims=True))
        return qb, *(jnp.concatenate(rows, axis=0) for rows in (peaks, totals, dots))

    def add(qb, peak, total, dots):
        before = run[qb, :HEADS]
        m = jnp.maximum(before, peak)
        old, new = jnp.exp(before - m), jnp.exp(peak - m)
        run[qb, :HEADS] = m
        run[qb, HEADS : 2 * HEADS] = run[qb, HEADS : 2 * HEADS] * old + total * new
        run[qb, 2 * HEADS :] = run[qb, 2 * HEADS :] * old + dots * new

    def step(g, carry):
        for found in [tile(g * UNROLL + u) for u in range(UNROLL)]:
            add(*found)
        return carry

    lax.fori_loop(0, (count + UNROLL - 1) // UNROLL, step, 0)
    for b in range(nb):
        total = jnp.maximum(run[b, HEADS : 2 * HEADS], 1e-30)
        out_ref[b, :HEADS] = run[b, :HEADS] + jnp.log(total)
        out_ref[b, HEADS:] = run[b, 2 * HEADS :] / total


def stats(count, coords, qt, gt, keys, values, masks):
    nb = qt.shape[0]
    smem, vmem = pl.BlockSpec(memory_space=pltpu.SMEM), pl.BlockSpec(memory_space=VMEM)
    return pl.pallas_call(
        stats_kernel,
        out_shape=VMEM((nb, 2 * HEADS, BLOCK), F32),
        in_specs=[smem, smem] + [vmem] * 5,
        out_specs=vmem,
        scratch_shapes=[VMEM((nb, 3 * HEADS, BLOCK), F32)],
        compiler_params=pltpu.CompilerParams(vmem_limit_bytes=8 * 2**20),
        name="stats",
    )(count, coords, qt, gt, keys, values, masks)


def merge_kernel(nb, st_ref, out_ref, acc, kacc, vacc, land, fin, send, recv, fsend, frecv):
    reader, blk = lax.axis_index("reader"), lax.axis_index("blk")
    peer = lambda d: lax.rem(blk + d, nb)
    source = lambda d: lax.rem(blk + nb - d, nb)
    barrier = pltpu.get_barrier_semaphore()
    for d in range(1, nb):
        pl.semaphore_signal(barrier, inc=1, device_id=(reader, peer(d)), device_id_type=MESH)

    def clear(ref):
        def one(b, carry):
            ref[b] = jnp.zeros(ref.shape[1:], F32)
            return carry

        lax.fori_loop(0, ref.shape[0], one, 0)

    def part(d):
        return remote(st_ref.at[peer(d)], land.at[d], send.at[d], recv.at[d], (reader, peer(d)))

    def whole(d):
        return remote(fin.at[0], fin.at[d], fsend.at[d], frecv.at[d], (reader, peer(d)))

    clear(kacc)
    pl.semaphore_wait(barrier, nb - 1)
    for d in range(1, nb):
        part(d).start()
    land[0] = st_ref[blk]
    clear(vacc)
    for d in range(1, nb):
        part(d).wait()
    m = land[0, :HEADS]
    for d in range(1, nb):
        m = jnp.maximum(m, land[d, :HEADS])
    total = jnp.zeros_like(m)
    dots = jnp.zeros_like(m)
    for d in range(nb):
        weight = jnp.exp(land[d, :HEADS] - m)
        total += weight
        dots += land[d, HEADS:] * weight
    fin[0, :HEADS] = m + jnp.log(total)
    fin[0, HEADS:] = dots / total
    for d in range(1, nb):
        whole(d).start()
    out_ref[blk] = fin[0]
    clear(acc)
    for d in range(1, nb):
        whole(d).wait()
        out_ref[source(d)] = fin[d]


def merge(partial, nr):
    nb = partial.shape[0]
    vmem = pl.BlockSpec(memory_space=VMEM)
    return pl.pallas_call(
        functools.partial(merge_kernel, nb),
        out_shape=[
            VMEM(partial.shape, F32),
            VMEM((nb, 2 * D, BLOCK), F32),
            VMEM((nr, BLOCK, D), F32),
            VMEM((nr, BLOCK, D), F32),
        ],
        in_specs=[vmem],
        out_specs=[vmem] * 4,
        scratch_shapes=[
            VMEM(partial.shape, F32),
            VMEM(partial.shape, F32),
            *[pltpu.SemaphoreType.DMA((nb,))] * 4,
        ],
        compiler_params=pltpu.CompilerParams(
            collective_id=1, has_side_effects=True, vmem_limit_bytes=4 * 2**20
        ),
        name="merge",
    )(partial)


def lane_split(block):
    lane = lax.broadcasted_iota(jnp.int32, block.shape, 1)
    zero = jnp.zeros_like(block)
    return jnp.concatenate(
        [jnp.where(lane < HEAD_DIM, block, zero), jnp.where(lane >= HEAD_DIM, block, zero)], axis=0
    )


def grad_kernel(
    count_ref, coords_ref, qt_ref, gt_ref, qn_ref, gn_ref, k_ref, v_ref, kt_ref, vt_ref, mask_ref, fin_ref, wkt_ref,
    wvt_ref, acc_in, kacc_in, vacc_in, acc, kacc, vacc, kv_ref, probs, dscores,
):
    count = count_ref[0, 0]

    def scores(t, u):
        qb, kb, p = (coords_ref[0, c, 0, t] for c in range(3))
        bias = tile_bias(mask_ref[p], t, count)
        for pair in range(HEADS // 2):
            two = slice(pair * 128, pair * 128 + 128)
            s2 = pair_product(k_ref[kb, :, two], qt_ref[qb, two])
            d2 = pair_product(v_ref[kb, :, two], gt_ref[qb, two])
            for half in range(2):
                h = pair * 2 + half
                lanes = slice(half * BLOCK, (half + 1) * BLOCK)
                prob = jnp.exp(s2[:, lanes] + bias - fin_ref[qb, h : h + 1])
                probs[u, h] = prob.astype(BF16)
                delta = fin_ref[qb, HEADS + h : HEADS + h + 1]
                dscores[u, h] = (prob * (d2[:, lanes] - delta)).astype(BF16)

    def products(t, u):
        qb, kb = coords_ref[0, 0, 0, t], coords_ref[0, 1, 0, t]
        for pair in range(HEADS // 2):
            for h in (2 * pair, 2 * pair + 1):
                head = slice(h * HEAD_DIM, (h + 1) * HEAD_DIM)
                ghead = slice(D + h * HEAD_DIM, D + (h + 1) * HEAD_DIM)
                acc[qb, head] += dot(vt_ref[kb, head], probs[u, h])
                acc[qb, ghead] += dot(kt_ref[kb, head], dscores[u, h])
            two = slice(pair * 128, pair * 128 + 128)
            low = jnp.concatenate([probs[u, 2 * pair], probs[u, 2 * pair + 1]], axis=1)
            ds = jnp.concatenate([dscores[u, 2 * pair], dscores[u, 2 * pair + 1]], axis=1)
            kacc[kb, :, two] += dot(ds, lane_split(qn_ref[qb, :, two]))
            vacc[kb, :, two] += dot(low, lane_split(gn_ref[qb, :, two]))

    def step(g, carry):
        for u in range(UNROLL):
            scores(g * UNROLL + u, u)
        for u in range(UNROLL):
            products(g * UNROLL + u, u)
        return carry

    lax.fori_loop(0, (count + UNROLL - 1) // UNROLL, step, 0)
    for side in range(2):
        rows = pl.ds(side * 4, 4)
        keys = kacc[rows].reshape(4 * BLOCK, D).astype(BF16)
        values = vacc[rows].reshape(4 * BLOCK, D).astype(BF16)
        total = dot(keys, wkt_ref[...]) + dot(values, wvt_ref[...])
        kv_ref[:, side] = total.reshape(4, BLOCK, D).astype(BF16)


def grads(count, coords, arrays, acc, kacc, vacc):
    smem, vmem = pl.BlockSpec(memory_space=pltpu.SMEM), pl.BlockSpec(memory_space=VMEM)
    first = 2 + len(arrays)
    out = pl.pallas_call(
        grad_kernel,
        out_shape=[
            VMEM(acc.shape, F32),
            VMEM(kacc.shape, F32),
            VMEM(vacc.shape, F32),
            VMEM((4, 2, BLOCK, D), BF16),
        ],
        in_specs=[smem, smem] + [vmem] * (len(arrays) + 3),
        out_specs=[vmem] * 4,
        scratch_shapes=[VMEM((UNROLL, HEADS, BLOCK, BLOCK), BF16)] * 2,
        input_output_aliases={first: 0, first + 1: 1, first + 2: 2},
        compiler_params=pltpu.CompilerParams(vmem_limit_bytes=12 * 2**20),
        name="grads",
    )(count, coords, *arrays, acc, kacc, vacc)
    return out[0], out[3]


def reduce_kernel(
    p_ref, kv_ref, wq_ref, attn_ref, grad_ref,
    to_sib, from_sib, sums, land, kland, ksum, send, recv,
):
    reader, blk, z, x, core, xh, y = place()
    zp, zm, xn, sib, yp, ym, xp = neighbours()
    links = Links(send, recv, sib)
    at = blocks()
    y_m, y_p, y_2 = lax.rem(y + 3, 4), lax.rem(y + 1, 4), lax.rem(y + 2, 4)
    order = [(2, 1), (1, 1), (3, 1), (2, 0), (0, 1), (1, 0), (3, 0), (0, 0)]
    part = lambda c: pl.ds(c * D, D)
    parts = [(i, c) for i in range(8) for c in range(2)]
    parts = [(0, 0), (1, 0), (2, 0), (0, 1), (1, 1), (2, 1)] + parts[6:]

    barrier = pltpu.get_barrier_semaphore()
    for device in (zp, zm, xn, sib, yp, ym, xp):
        pl.semaphore_signal(barrier, inc=1, device_id=device, device_id_type=MESH)
    for i, c in parts[:6]:
        to_sib[i, c] = p_ref[at(*order[i], 1), part(c)].astype(BF16)
    pl.semaphore_wait(barrier, 7)
    for i, c in parts[:6]:
        links.start(40 + 2 * i + c, to_sib.at[i, c], from_sib.at[i, c], sib)
    links.start(0, kv_ref.at[y_2, 0], kland.at[0, 0], yp)
    links.start(1, kv_ref.at[y_2, 1], kland.at[0, 1], ym)
    links.start(2, kv_ref.at[y_p, 1], kland.at[1, 1], yp)
    links.start(3, kv_ref.at[y_m, 0], kland.at[2, 0], ym)
    for i, c in parts[6:]:
        to_sib[i, c] = p_ref[at(*order[i], 1), part(c)].astype(BF16)
        links.start(40 + 2 * i + c, to_sib.at[i, c], from_sib.at[i, c], sib)

    def both(i, c):
        links.arrive(40 + 2 * i + c, from_sib.at[i, c])
        return p_ref[at(*order[i]), part(c)] + from_sib[i, c].astype(F32)

    def put(channel, i, c, value, slot, device):
        sums[i, c] = value.astype(BF16)
        links.start(channel, sums.at[i, c], land.at[slot, c], device)

    def landed(channel, slot, c):
        links.arrive(channel, land.at[slot, c])
        return land[slot, c].astype(F32)

    for c in range(2):
        put(10 + c, 0, c, both(0, c), 0, xn)
        put(12 + c, 1, c, both(1, c), 1, zp)
        put(14 + c, 2, c, both(2, c), 2, zm)
    far = [both(3, c) for c in range(2)]
    put(16, 3, 0, far[0] + landed(10, 0, 0), 6, zp)

    links.arrive(0, kland.at[0, 0])
    ksum[0] = (kv_ref[y_p, 0].astype(F32) + kland[0, 0].astype(F32)).astype(BF16)
    links.start(4, ksum.at[0], kland.at[1, 0], yp)
    links.arrive(1, kland.at[0, 1])
    ksum[1] = (kv_ref[y_m, 1].astype(F32) + kland[0, 1].astype(F32)).astype(BF16)
    links.start(5, ksum.at[1], kland.at[2, 1], ym)

    put(18, 4, 0, both(4, 0) + landed(12, 1, 0) + landed(14, 2, 0), 3, xn)
    put(17, 3, 1, far[1] + landed(11, 0, 1), 6, zm)
    put(21, 5, 1, both(5, 1), 4, zp)
    put(22, 6, 0, both(6, 0), 5, zm)
    put(19, 4, 1, both(4, 1) + landed(13, 1, 1) + landed(15, 2, 1), 3, xn)

    up, down = both(5, 0), both(6, 1)
    put(20, 5, 0, up + landed(16, 6, 0), 4, zp)
    put(23, 6, 1, down + landed(17, 6, 1), 5, zm)

    links.arrive(4, kland.at[1, 0])
    links.arrive(2, kland.at[1, 1])
    links.arrive(3, kland.at[2, 0])
    links.arrive(5, kland.at[2, 1])
    ksum[2] = (
        kv_ref[y, 1 - xh].astype(F32) + kland[1, 1 - xh].astype(F32) + kland[2, 1 - xh].astype(F32)
    ).astype(BF16)
    links.start(6, ksum.at[2], ksum.at[3], xp)
    nodes = kv_ref[y, xh].astype(F32) + kland[1, xh].astype(F32) + kland[2, xh].astype(F32)

    outputs = both(7, 0) + landed(18, 3, 0)
    queries = both(7, 1) + landed(19, 3, 1)
    links.arrive(6, ksum.at[3])
    nodes += ksum[3].astype(F32)
    outputs += landed(22, 5, 0)
    queries += landed(21, 4, 1)
    outputs += landed(20, 4, 0)
    attn_ref[...] = outputs.T.astype(BF16)
    queries += landed(23, 5, 1)
    nodes += dot(wq_ref[...], (queries * SCALE).astype(BF16)).T
    grad_ref[...] = nodes.astype(BF16)
    links.finish()


def reduce(parts, key_parts, w_query):
    vmem = pl.BlockSpec(memory_space=VMEM)
    block = (2, D, BLOCK)
    return pl.pallas_call(
        reduce_kernel,
        out_shape=[jax.ShapeDtypeStruct((BLOCK, D), BF16)] * 2,
        in_specs=[vmem] * 3,
        out_specs=[vmem] * 2,
        scratch_shapes=[
            VMEM((8, *block), BF16),
            VMEM((8, *block), BF16),
            VMEM((7, *block), BF16),
            VMEM((7, *block), BF16),
            VMEM((3, 2, BLOCK, D), BF16),
            VMEM((4, BLOCK, D), BF16),
            pltpu.SemaphoreType.DMA((56,)),
            pltpu.SemaphoreType.DMA((56,)),
        ],
        compiler_params=pltpu.CompilerParams(
            collective_id=2, has_side_effects=True, vmem_limit_bytes=24 * 2**20
        ),
        name="reduce",
    )(parts, key_parts, w_query)


def local(features, cotangent, w_query, w_key, w_value, tile_coords, tile_count, mask_table):
    masks = mask_table.transpose(0, 2, 1)
    coords = tile_coords.transpose(0, 3, 1, 2)
    qt, gt, qn, gn, keys, values, keys_t, values_t, masks, wq, wkt, wvt = gather(
        features, cotangent, w_query, w_key, w_value, masks
    )
    partial = stats(tile_count, coords, qt, gt, keys, values, masks)
    fin, acc, kacc, vacc = merge(partial, keys.shape[0])
    arrays = (qt, gt, qn, gn, keys, values, keys_t, values_t, masks, fin, wkt, wvt)
    parts, key_parts = grads(tile_count, coords, arrays, acc, kacc, vacc)
    return tuple(reduce(parts, key_parts, wq))


def solution(mesh):
    return jax.shard_map(
        local,
        mesh=mesh,
        in_specs=(
            P(("reader", "blk"), None),
            P(("reader", "blk"), None),
            P(),
            P(),
            P(),
            P("reader", "blk", None, None),
            P("reader", "blk"),
            P(),
        ),
        out_specs=(P(("reader", "blk"), None), P(("reader", "blk"), None)),
        check_vma=False,
    )
```

time: 100 us -> 88 us (0.88)
  the two profiles are of different devices: /device:TPU:0 before, /device:TPU:8 now
where the time goes in v3:
time: 88 us; the launch traced here: 87.9 us
  Pallas kernels  85.2 us (97%)
  between operations  1.35 us (2%)
  local copies, waits for them, and re-layouts  1.32 us (2%)
    pallas_call x1, Pallas kernels, reduce(): pl.pallas_call(reduce_kernel, out_shape=[jax.ShapeDtypeStruct((BLOCK, D),...  32.6 us
    pallas_call x1, Pallas kernels, gather(): pl.pallas_call(gather_kernel, out_shape=[VMEM((nb, D, BLOCK), BF16), VMEM...  27.3 us
    pallas_call x1, Pallas kernels, merge(): pl.pallas_call(functools.partial(merge_kernel, nb), out_shape=[VMEM(parti...  11.4 us
    pallas_call x1, Pallas kernels, grads(): pl.pallas_call(grad_kernel, out_shape=[VMEM(acc.shape, F32), VMEM(kacc.sh...  9.55 us
    pallas_call x1, Pallas kernels, stats(): pl.pallas_call(stats_kernel, out_shape=VMEM((nb, 2 * HEADS, BLOCK), F32),...  4.39 us

profile of v3, /device:TPU:8, one launch (start us, length us, event | category | flops | bytes accessed | tf_op | source)
XLA Modules:
  0.0 87.9 jit_solution(9714856789385017628)
XLA Ops:
  0.6 0.0 copy-start
  1.3 27.3 %gather.1 = (bf16[16,512,128]{2,1,0:T(8,128)(2,1)S(1)}, bf16[16,512,128]{2,1,0:T(8,128)(2,1)S(1)}, bf16[16,128,512]{2,1,0:T(8,128)(2,1)S(1)}, bf16[16,128,512]{2...) custom-call(bf16[128,512]{1,0:T(8,128)(2,1)} %x_hbm.1, ...), custom_call_target="tpu_custom_call" | custom-call | tf_op jit(solution)/shard_map/gather/pallas_call | solution.py:244
  28.6 0.0 copy-done
  28.6 4.4 %stats.1.st_ref = f32[16,16,128]{2,1,0:T(8,128)S(1)} custom-call(s32[1,1]{1,0:T(1,128)S(6)} %copy.18.count_ref, s32[1,3,1,32]{3,2,1,0:T(1,128)S(1)} %bitcast.2, bf16[16,512,128]{2,1,0:T(8,128)(2,1)S(1)} %get-tuple-element.20.qt_ref, bf16[16,512,128]{2,1,0:T(8,128)(2,1)S(1)} %get-tuple-element.21.gt_ref, bf16[8,128,512]{2,1,0:T(8,128)(2,1)S(1)} %get-tuple-element.24.k_ref, ...), custom_call_target="tpu_custom_call" | custom-call | tf_op jit(solution)/shard_map/stats/pallas_call | solution.py:346
  33.0 11.4 %merge.1 = (f32[16,16,128]{2,1,0:T(8,128)S(1)}, f32[16,1024,128]{2,1,0:T(8,128)S(1)}, f32[8,128,512]{2,1,0:T(8,128)S(1)}, f32[8,128,512]{2,1,0:T(8,128)S(1)}) custom-call(f32[16,16,128]{2,1,0:T(8,128)S(1)} %stats.1.st_ref), custom_call_target="tpu_custom_call" | custom-call | tf_op jit(solution)/shard_map/merge/pallas_call | solution.py:409
  44.4 9.6 %grads.1 = (f32[16,1024,128]{2,1,0:T(8,128)S(1)}, f32[8,128,512]{2,1,0:T(8,128)S(1)}, f32[8,128,512]{2,1,0:T(8,128)S(1)}, bf16[4,2,128,512]{3,2,1,0:T(8,128)(2,1)S(1)}) custom-call(s32[1,1]{1,0:T(1,128)S(6)} %copy.18.count_ref, s32[1,3,1,32]{3,2,1,0:T(1,128)S(1)} %bitcast.3, ...), custom_call_target="tpu_custom_call", output_to_operand_aliasing={{0}: (14, {}), {1}: (15, {}), {2}: (16, {})} | custom-call | tf_op jit(solution)/shard_map/grads/pallas_call | solution.py:493
  54.0 32.6 %reduce.1 = (bf16[128,512]{1,0:T(8,128)(2,1)S(1)}, bf16[128,512]{1,0:T(8,128)(2,1)S(1)}) custom-call(f32[16,1024,128]{2,1,0:T(8,128)S(1)} %get-tuple-element.35.p_ref, bf16[4,2,128,512]{3,2,1,0:T(8,128)(2,1)S(1)} %get-tuple-element.36.kv_ref, bf16[512,512]{1,0:T(8,128)(2,1)S(1)} %get-tuple-element.37.wq_ref), custom_call_target="tpu_custom_call" | custom-call | tf_op jit(solution)/shard_map/reduce/pallas_call | solution.py:604
  86.6 0.7 copy.19
  87.2 0.7 copy.20
Async XLA Ops:
  0.6 28.0 %copy-start = (s32[1,1,32,3]{2,1,3,0:T(1,128)S(1)}, s32[1,1,32,3]{2,1,3,0:T(1,128)}, u32[]{:S(2)}) copy-start(s32[1,1,32,3]{2,1,3,0:T(1,128)} %param.13) | copy-start | bytes 1156

commit v4 on v3

v4 whole, which is shorter than its diff:
```python
import functools

import jax
import jax.numpy as jnp
from jax import lax
from jax.experimental import pallas as pl
from jax.experimental.pallas import tpu as pltpu
from jax.sharding import PartitionSpec as P

HEADS = 8
HEAD_DIM = 64
D = 512
BLOCK = 128
SCALE = 0.125
FLOOR = -1e20
NEG_FILL = -1e30
MESH = pl.DeviceIdType.MESH
F32 = jnp.float32
BF16 = jnp.bfloat16
VMEM = pltpu.VMEM


def dot(a, b):
    return jnp.dot(a, b, preferred_element_type=F32)


def remote(src, dst, send, recv, device):
    return pltpu.make_async_remote_copy(
        src_ref=src, dst_ref=dst, send_sem=send, recv_sem=recv, device_id=device, device_id_type=MESH
    )


class Links:
    def __init__(self, send, recv, self_device):
        self.send, self.recv, self.anyone, self.started = send, recv, self_device, {}

    def start(self, i, src, dst, device):
        copy = remote(src, dst, self.send.at[i], self.recv.at[i], device)
        self.started[i] = copy
        copy.start()

    def arrive(self, i, dst):
        remote(dst, dst, self.send.at[i], self.recv.at[i], self.anyone).wait_recv()

    def finish(self):
        for copy in self.started.values():
            copy.wait_send()


def place():
    reader, blk = lax.axis_index("reader"), lax.axis_index("blk")
    side = lax.rem(blk // 2, 2)
    return (reader // 4) * 2 + side, lax.rem(reader, 4), blk // 4, lax.rem(blk, 2), side


def device(x, y, z, core):
    return (x // 2) * 4 + y, z * 4 + lax.rem(x, 2) * 2 + core


def ahead(i, d):
    return lax.rem(i + d, 4)


def neighbours():
    x, y, z, core, _ = place()
    return (
        device(ahead(x, 1), y, z, core),
        device(ahead(x, 3), y, z, core),
        device(x, ahead(y, 1), z, core),
        device(x, ahead(y, 3), z, core),
        device(x, y, ahead(z, 1), core),
        device(x, y, ahead(z, 3), core),
        device(x, y, z, 1 - core),
    )


def enter():
    barrier = pltpu.get_barrier_semaphore()
    for one in neighbours():
        pl.semaphore_signal(barrier, inc=1, device_id=one, device_id_type=MESH)
    return lambda: pl.semaphore_wait(barrier, 7)


HALF = BLOCK // 2
QUARTER = HALF // 2


class HalfGather:
    def __init__(self, links, base, buf, source, first, second):
        self.links, self.base, self.buf, self.source = links, base, buf, source
        self.me1, self.up1, self.down1 = first
        self.me2, self.up2, self.down2 = second

    def piece(self, d1, d2):
        return self.buf.at[ahead(self.me2, d2), ahead(self.me1, d1)]

    def quarter(self, d1, q):
        return self.buf.at[self.me2, ahead(self.me1, d1), pl.ds(q * QUARTER, QUARTER)]

    def spread(self, d1, src=None):
        ref = self.piece(d1, 0)
        self.links.start(self.base + 4 + d1, ref if src is None else src, ref, self.up2)
        self.links.start(self.base + 8 + d1, ref if src is None else src, ref, self.down2)

    def own(self):
        ref = self.piece(0, 0)
        self.links.start(self.base, self.source, ref, self.up1)
        self.links.start(self.base + 1, self.source, ref, self.down1)
        self.spread(0, self.source)

    def near(self):
        self.links.arrive(self.base, self.piece(3, 0))
        self.links.start(self.base + 2, self.quarter(3, 0), self.quarter(3, 0), self.up1)
        self.spread(3)
        self.links.arrive(self.base + 1, self.piece(1, 0))
        self.links.start(self.base + 3, self.quarter(1, 1), self.quarter(1, 1), self.down1)
        self.spread(1)

    def far(self):
        self.links.arrive(self.base + 2, self.quarter(2, 0))
        self.links.arrive(self.base + 3, self.quarter(2, 1))
        self.spread(2)

    def relay(self, d1):
        up = d1 < 2
        ref = self.piece(d1, 3 if up else 1)
        self.links.arrive(self.base + (4 if up else 8) + d1, ref)
        self.links.start(self.base + 12 + d1, ref, ref, self.up2 if up else self.down2)

    def rest(self, up):
        for d1 in (3, 2) if up else (0, 1):
            self.links.arrive(self.base + (4 if up else 8) + d1, self.piece(d1, 3 if up else 1))

    def last(self):
        for d1 in (0, 3, 1, 2):
            self.links.arrive(self.base + 12 + d1, self.piece(d1, 2))


def gather_kernel(
    x_hbm, g_hbm, wq_hbm, wk_hbm, wv_hbm, mask_hbm, coords_hbm, count_ref,
    qt_ref, gt_ref, qn_ref, gn_ref, k_ref, v_ref, mask_ref, wq_ref, wk_ref, wv_ref, coords_own, coords_out, count_out,
    xb, low, high, count_buf, send, recv, local,
):
    x, y, z, core, side = place()
    xp, xm, yp, ym, zp, zm, sib = neighbours()
    links = Links(send, recv, sib)
    begin = enter()
    count_buf[...] = jnp.full(count_buf.shape, count_ref[0, 0], jnp.int32)
    loads = [
        pltpu.make_async_copy(src, dst, local.at[i])
        for i, (src, dst) in enumerate(
            [
                (x_hbm.at[pl.ds(0, HALF)], low.at[y, x]), (x_hbm.at[pl.ds(HALF, HALF)], high.at[x, y]),
                (wk_hbm, wk_ref), (wv_hbm, wv_ref), (x_hbm, xb.at[z, core]), (g_hbm, gn_ref.at[z, core]),
                (wq_hbm, wq_ref), (mask_hbm, mask_ref), (coords_hbm, coords_own),
            ]
        )
    ]
    for load in loads:
        load.start()
    rings = [
        HalfGather(links, 16, low, x_hbm.at[pl.ds(0, HALF)], (x, xp, xm), (y, yp, ym)),
        HalfGather(links, 32, high, x_hbm.at[pl.ds(HALF, HALF)], (y, yp, ym), (x, xp, xm)),
    ]
    begin()

    for ring in rings:
        ring.own()
    links.start(0, x_hbm, xb.at[z, core], zp)
    links.start(2, x_hbm, xb.at[z, core], zm)
    links.start(1, g_hbm, gn_ref.at[z, core], zp)
    links.start(3, g_hbm, gn_ref.at[z, core], zm)
    links.start(8, x_hbm, xb.at[z, core], sib)
    links.start(9, g_hbm, gn_ref.at[z, core], sib)
    other = device(x + 1 - 2 * side, y, z, core)
    links.start(6, coords_hbm, coords_out, other)
    links.start(7, count_buf, count_out, other)

    def arrive(i, ref, dz, c=core):
        links.arrive(i, ref.at[ahead(z, dz), c])

    def pass_on(i, ref, dz, to):
        block = ref.at[ahead(z, dz), core]
        links.start(i, block, block, to)

    def prepare(dz):
        b = ahead(z, dz)
        rows = xb[b].reshape(2 * BLOCK, D)
        q = (dot(rows, wq_ref[...]).astype(BF16).astype(F32) * SCALE).astype(BF16)
        for c in range(2):
            one = q[c * BLOCK : (c + 1) * BLOCK]
            qn_ref[b, c] = one
            qt_ref[b, c] = one.T
            gt_ref[b, c] = gn_ref[b, c].T

    def project(half, d):
        at = ahead(x if half else y, d)
        rows = (high if half else low)[at].reshape(4 * HALF, D)
        for weight, out in ((wk_ref, k_ref), (wv_ref, v_ref)):
            found = dot(rows, weight[...]).astype(BF16).reshape(4, HALF, D)
            if half:
                out[at, :, HALF:] = found
            else:
                out[:, at, :HALF] = found

    for i in range(7):
        loads[i].wait()
    for ring in rings:
        ring.near()
    for ring in rings:
        ring.relay(0)
    arrive(0, xb, 3)
    pass_on(4, xb, 3, zp)
    for ring in rings:
        ring.far()
    for ring in rings:
        ring.relay(3)
        ring.relay(1)
    pass_on(10, xb, 3, sib)
    arrive(2, xb, 1)
    pass_on(12, xb, 1, sib)
    project(0, 0)
    project(1, 0)

    arrive(3, gn_ref, 1)
    pass_on(5, gn_ref, 1, zm)
    pass_on(13, gn_ref, 1, sib)
    arrive(1, gn_ref, 3)
    pass_on(11, gn_ref, 3, sib)
    for ring in rings:
        ring.relay(2)
    arrive(8, xb, 0, 1 - core)
    arrive(9, gn_ref, 0, 1 - core)
    prepare(0)
    for half, ring in enumerate(rings):
        ring.rest(True)
        project(half, 3)
        ring.rest(False)
        project(half, 1)
    arrive(4, xb, 2)
    pass_on(14, xb, 2, sib)
    for i, dz in ((10, 3), (12, 1)):
        arrive(i, xb, dz, 1 - core)
        arrive(i + 1, gn_ref, dz, 1 - core)
        prepare(dz)
        if i == 10:
            arrive(5, gn_ref, 2)
            pass_on(15, gn_ref, 2, sib)
    for half, ring in enumerate(rings):
        ring.last()
        project(half, 2)
    arrive(14, xb, 2, 1 - core)
    arrive(15, gn_ref, 2, 1 - core)
    prepare(2)
    links.arrive(6, coords_out)
    links.arrive(7, count_out)
    loads[7].wait()
    loads[8].wait()
    links.finish()


def gather(features, cotangent, w_query, w_key, w_value, masks, coords, count):
    hbm, vmem = pl.BlockSpec(memory_space=pltpu.HBM), pl.BlockSpec(memory_space=VMEM)
    operands = (features, cotangent, w_query, w_key, w_value, masks, coords)
    return pl.pallas_call(
        gather_kernel,
        out_shape=[
            VMEM((4, 2, D, BLOCK), BF16),
            VMEM((4, 2, D, BLOCK), BF16),
            VMEM((4, 2, BLOCK, D), BF16),
            VMEM((4, 2, BLOCK, D), BF16),
            VMEM((4, 4, BLOCK, D), BF16),
            VMEM((4, 4, BLOCK, D), BF16),
            VMEM(masks.shape, jnp.int32),
            VMEM((D, D), BF16),
            VMEM((D, D), BF16),
            VMEM((D, D), BF16),
            VMEM(coords.shape, jnp.int32),
            VMEM(coords.shape, jnp.int32),
            VMEM((8, 128), jnp.int32),
        ],
        in_specs=[hbm] * 7 + [pl.BlockSpec(memory_space=pltpu.SMEM)],
        out_specs=[vmem] * 13,
        scratch_shapes=[
            VMEM((4, 2, BLOCK, D), BF16),
            VMEM((4, 4, HALF, D), BF16),
            VMEM((4, 4, HALF, D), BF16),
            VMEM((8, 128), jnp.int32),
            pltpu.SemaphoreType.DMA((48,)),
            pltpu.SemaphoreType.DMA((48,)),
            pltpu.SemaphoreType.DMA((9,)),
        ],
        compiler_params=pltpu.CompilerParams(
            collective_id=0, has_side_effects=True, vmem_limit_bytes=16 * 2**20
        ),
        name="gather",
    )(*(pltpu.with_memory_space_constraint(a, pltpu.HBM) for a in operands), count)


def tile_bias(words, first, used):
    spread = jnp.concatenate(
        [jnp.broadcast_to(words[w : w + 1], (32, BLOCK)) for w in range(BLOCK // 32)], axis=0
    )
    key = lax.broadcasted_iota(jnp.int32, (BLOCK, BLOCK), 0)
    query = lax.broadcasted_iota(jnp.int32, (BLOCK, BLOCK), 1)
    bits = (lax.shift_right_logical(spread, key & 31) | jnp.where(key == query, first, 0)) & used
    return jnp.where(bits > 0, 0.0, NEG_FILL).astype(F32)


def pair_product(left, right):
    zero = jnp.zeros((HEAD_DIM, BLOCK), right.dtype)
    top = jnp.concatenate([right[:HEAD_DIM], zero], axis=1)
    bottom = jnp.concatenate([zero, right[HEAD_DIM:]], axis=1)
    return dot(left, jnp.concatenate([top, bottom], axis=0))


UNROLL = 4
LIST = 2 * 32 + UNROLL


def stats_kernel(
    count_ref, coords_ref, count2_ref, coords2_ref, qt_ref, gt_ref, k_ref, v_ref, mask_ref, out_ref, list_ref, run
):
    nb = run.shape[0]
    row = lax.broadcasted_iota(jnp.int32, run.shape, 1)
    run[...] = jnp.where(row < HEADS, FLOOR, 0.0).astype(F32)
    side = lax.rem(lax.axis_index("blk") // 2, 2)

    def collect(counts, coords, column, found):
        def one(i, found):
            qb, kb, p = (coords[0, c, 0, i] for c in range(3))
            list_ref[0, found] = lax.shift_right_logical(qb, 2) * 2 + (qb & 1)
            list_ref[1, found] = (lax.shift_right_logical(kb, 2) * 2 + column) * 4 + (kb & 3)
            list_ref[2, found] = p
            list_ref[3, found] = jnp.where(i + found + (column != side) == 0, 1, 0)
            list_ref[4, found] = 1
            return found + jnp.where((lax.shift_right_logical(qb, 1) & 1) == side, 1, 0)

        return lax.fori_loop(0, counts[0, 0], one, found)

    count = collect(count_ref, coords_ref, side, 0)
    count = collect(count2_ref, coords2_ref, 1 - side, count)
    for u in range(UNROLL):
        for i in range(5):
            list_ref[i, count + u] = 0
    list_ref[5, 0] = count

    def tile(t):
        qb, kb, p = (list_ref[c, t] for c in range(3))
        bias = tile_bias(mask_ref[p], list_ref[3, t], list_ref[4, t])
        peaks, totals, dots = [], [], []
        for pair in range(HEADS // 2):
            two = slice(pair * 128, pair * 128 + 128)
            s2 = pair_product(k_ref[kb, :, two], qt_ref[qb, two])
            d2 = pair_product(v_ref[kb, :, two], gt_ref[qb, two])
            for half in range(2):
                lanes = slice(half * BLOCK, (half + 1) * BLOCK)
                s = s2[:, lanes] + bias
                peak = jnp.max(s, axis=0, keepdims=True)
                e = jnp.exp(s - peak)
                peaks.append(peak)
                totals.append(jnp.sum(e, axis=0, keepdims=True))
                dots.append(jnp.sum(e * d2[:, lanes], axis=0, keepdims=True))
        return qb, *(jnp.concatenate(rows, axis=0) for rows in (peaks, totals, dots))

    def add(qb, peak, total, dots):
        before = run[qb, :HEADS]
        m = jnp.maximum(before, peak)
        old, new = jnp.exp(before - m), jnp.exp(peak - m)
        run[qb, :HEADS] = m
        run[qb, HEADS : 2 * HEADS] = run[qb, HEADS : 2 * HEADS] * old + total * new
        run[qb, 2 * HEADS :] = run[qb, 2 * HEADS :] * old + dots * new

    def step(g, carry):
        for found in [tile(g * UNROLL + u) for u in range(UNROLL)]:
            add(*found)
        return carry

    lax.fori_loop(0, (count + UNROLL - 1) // UNROLL, step, 0)
    for b in range(nb):
        total = jnp.maximum(run[b, HEADS : 2 * HEADS], 1e-30)
        out_ref[b, :HEADS] = run[b, :HEADS] + jnp.log(total)
        out_ref[b, HEADS:] = run[b, 2 * HEADS :] / total


def stats(count, coords, count2, coords2, qt, gt, keys, values, masks):
    nb = qt.shape[0]
    smem, vmem = pl.BlockSpec(memory_space=pltpu.SMEM), pl.BlockSpec(memory_space=VMEM)
    return pl.pallas_call(
        stats_kernel,
        out_shape=[VMEM((nb, 2 * HEADS, BLOCK), F32), jax.ShapeDtypeStruct((8, LIST), jnp.int32)],
        in_specs=[smem] * 4 + [vmem] * 5,
        out_specs=[vmem, smem],
        scratch_shapes=[VMEM((nb, 3 * HEADS, BLOCK), F32)],
        compiler_params=pltpu.CompilerParams(vmem_limit_bytes=8 * 2**20),
        name="stats",
    )(count, coords, count2, coords2, qt, gt, keys, values, masks)


def merge_kernel(
    st_ref, k_ref, v_ref, wk_ref, wv_ref, out_ref, acc, kacc, vacc, kt_ref, vt_ref, wkt_ref, wvt_ref,
    land, fin, send, recv, fsend, frecv,
):
    x, y, z, core, _ = place()
    nb = st_ref.shape[0]
    me = z * 2 + core
    block = lambda d: lax.rem(me + d, nb)
    peer = lambda d: device(x, y, block(d) // 2, lax.rem(block(d), 2))
    source = lambda d: lax.rem(me + nb - d, nb)
    barrier = pltpu.get_barrier_semaphore()
    for d in range(1, nb):
        pl.semaphore_signal(barrier, inc=1, device_id=peer(d), device_id_type=MESH)

    def part(d):
        return remote(st_ref.at[block(d)], land.at[d], send.at[d], recv.at[d], peer(d))

    def whole(d):
        return remote(fin.at[0], fin.at[d], fsend.at[d], frecv.at[d], peer(d))

    def turn(b, carry):
        kt_ref[b] = k_ref[b].T
        vt_ref[b] = v_ref[b].T
        return carry

    def clear(b, carry):
        kacc[b] = jnp.zeros(kacc.shape[1:], F32)
        vacc[b] = jnp.zeros(vacc.shape[1:], F32)
        return carry

    def clear_queries(b, carry):
        acc[b] = jnp.zeros(acc.shape[1:], F32)
        return carry

    wkt_ref[...] = wk_ref[...].T
    wvt_ref[...] = wv_ref[...].T
    pl.semaphore_wait(barrier, nb - 1)
    for d in range(1, nb):
        part(d).start()
    land[0] = st_ref[me]
    lax.fori_loop(0, 16, turn, 0)
    for d in range(1, nb):
        part(d).wait()
    m = land[0, :HEADS]
    for d in range(1, nb):
        m = jnp.maximum(m, land[d, :HEADS])
    total = jnp.zeros_like(m)
    dots = jnp.zeros_like(m)
    for d in range(nb):
        weight = jnp.exp(land[d, :HEADS] - m)
        total += weight
        dots += land[d, HEADS:] * weight
    fin[0, :HEADS] = m + jnp.log(total)
    fin[0, HEADS:] = dots / total
    for d in range(1, nb):
        whole(d).start()
    out_ref[me] = fin[0]
    lax.fori_loop(0, 16, clear, 0)
    lax.fori_loop(0, nb, clear_queries, 0)
    for d in range(1, nb):
        whole(d).wait()
        out_ref[source(d)] = fin[d]


def merge(partial, keys, values, wk, wv):
    nb, nk = partial.shape[0], keys.shape[0]
    vmem = pl.BlockSpec(memory_space=VMEM)
    return pl.pallas_call(
        merge_kernel,
        out_shape=[
            VMEM(partial.shape, F32),
            VMEM((nb, 2 * D, BLOCK), F32),
            VMEM((nk, BLOCK, D), F32),
            VMEM((nk, BLOCK, D), F32),
            VMEM((nk, D, BLOCK), BF16),
            VMEM((nk, D, BLOCK), BF16),
            VMEM((D, D), BF16),
            VMEM((D, D), BF16),
        ],
        in_specs=[vmem] * 5,
        out_specs=[vmem] * 8,
        scratch_shapes=[
            VMEM(partial.shape, F32),
            VMEM(partial.shape, F32),
            *[pltpu.SemaphoreType.DMA((nb,))] * 4,
        ],
        compiler_params=pltpu.CompilerParams(
            collective_id=1, has_side_effects=True, vmem_limit_bytes=4 * 2**20
        ),
        name="merge",
    )(partial, keys, values, wk, wv)


def lane_split(block):
    lane = lax.broadcasted_iota(jnp.int32, block.shape, 1)
    zero = jnp.zeros_like(block)
    return jnp.concatenate(
        [jnp.where(lane < HEAD_DIM, block, zero), jnp.where(lane >= HEAD_DIM, block, zero)], axis=0
    )


def grad_kernel(
    list_ref, qt_ref, gt_ref, qn_ref, gn_ref, k_ref, v_ref, kt_ref, vt_ref, mask_ref, fin_ref, wkt_ref,
    wvt_ref, acc_in, kacc_in, vacc_in, acc, kacc, vacc, low_ref, high_ref, probs, dscores,
):
    count = list_ref[5, 0]

    def scores(t, u):
        qb, kb, p = (list_ref[c, t] for c in range(3))
        bias = tile_bias(mask_ref[p], list_ref[3, t], list_ref[4, t])
        for pair in range(HEADS // 2):
            two = slice(pair * 128, pair * 128 + 128)
            s2 = pair_product(k_ref[kb, :, two], qt_ref[qb, two])
            d2 = pair_product(v_ref[kb, :, two], gt_ref[qb, two])
            for half in range(2):
                h = pair * 2 + half
                lanes = slice(half * BLOCK, (half + 1) * BLOCK)
                prob = jnp.exp(s2[:, lanes] + bias - fin_ref[qb, h : h + 1])
                probs[u, h] = prob.astype(BF16)
                delta = fin_ref[qb, HEADS + h : HEADS + h + 1]
                dscores[u, h] = (prob * (d2[:, lanes] - delta)).astype(BF16)

    def products(t, u):
        qb, kb = list_ref[0, t], list_ref[1, t]
        for pair in range(HEADS // 2):
            for h in (2 * pair, 2 * pair + 1):
                head = slice(h * HEAD_DIM, (h + 1) * HEAD_DIM)
                ghead = slice(D + h * HEAD_DIM, D + (h + 1) * HEAD_DIM)
                acc[qb, head] += dot(vt_ref[kb, head], probs[u, h])
                acc[qb, ghead] += dot(kt_ref[kb, head], dscores[u, h])
            two = slice(pair * 128, pair * 128 + 128)
            low = jnp.concatenate([probs[u, 2 * pair], probs[u, 2 * pair + 1]], axis=1)
            ds = jnp.concatenate([dscores[u, 2 * pair], dscores[u, 2 * pair + 1]], axis=1)
            kacc[kb, :, two] += dot(ds, lane_split(qn_ref[qb, :, two]))
            vacc[kb, :, two] += dot(low, lane_split(gn_ref[qb, :, two]))

    def step(g, carry):
        for u in range(UNROLL):
            scores(g * UNROLL + u, u)
        for u in range(UNROLL):
            products(g * UNROLL + u, u)
        return carry

    lax.fori_loop(0, (count + UNROLL - 1) // UNROLL, step, 0)
    for x in range(4):
        rows = pl.ds(x * 4, 4)
        keys = kacc[rows].reshape(4 * BLOCK, D).astype(BF16)
        values = vacc[rows].reshape(4 * BLOCK, D).astype(BF16)
        total = (dot(keys, wkt_ref[...]) + dot(values, wvt_ref[...])).reshape(4, BLOCK, D).astype(BF16)
        low_ref[:, x] = total[:, :HALF]
        high_ref[x] = total[:, HALF:]


def grads(tiles, arrays, acc, kacc, vacc):
    smem, vmem = pl.BlockSpec(memory_space=pltpu.SMEM), pl.BlockSpec(memory_space=VMEM)
    first = 1 + len(arrays)
    out = pl.pallas_call(
        grad_kernel,
        out_shape=[
            VMEM(acc.shape, F32),
            VMEM(kacc.shape, F32),
            VMEM(vacc.shape, F32),
            VMEM((4, 4, HALF, D), BF16),
            VMEM((4, 4, HALF, D), BF16),
        ],
        in_specs=[smem] + [vmem] * (len(arrays) + 3),
        out_specs=[vmem] * 5,
        scratch_shapes=[VMEM((UNROLL, HEADS, BLOCK, BLOCK), BF16)] * 2,
        input_output_aliases={first: 0, first + 1: 1, first + 2: 2},
        compiler_params=pltpu.CompilerParams(vmem_limit_bytes=12 * 2**20),
        name="grads",
    )(tiles, *arrays, acc, kacc, vacc)
    return out[0], out[3], out[4]


class HalfReduce:
    def __init__(self, links, base, buf, land, quarters, out, first, second):
        self.links, self.base, self.buf, self.land, self.quarters, self.out = links, base, buf, land, quarters, out
        self.me1, self.up1, self.down1 = first
        self.me2, self.up2, self.down2 = second

    def at(self, d1, d2):
        return ahead(self.me2, d2), ahead(self.me1, d1)

    def send(self, d1, d2, channel, src, to):
        self.links.start(self.base + channel, src, self.land.at[channel], to)

    def landed(self, channel):
        self.links.arrive(self.base + channel, self.land.at[channel])
        return self.land[channel].astype(F32)

    def own(self):
        for d1 in range(4):
            self.send(d1, 2, 12 + d1, self.buf.at[self.at(d1, 2)], self.up2 if d1 < 2 else self.down2)
        for d1 in range(4):
            up = d1 >= 2
            d2, channel = (1, 4 + d1) if up else (3, 8 + d1)
            self.send(d1, d2, channel, self.buf.at[self.at(d1, d2)], self.up2 if up else self.down2)

    def middle(self):
        for d1 in (2, 0, 3, 1):
            up = d1 < 2
            d2, channel = (1, 4 + d1) if up else (3, 8 + d1)
            total = self.buf[self.at(d1, d2)].astype(F32) + self.landed(12 + d1)
            self.out[d1] = total.astype(BF16)
            self.send(d1, d2, channel, self.out.at[d1], self.up2 if up else self.down2)

    def row(self, d1):
        return self.buf[self.at(d1, 0)].astype(F32) + self.landed(4 + d1) + self.landed(8 + d1)

    def cross(self):
        self.out[4] = self.row(2).astype(BF16)
        for q, to in ((0, self.up1), (1, self.down1)):
            rows = pl.ds(q * QUARTER, QUARTER)
            self.links.start(self.base + 2 + q, self.out.at[4, rows], self.quarters.at[rows], to)

    def finals(self):
        up, down = self.row(1), self.row(3)
        self.links.arrive(self.base + 2, self.quarters.at[pl.ds(0, QUARTER)])
        self.out[5, :QUARTER] = (up[:QUARTER] + self.quarters[:QUARTER].astype(F32)).astype(BF16)
        self.out[5, QUARTER:] = up[QUARTER:].astype(BF16)
        self.send(1, 0, 0, self.out.at[5], self.up1)
        self.links.arrive(self.base + 3, self.quarters.at[pl.ds(QUARTER, QUARTER)])
        self.out[6, :QUARTER] = down[:QUARTER].astype(BF16)
        self.out[6, QUARTER:] = (down[QUARTER:] + self.quarters[QUARTER:].astype(F32)).astype(BF16)
        self.send(3, 0, 1, self.out.at[6], self.down1)

    def result(self):
        return self.row(0) + self.landed(0) + self.landed(1)


def reduce_kernel(
    p_ref, low_ref, high_ref, wq_ref, attn_ref, grad_ref,
    to_sib, from_sib, sums, land, kland, quarters, ksums, send, recv,
):
    x, y, z, core, _ = place()
    xp, xm, yp, ym, zp, zm, sib = neighbours()
    links = Links(send, recv, sib)
    begin = enter()
    order = [2, 1, 3, 0]
    part = lambda c: pl.ds(c * D, D)
    parts = [(0, 0), (0, 1), (1, 1), (2, 0), (1, 0), (2, 1), (3, 0), (3, 1)]
    rings = [
        HalfReduce(links, 16, low_ref, kland.at[0], quarters.at[0], ksums.at[0], (x, xp, xm), (y, yp, ym)),
        HalfReduce(links, 32, high_ref, kland.at[1], quarters.at[1], ksums.at[1], (y, yp, ym), (x, xp, xm)),
    ]

    def block(i, c, mine):
        return p_ref[ahead(z, order[i]) * 2 + (core if mine else 1 - core), part(c)]

    for i, c in parts:
        to_sib[i, c] = block(i, c, False).astype(BF16)
    begin()
    for i, c in parts[:4]:
        links.start(8 + 2 * i + c, to_sib.at[i, c], from_sib.at[i, c], sib)
    for ring in rings:
        ring.own()
    for i, c in parts[4:]:
        links.start(8 + 2 * i + c, to_sib.at[i, c], from_sib.at[i, c], sib)

    def both(i, c):
        links.arrive(8 + 2 * i + c, from_sib.at[i, c])
        return block(i, c, True) + from_sib[i, c].astype(F32)

    def put(channel, i, c, value, to):
        sums[i, c] = value.astype(BF16)
        links.start(channel, sums.at[i, c], land.at[channel], to)

    def landed(channel):
        links.arrive(channel, land.at[channel])
        return land[channel].astype(F32)

    put(0, 0, 0, both(0, 0), zp)
    put(1, 0, 1, both(0, 1), zm)
    put(2, 1, 1, both(1, 1), zp)
    put(3, 2, 0, both(2, 0), zm)
    for ring in rings:
        ring.middle()
    up, down = both(1, 0), both(2, 1)
    put(4, 1, 0, up + landed(0), zp)
    put(5, 2, 1, down + landed(1), zm)
    for ring in rings:
        ring.cross()
    for ring in rings:
        ring.finals()
    outputs = both(3, 0) + landed(3) + landed(4)
    attn_ref[...] = outputs.T.astype(BF16)
    queries = both(3, 1) + landed(2) + landed(5)
    nodes = dot(wq_ref[...], (queries * SCALE).astype(BF16)).T
    for half, ring in enumerate(rings):
        rows = slice(half * HALF, (half + 1) * HALF)
        grad_ref[rows] = (nodes[rows] + ring.result()).astype(BF16)
    links.finish()


def reduce(parts, low, high, w_query):
    vmem = pl.BlockSpec(memory_space=VMEM)
    block = (2, D, BLOCK)
    return pl.pallas_call(
        reduce_kernel,
        out_shape=[jax.ShapeDtypeStruct((BLOCK, D), BF16)] * 2,
        in_specs=[vmem] * 4,
        out_specs=[vmem] * 2,
        scratch_shapes=[
            VMEM((4, *block), BF16),
            VMEM((4, *block), BF16),
            VMEM((3, *block), BF16),
            VMEM((6, D, BLOCK), BF16),
            VMEM((2, 16, HALF, D), BF16),
            VMEM((2, HALF, D), BF16),
            VMEM((2, 7, HALF, D), BF16),
            pltpu.SemaphoreType.DMA((48,)),
            pltpu.SemaphoreType.DMA((48,)),
        ],
        compiler_params=pltpu.CompilerParams(
            collective_id=2, has_side_effects=True, vmem_limit_bytes=24 * 2**20
        ),
        name="reduce",
    )(parts, low, high, w_query)


def local(features, cotangent, w_query, w_key, w_value, tile_coords, tile_count, mask_table):
    masks = mask_table.transpose(0, 2, 1)
    coords = tile_coords.transpose(0, 3, 1, 2)
    found = gather(features, cotangent, w_query, w_key, w_value, masks, coords, tile_count)
    qt, gt, qn, gn, keys, values = (a.reshape(-1, *a.shape[2:]) for a in found[:6])
    masks, wq, wk, wv, coords, coords2, count2 = found[6:]
    partial, tiles = stats(tile_count, coords, count2, coords2, qt, gt, keys, values, masks)
    fin, acc, kacc, vacc, keys_t, values_t, wkt, wvt = merge(partial, keys, values, wk, wv)
    arrays = (qt, gt, qn, gn, keys, values, keys_t, values_t, masks, fin, wkt, wvt)
    parts, low, high = grads(tiles, arrays, acc, kacc, vacc)
    return tuple(reduce(parts, low, high, wq))


def solution(mesh):
    return jax.shard_map(
        local,
        mesh=mesh,
        in_specs=(
            P(("reader", "blk"), None),
            P(("reader", "blk"), None),
            P(),
            P(),
            P(),
            P("reader", "blk", None, None),
            P("reader", "blk"),
            P(),
        ),
        out_specs=(P(("reader", "blk"), None), P(("reader", "blk"), None)),
        check_vma=False,
    )
```

time: 88 us -> 75 us (0.85)
  the two profiles are of different devices: /device:TPU:8 before, /device:TPU:0 now
where the time goes in v4:
time: 75 us; the launch traced here: 73.8 us
  Pallas kernels  71.2 us (95%)
  between operations  1.32 us (2%)
  local copies, waits for them, and re-layouts  1.31 us (2%)
    pallas_call x1, Pallas kernels, gather(): pl.pallas_call(gather_kernel, out_shape=[VMEM((4, 2, D, BLOCK), BF16), VM...  25.4 us
    pallas_call x1, Pallas kernels, reduce(): pl.pallas_call(reduce_kernel, out_shape=[jax.ShapeDtypeStruct((BLOCK, D),...  23.1 us
    pallas_call x1, Pallas kernels, merge(): pl.pallas_call(merge_kernel, out_shape=[VMEM(partial.shape, F32), VMEM((n...  9.2 us
    pallas_call x1, Pallas kernels, grads(): pl.pallas_call(grad_kernel, out_shape=[VMEM(acc.shape, F32), VMEM(kacc.sh...  8.91 us
    pallas_call x1, Pallas kernels, stats(): pl.pallas_call(stats_kernel, out_shape=[VMEM((nb, 2 * HEADS, BLOCK), F32)...  4.59 us

profile of v4, /device:TPU:0, one launch (start us, length us, event | category | flops | bytes accessed | tf_op | source)
XLA Modules:
  0.0 73.8 jit_solution(9631502280538774373)
XLA Ops:
  1.3 25.4 %gather.1 = (bf16[4,2,512,128]{3,2,1,0:T(8,128)(2,1)S(1)}, bf16[4,2,512,128]{3,2,1,0:T(8,128)(2,1)S(1)}, bf16[4,2,128,512]{3,2,1,0:T(8,128)(2,1)S(1)}, bf16[4,2,...) custom-call(bf16[128,512]{1,0:T(8,128)(2,1)} %x_hbm.1, ...), custom_call_target="tpu_custom_call" | custom-call | tf_op jit(solution)/shard_map/gather/pallas_call | solution.py:265
  26.7 4.6 %stats.1 = (f32[8,16,128]{2,1,0:T(8,128)S(1)}, s32[8,68]{1,0:T(8,128)S(1)}) custom-call(s32[1,1]{1,0:T(1,128)S(6)} %copy.18.count_ref, s32[1,3,1,32]{3,2,1,0:T(1,128)S(1)} %get-tuple-element.28.coords_ref, s32[8,128]{1,0:T(8,128)S(1)} %get-tuple-element.29.count2_ref, s32[1,3,1,32]{3,2,1,0:T(1,128)S(1)} %get-tuple-element.30.coords2_ref, ...), custom_call_target="tpu_custom_call" | custom-call | tf_op jit(solution)/shard_map/stats/pallas_call | solution.py:389
  31.3 9.2 %merge.1 = (f32[8,16,128]{2,1,0:T(8,128)S(1)}, f32[8,1024,128]{2,1,0:T(8,128)S(1)}, f32[16,128,512]{2,1,0:T(8,128)S(1)}, f32[16,128,512]{2,1,0:T(8,128)S(1)}, bf...) custom-call(f32[8,16,128]{2,1,0:T(8,128)S(1)} %get-tuple-element.39., ...), custom_call_target="tpu_custom_call" | custom-call | tf_op jit(solution)/shard_map/merge/pallas_call | solution.py:467
  40.5 8.9 %grads.1 = (f32[8,1024,128]{2,1,0:T(8,128)S(1)}, f32[16,128,512]{2,1,0:T(8,128)S(1)}, f32[16,128,512]{2,1,0:T(8,128)S(1)}, bf16[4,4,64,512]{3,2,1,0:T(8,128)(2,1)S(1)}, bf16[4,4,64,512]{3,2,1,0:T(8,128)(2,1)S(1)}) custom-call(s32[8,68]{1,0:T(8,128)S(1)} %get-tuple-element.36.list_ref, ...), custom_call_target="tpu_custom_call", output_to_operand_aliasing={{0}: (13, {}), {1}: (14, {}), {2}: (15, {})} | custom-call | tf_op jit(solution)/shard_map/grads/pallas_call | solution.py:556
  49.4 23.1 %reduce.1 = (bf16[128,512]{1,0:T(8,128)(2,1)S(1)}, bf16[128,512]{1,0:T(8,128)(2,1)S(1)}) custom-call(f32[8,1024,128]{2,1,0:T(8,128)S(1)} %get-tuple-element.50.p_ref, bf16[4,4,64,512]{3,2,1,0:T(8,128)(2,1)S(1)} %get-tuple-element.51.low_ref, bf16[4,4,64,512]{3,2,1,0:T(8,128)(2,1)S(1)} %get-tuple-element.52.high_ref, ...), custom_call_target="tpu_custom_call" | custom-call | tf_op jit(solution)/shard_map/reduce/pallas_call | solution.py:698
  72.5 0.7 copy.19
  73.2 0.7 copy.20

commit v5 on v4

--- a/solution.py
+++ b/solution.py
@@ -151,7 +151,7 @@
         for i, (src, dst) in enumerate(
             [
                 (x_hbm.at[pl.ds(0, HALF)], low.at[y, x]), (x_hbm.at[pl.ds(HALF, HALF)], high.at[x, y]),
-                (wk_hbm, wk_ref), (wv_hbm, wv_ref), (x_hbm, xb.at[z, core]), (g_hbm, gn_ref.at[z, core]),
+                (x_hbm, xb.at[z, core]), (g_hbm, gn_ref.at[z, core]), (wk_hbm, wk_ref), (wv_hbm, wv_ref),
                 (wq_hbm, wq_ref), (mask_hbm, mask_ref), (coords_hbm, coords_own),
             ]
         )
@@ -159,19 +159,21 @@
     for load in loads:
         load.start()
     rings = [
-        HalfGather(links, 16, low, x_hbm.at[pl.ds(0, HALF)], (x, xp, xm), (y, yp, ym)),
-        HalfGather(links, 32, high, x_hbm.at[pl.ds(HALF, HALF)], (y, yp, ym), (x, xp, xm)),
+        HalfGather(links, 16, low, low.at[y, x], (x, xp, xm), (y, yp, ym)),
+        HalfGather(links, 32, high, high.at[x, y], (y, yp, ym), (x, xp, xm)),
     ]
+    for i in range(4):
+        loads[i].wait()
     begin()
 
     for ring in rings:
         ring.own()
-    links.start(0, x_hbm, xb.at[z, core], zp)
-    links.start(2, x_hbm, xb.at[z, core], zm)
-    links.start(1, g_hbm, gn_ref.at[z, core], zp)
-    links.start(3, g_hbm, gn_ref.at[z, core], zm)
-    links.start(8, x_hbm, xb.at[z, core], sib)
-    links.start(9, g_hbm, gn_ref.at[z, core], sib)
+    links.start(0, xb.at[z, core], xb.at[z, core], zp)
+    links.start(2, xb.at[z, core], xb.at[z, core], zm)
+    links.start(1, gn_ref.at[z, core], gn_ref.at[z, core], zp)
+    links.start(3, gn_ref.at[z, core], gn_ref.at[z, core], zm)
+    links.start(8, xb.at[z, core], xb.at[z, core], sib)
+    links.start(9, gn_ref.at[z, core], gn_ref.at[z, core], sib)
     other = device(x + 1 - 2 * side, y, z, core)
     links.start(6, coords_hbm, coords_out, other)
     links.start(7, count_buf, count_out, other)
@@ -203,8 +205,6 @@
             else:
                 out[:, at, :HALF] = found
 
-    for i in range(7):
-        loads[i].wait()
     for ring in rings:
         ring.near()
     for ring in rings:
@@ -219,6 +219,8 @@
     pass_on(10, xb, 3, sib)
     arrive(2, xb, 1)
     pass_on(12, xb, 1, sib)
+    for i in range(4, 7):
+        loads[i].wait()
     project(0, 0)
     project(1, 0)
 
@@ -316,10 +318,16 @@
 
 UNROLL = 4
 LIST = 2 * 32 + UNROLL
+KEPT = 32
+
+
+def unpacked(word):
+    return word & 7, lax.shift_right_logical(word, 3) & 15, lax.shift_right_logical(word, 8), lax.shift_right_logical(word, 7) & 1
 
 
 def stats_kernel(
-    count_ref, coords_ref, count2_ref, coords2_ref, qt_ref, gt_ref, k_ref, v_ref, mask_ref, out_ref, list_ref, run
+    count_ref, coords_ref, count2_ref, coords2_ref, qt_ref, gt_ref, k_ref, v_ref, mask_ref,
+    out_ref, list_ref, kept_e, kept_d, peaks_ref, run,
 ):
     nb = run.shape[0]
     row = lax.broadcasted_iota(jnp.int32, run.shape, 1)
@@ -329,11 +337,9 @@
     def collect(counts, coords, column, found):
         def one(i, found):
             qb, kb, p = (coords[0, c, 0, i] for c in range(3))
-            list_ref[0, found] = lax.shift_right_logical(qb, 2) * 2 + (qb & 1)
-            list_ref[1, found] = (lax.shift_right_logical(kb, 2) * 2 + column) * 4 + (kb & 3)
-            list_ref[2, found] = p
-            list_ref[3, found] = jnp.where(i + found + (column != side) == 0, 1, 0)
-            list_ref[4, found] = 1
+            key = lax.shift_right_logical(kb, 2) * 8 + column * 4 + (kb & 3)
+            first = jnp.where(i + found + (column != side) == 0, 128, 0)
+            list_ref[found] = lax.shift_right_logical(qb, 2) * 2 + (qb & 1) + key * 8 + first + p * 256
             return found + jnp.where((lax.shift_right_logical(qb, 1) & 1) == side, 1, 0)
 
         return lax.fori_loop(0, counts[0, 0], one, found)
@@ -341,27 +347,32 @@
     count = collect(count_ref, coords_ref, side, 0)
     count = collect(count2_ref, coords2_ref, 1 - side, count)
     for u in range(UNROLL):
-        for i in range(5):
-            list_ref[i, count + u] = 0
-    list_ref[5, 0] = count
+        list_ref[count + u] = 0
+    list_ref[LIST] = count
 
     def tile(t):
-        qb, kb, p = (list_ref[c, t] for c in range(3))
-        bias = tile_bias(mask_ref[p], list_ref[3, t], list_ref[4, t])
+        qb, kb, p, first = unpacked(list_ref[t])
+        bias = tile_bias(mask_ref[p], first, jnp.where(t < count, 1, 0))
+        slot = jnp.minimum(t, KEPT)
         peaks, totals, dots = [], [], []
         for pair in range(HEADS // 2):
             two = slice(pair * 128, pair * 128 + 128)
             s2 = pair_product(k_ref[kb, :, two], qt_ref[qb, two])
             d2 = pair_product(v_ref[kb, :, two], gt_ref[qb, two])
             for half in range(2):
+                h = 2 * pair + half
                 lanes = slice(half * BLOCK, (half + 1) * BLOCK)
                 s = s2[:, lanes] + bias
                 peak = jnp.max(s, axis=0, keepdims=True)
                 e = jnp.exp(s - peak)
+                kept_e[slot, h] = e.astype(BF16)
+                kept_d[slot, h] = d2[:, lanes].astype(BF16)
                 peaks.append(peak)
                 totals.append(jnp.sum(e, axis=0, keepdims=True))
                 dots.append(jnp.sum(e * d2[:, lanes], axis=0, keepdims=True))
-        return qb, *(jnp.concatenate(rows, axis=0) for rows in (peaks, totals, dots))
+        peak, total, dot_sum = (jnp.concatenate(rows, axis=0) for rows in (peaks, totals, dots))
+        peaks_ref[slot] = peak
+        return qb, peak, total, dot_sum
 
     def add(qb, peak, total, dots):
         before = run[qb, :HEADS]
@@ -388,17 +399,23 @@
     smem, vmem = pl.BlockSpec(memory_space=pltpu.SMEM), pl.BlockSpec(memory_space=VMEM)
     return pl.pallas_call(
         stats_kernel,
-        out_shape=[VMEM((nb, 2 * HEADS, BLOCK), F32), jax.ShapeDtypeStruct((8, LIST), jnp.int32)],
+        out_shape=[
+            VMEM((nb, 2 * HEADS, BLOCK), F32),
+            jax.ShapeDtypeStruct((LIST + 1,), jnp.int32),
+            VMEM((KEPT + 1, HEADS, BLOCK, BLOCK), BF16),
+            VMEM((KEPT + 1, HEADS, BLOCK, BLOCK), BF16),
+            VMEM((KEPT + 1, HEADS, BLOCK), F32),
+        ],
         in_specs=[smem] * 4 + [vmem] * 5,
-        out_specs=[vmem, smem],
+        out_specs=[vmem, smem, vmem, vmem, vmem],
         scratch_shapes=[VMEM((nb, 3 * HEADS, BLOCK), F32)],
-        compiler_params=pltpu.CompilerParams(vmem_limit_bytes=8 * 2**20),
+        compiler_params=pltpu.CompilerParams(vmem_limit_bytes=4 * 2**20),
         name="stats",
     )(count, coords, count2, coords2, qt, gt, keys, values, masks)
 
 
 def merge_kernel(
-    st_ref, k_ref, v_ref, wk_ref, wv_ref, out_ref, acc, kacc, vacc, kt_ref, vt_ref, wkt_ref, wvt_ref,
+    st_ref, k_ref, v_ref, wk_ref, wv_ref, kept_e, kept_d, out_ref, acc, kacc, vacc, kt_ref, vt_ref, wkt_ref, wvt_ref,
     land, fin, send, recv, fsend, frecv,
 ):
     x, y, z, core, _ = place()
@@ -461,7 +478,7 @@
         out_ref[source(d)] = fin[d]
 
 
-def merge(partial, keys, values, wk, wv):
+def merge(partial, keys, values, wk, wv, kept_e, kept_d):
     nb, nk = partial.shape[0], keys.shape[0]
     vmem = pl.BlockSpec(memory_space=VMEM)
     return pl.pallas_call(
@@ -476,7 +493,7 @@
             VMEM((D, D), BF16),
             VMEM((D, D), BF16),
         ],
-        in_specs=[vmem] * 5,
+        in_specs=[vmem] * 7,
         out_specs=[vmem] * 8,
         scratch_shapes=[
             VMEM(partial.shape, F32),
@@ -487,7 +504,7 @@
             collective_id=1, has_side_effects=True, vmem_limit_bytes=4 * 2**20
         ),
         name="merge",
-    )(partial, keys, values, wk, wv)
+    )(partial, keys, values, wk, wv, *(pltpu.with_memory_space_constraint(a, pltpu.VMEM) for a in (kept_e, kept_d)))
 
 
 def lane_split(block):
@@ -499,14 +516,14 @@
 
 
 def grad_kernel(
-    list_ref, qt_ref, gt_ref, qn_ref, gn_ref, k_ref, v_ref, kt_ref, vt_ref, mask_ref, fin_ref, wkt_ref,
-    wvt_ref, acc_in, kacc_in, vacc_in, acc, kacc, vacc, low_ref, high_ref, probs, dscores,
+    list_ref, qt_ref, gt_ref, qn_ref, gn_ref, k_ref, v_ref, kt_ref, vt_ref, mask_ref, fin_ref,
+    kept_e, kept_d, peaks_ref, acc_in, kacc_in, vacc_in, acc, kacc, vacc, probs, dscores,
 ):
-    count = list_ref[5, 0]
+    count = list_ref[LIST]
 
     def scores(t, u):
-        qb, kb, p = (list_ref[c, t] for c in range(3))
-        bias = tile_bias(mask_ref[p], list_ref[3, t], list_ref[4, t])
+        qb, kb, p, first = unpacked(list_ref[t])
+        bias = tile_bias(mask_ref[p], first, jnp.where(t < count, 1, 0))
         for pair in range(HEADS // 2):
             two = slice(pair * 128, pair * 128 + 128)
             s2 = pair_product(k_ref[kb, :, two], qt_ref[qb, two])
@@ -519,8 +536,17 @@
                 delta = fin_ref[qb, HEADS + h : HEADS + h + 1]
                 dscores[u, h] = (prob * (d2[:, lanes] - delta)).astype(BF16)
 
+    def kept_scores(t, u):
+        qb = unpacked(list_ref[t])[0]
+        factor = jnp.exp(peaks_ref[t] - fin_ref[qb, :HEADS])
+        for h in range(HEADS):
+            prob = kept_e[t, h].astype(F32) * factor[h : h + 1]
+            probs[u, h] = prob.astype(BF16)
+            delta = fin_ref[qb, HEADS + h : HEADS + h + 1]
+            dscores[u, h] = (prob * (kept_d[t, h].astype(F32) - delta)).astype(BF16)
+
     def products(t, u):
-        qb, kb = list_ref[0, t], list_ref[1, t]
+        qb, kb = unpacked(list_ref[t])[:2]
         for pair in range(HEADS // 2):
             for h in (2 * pair, 2 * pair + 1):
                 head = slice(h * HEAD_DIM, (h + 1) * HEAD_DIM)
@@ -533,43 +559,36 @@
             kacc[kb, :, two] += dot(ds, lane_split(qn_ref[qb, :, two]))
             vacc[kb, :, two] += dot(low, lane_split(gn_ref[qb, :, two]))
 
-    def step(g, carry):
+    def step(find, g, carry):
         for u in range(UNROLL):
-            scores(g * UNROLL + u, u)
+            find(g * UNROLL + u, u)
         for u in range(UNROLL):
             products(g * UNROLL + u, u)
         return carry
 
-    lax.fori_loop(0, (count + UNROLL - 1) // UNROLL, step, 0)
-    for x in range(4):
-        rows = pl.ds(x * 4, 4)
-        keys = kacc[rows].reshape(4 * BLOCK, D).astype(BF16)
-        values = vacc[rows].reshape(4 * BLOCK, D).astype(BF16)
-        total = (dot(keys, wkt_ref[...]) + dot(values, wvt_ref[...])).reshape(4, BLOCK, D).astype(BF16)
-        low_ref[:, x] = total[:, :HALF]
-        high_ref[x] = total[:, HALF:]
+    groups = (count + UNROLL - 1) // UNROLL
+    kept = jnp.minimum(groups, KEPT // UNROLL)
+    lax.fori_loop(0, kept, functools.partial(step, kept_scores), 0)
+    lax.fori_loop(kept, groups, functools.partial(step, scores), 0)
 
 
 def grads(tiles, arrays, acc, kacc, vacc):
     smem, vmem = pl.BlockSpec(memory_space=pltpu.SMEM), pl.BlockSpec(memory_space=VMEM)
     first = 1 + len(arrays)
-    out = pl.pallas_call(
+    return pl.pallas_call(
         grad_kernel,
         out_shape=[
             VMEM(acc.shape, F32),
             VMEM(kacc.shape, F32),
             VMEM(vacc.shape, F32),
-            VMEM((4, 4, HALF, D), BF16),
-            VMEM((4, 4, HALF, D), BF16),
         ],
         in_specs=[smem] + [vmem] * (len(arrays) + 3),
-        out_specs=[vmem] * 5,
+        out_specs=[vmem] * 3,
         scratch_shapes=[VMEM((UNROLL, HEADS, BLOCK, BLOCK), BF16)] * 2,
         input_output_aliases={first: 0, first + 1: 1, first + 2: 2},
-        compiler_params=pltpu.CompilerParams(vmem_limit_bytes=12 * 2**20),
+        compiler_params=pltpu.CompilerParams(vmem_limit_bytes=5 * 2**20),
         name="grads",
     )(tiles, *arrays, acc, kacc, vacc)
-    return out[0], out[3], out[4]
 
 
 class HalfReduce:
@@ -588,9 +607,11 @@
         self.links.arrive(self.base + channel, self.land.at[channel])
         return self.land[channel].astype(F32)
 
-    def own(self):
+    def first(self):
         for d1 in range(4):
             self.send(d1, 2, 12 + d1, self.buf.at[self.at(d1, 2)], self.up2 if d1 < 2 else self.down2)
+
+    def second(self):
         for d1 in range(4):
             up = d1 >= 2
             d2, channel = (1, 4 + d1) if up else (3, 8 + d1)
@@ -629,8 +650,8 @@
 
 
 def reduce_kernel(
-    p_ref, low_ref, high_ref, wq_ref, attn_ref, grad_ref,
-    to_sib, from_sib, sums, land, kland, quarters, ksums, send, recv,
+    p_ref, kacc, vacc, wkt_ref, wvt_ref, outputs_ref, queries_ref, nodes_ref,
+    low, high, to_sib, from_sib, sums, land, kland, quarters, ksums, send, recv,
 ):
     x, y, z, core, _ = place()
     xp, xm, yp, ym, zp, zm, sib = neighbours()
@@ -640,21 +661,32 @@
     part = lambda c: pl.ds(c * D, D)
     parts = [(0, 0), (0, 1), (1, 1), (2, 0), (1, 0), (2, 1), (3, 0), (3, 1)]
     rings = [
-        HalfReduce(links, 16, low_ref, kland.at[0], quarters.at[0], ksums.at[0], (x, xp, xm), (y, yp, ym)),
-        HalfReduce(links, 32, high_ref, kland.at[1], quarters.at[1], ksums.at[1], (y, yp, ym), (x, xp, xm)),
+        HalfReduce(links, 16, low, kland.at[0], quarters.at[0], ksums.at[0], (x, xp, xm), (y, yp, ym)),
+        HalfReduce(links, 32, high, kland.at[1], quarters.at[1], ksums.at[1], (y, yp, ym), (x, xp, xm)),
     ]
 
     def block(i, c, mine):
         return p_ref[ahead(z, order[i]) * 2 + (core if mine else 1 - core), part(c)]
 
-    for i, c in parts:
+    def weigh(half, d):
+        at = ahead(x if half else y, d)
+        total = 0.0
+        for found, weight in ((kacc, wkt_ref), (vacc, wvt_ref)):
+            rows = found[at, :, HALF:] if half else found[:, at, :HALF]
+            total += dot(rows.reshape(4 * HALF, D).astype(BF16), weight[...])
+        (high if half else low)[at] = total.reshape(4, HALF, D).astype(BF16)
+
+    for i, c in parts[:4]:
         to_sib[i, c] = block(i, c, False).astype(BF16)
+    weigh(0, 2)
     begin()
     for i, c in parts[:4]:
         links.start(8 + 2 * i + c, to_sib.at[i, c], from_sib.at[i, c], sib)
-    for ring in rings:
-        ring.own()
+    rings[0].first()
+    weigh(1, 2)
+    rings[1].first()
     for i, c in parts[4:]:
+        to_sib[i, c] = block(i, c, False).astype(BF16)
         links.start(8 + 2 * i + c, to_sib.at[i, c], from_sib.at[i, c], sib)
 
     def both(i, c):
@@ -673,8 +705,14 @@
     put(1, 0, 1, both(0, 1), zm)
     put(2, 1, 1, both(1, 1), zp)
     put(3, 2, 0, both(2, 0), zm)
+    for half, ring in enumerate(rings):
+        weigh(half, 1)
+        weigh(half, 3)
+        ring.second()
     for ring in rings:
         ring.middle()
+    weigh(0, 0)
+    weigh(1, 0)
     up, down = both(1, 0), both(2, 1)
     put(4, 1, 0, up + landed(0), zp)
     put(5, 2, 1, down + landed(1), zm)
@@ -682,25 +720,24 @@
         ring.cross()
     for ring in rings:
         ring.finals()
-    outputs = both(3, 0) + landed(3) + landed(4)
-    attn_ref[...] = outputs.T.astype(BF16)
-    queries = both(3, 1) + landed(2) + landed(5)
-    nodes = dot(wq_ref[...], (queries * SCALE).astype(BF16)).T
+    outputs_ref[...] = both(3, 0) + landed(3) + landed(4)
+    queries_ref[...] = ((both(3, 1) + landed(2) + landed(5)) * SCALE).astype(BF16)
     for half, ring in enumerate(rings):
-        rows = slice(half * HALF, (half + 1) * HALF)
-        grad_ref[rows] = (nodes[rows] + ring.result()).astype(BF16)
+        nodes_ref[half * HALF : (half + 1) * HALF] = ring.result()
     links.finish()
 
 
-def reduce(parts, low, high, w_query):
+def reduce(parts, kacc, vacc, wkt, wvt):
     vmem = pl.BlockSpec(memory_space=VMEM)
     block = (2, D, BLOCK)
     return pl.pallas_call(
         reduce_kernel,
-        out_shape=[jax.ShapeDtypeStruct((BLOCK, D), BF16)] * 2,
-        in_specs=[vmem] * 4,
-        out_specs=[vmem] * 2,
+        out_shape=[VMEM((D, BLOCK), F32), VMEM((D, BLOCK), BF16), VMEM((BLOCK, D), F32)],
+        in_specs=[vmem] * 5,
+        out_specs=[vmem] * 3,
         scratch_shapes=[
+            VMEM((4, 4, HALF, D), BF16),
+            VMEM((4, 4, HALF, D), BF16),
             VMEM((4, *block), BF16),
             VMEM((4, *block), BF16),
             VMEM((3, *block), BF16),
@@ -715,7 +752,24 @@
             collective_id=2, has_side_effects=True, vmem_limit_bytes=24 * 2**20
         ),
         name="reduce",
-    )(parts, low, high, w_query)
+    )(parts, kacc.reshape(4, 4, BLOCK, D), vacc.reshape(4, 4, BLOCK, D), wkt, wvt)
+
+
+def finish_kernel(outputs_ref, queries_ref, nodes_ref, wq_ref, attn_ref, grad_ref):
+    attn_ref[...] = outputs_ref[...].T.astype(BF16)
+    grad_ref[...] = (dot(wq_ref[...], queries_ref[...]).T + nodes_ref[...]).astype(BF16)
+
+
+def finish(outputs, queries, nodes, w_query):
+    vmem = pl.BlockSpec(memory_space=VMEM)
+    return pl.pallas_call(
+        finish_kernel,
+        out_shape=[jax.ShapeDtypeStruct((BLOCK, D), BF16)] * 2,
+        in_specs=[vmem] * 4,
+        out_specs=[vmem] * 2,
+        compiler_params=pltpu.CompilerParams(vmem_limit_bytes=8 * 2**20),
+        name="finish",
+    )(outputs, queries, nodes, w_query)
 
 
 def local(features, cotangent, w_query, w_key, w_value, tile_coords, tile_count, mask_table):
@@ -724,11 +778,11 @@
     found = gather(features, cotangent, w_query, w_key, w_value, masks, coords, tile_count)
     qt, gt, qn, gn, keys, values = (a.reshape(-1, *a.shape[2:]) for a in found[:6])
     masks, wq, wk, wv, coords, coords2, count2 = found[6:]
-    partial, tiles = stats(tile_count, coords, count2, coords2, qt, gt, keys, values, masks)
-    fin, acc, kacc, vacc, keys_t, values_t, wkt, wvt = merge(partial, keys, values, wk, wv)
-    arrays = (qt, gt, qn, gn, keys, values, keys_t, values_t, masks, fin, wkt, wvt)
-    parts, low, high = grads(tiles, arrays, acc, kacc, vacc)
-    return tuple(reduce(parts, low, high, wq))
+    partial, tiles, *kept = stats(tile_count, coords, count2, coords2, qt, gt, keys, values, masks)
+    fin, acc, kacc, vacc, keys_t, values_t, wkt, wvt = merge(partial, keys, values, wk, wv, *kept[:2])
+    arrays = (qt, gt, qn, gn, keys, values, keys_t, values_t, masks, fin, *kept)
+    parts, kacc, vacc = grads(tiles, arrays, acc, kacc, vacc)
+    return tuple(finish(*reduce(parts, kacc, vacc, wkt, wvt), wq))
 
 
 def solution(mesh):

time: 75 us -> 70.9 us (0.945)
  Pallas kernels: 71.2 us -> 68.9 us
  local copies, waits for them, and re-layouts: 1.31 us -> 0 us
    pallas_call x1, Pallas kernels: 8.91 us -> 6.91 us  [grads(): pl.pallas_call(grad_kernel, out_shape=[VMEM(acc.shape, F32), VMEM(kacc.sh...]
    pallas_call x1, Pallas kernels: 4.59 us -> 5.98 us  [stats(): pl.pallas_call(stats_kernel, out_shape=[VMEM((nb, 2 * HEADS, BLOCK), F32)...]
    unnamed x2 -> x0, local copies, waits for them, and re-layouts: 1.31 us -> none
    pallas_call x1 -> x2, Pallas kernels: 23.1 us -> 22.1 us  [the longest x1 21 us: reduce(): pl.pallas_call(reduce_kernel, out_shape=[VMEM((D, BLOCK), F32), VMEM((D,...]
where the time goes in v5:
time: 70.9 us; the launch traced here: 70.2 us
  Pallas kernels  68.9 us (97%)
  between operations  1.32 us (2%)
    pallas_call x1, Pallas kernels, gather(): pl.pallas_call(gather_kernel, out_shape=[VMEM((4, 2, D, BLOCK), BF16), VM...  25.1 us
    pallas_call x1, Pallas kernels, reduce(): pl.pallas_call(reduce_kernel, out_shape=[VMEM((D, BLOCK), F32), VMEM((D,...  21 us
    pallas_call x1, Pallas kernels, merge(): pl.pallas_call(merge_kernel, out_shape=[VMEM(partial.shape, F32), VMEM((n...  8.87 us
    pallas_call x1, Pallas kernels, grads(): pl.pallas_call(grad_kernel, out_shape=[VMEM(acc.shape, F32), VMEM(kacc.sh...  6.91 us
    pallas_call x1, Pallas kernels, stats(): pl.pallas_call(stats_kernel, out_shape=[VMEM((nb, 2 * HEADS, BLOCK), F32)...  5.98 us

profile of v5, /device:TPU:0, one launch (start us, length us, event | category | flops | bytes accessed | tf_op | source)
XLA Modules:
  0.0 70.2 jit_solution(570244437257758582)
XLA Ops:
  1.3 25.1 %gather.1 = (bf16[4,2,512,128]{3,2,1,0:T(8,128)(2,1)S(1)}, bf16[4,2,512,128]{3,2,1,0:T(8,128)(2,1)S(1)}, bf16[4,2,128,512]{3,2,1,0:T(8,128)(2,1)S(1)}, bf16[4,2,...) custom-call(bf16[128,512]{1,0:T(8,128)(2,1)} %x_hbm.1, ...), custom_call_target="tpu_custom_call" | custom-call | tf_op jit(solution)/shard_map/gather/pallas_call | solution.py:267
  26.4 6.0 %stats.1 = (f32[8,16,128]{2,1,0:T(8,128)S(1)}, s32[69]{0:T(128)S(1)}, bf16[33,8,128,128]{3,2,1,0:T(8,128)(2,1)S(1)}, bf16[33,8,128,128]{3,2,1,0:T(8,128)(2,1)S(1)}, f32[33,8,128]{2,1,0:T(8,128)S(1)}) custom-call(s32[1,1]{1,0:T(1,128)S(6)} %copy.16.count_ref, s32[1,3,1,32]{3,2,1,0:T(1,128)S(1)} %get-tuple-element.34.coords_ref, ...), custom_call_target="tpu_custom_call" | custom-call | tf_op jit(solution)/shard_map/stats/pallas_call | solution.py:400
  32.4 8.9 %merge.1 = (f32[8,16,128]{2,1,0:T(8,128)S(1)}, f32[8,1024,128]{2,1,0:T(8,128)S(1)}, f32[16,128,512]{2,1,0:T(8,128)S(1)}, f32[16,128,512]{2,1,0:T(8,128)S(1)}, bf...) custom-call(f32[8,16,128]{2,1,0:T(8,128)S(1)} %get-tuple-element.45., ...), custom_call_target="tpu_custom_call" | custom-call | tf_op jit(solution)/shard_map/merge/pallas_call | solution.py:484
  41.3 6.9 %grads.1 = (f32[8,1024,128]{2,1,0:T(8,128)S(1)}, f32[16,128,512]{2,1,0:T(8,128)S(1)}, f32[16,128,512]{2,1,0:T(8,128)S(1)}) custom-call(s32[69]{0:T(128)S(1)} %get-tuple-element.42.list_ref, bf16[8,512,128]{2,1,0:T(8,128)(2,1)S(1)} %bitcast.19, bf16[8,512,128]{2,1,0:T(8,128)(2,1)S(1)} %bitcast.21, ...), custom_call_target="tpu_custom_call", output_to_operand_aliasing={{0}: (14, {}), {1}: (15, {}), {2}: (16, {})} | custom-call | tf_op jit(solution)/shard_map/grads/pallas_call | solution.py:578
  48.2 21.0 %reduce.1 = (f32[512,128]{1,0:T(8,128)S(1)}, bf16[512,128]{1,0:T(8,128)(2,1)S(1)}, f32[128,512]{1,0:T(8,128)S(1)}) custom-call(f32[8,1024,128]{2,1,0:T(8,128)S(1)} %get-tuple-element.57.p_ref, f32[4,4,128,512]{3,2,1,0:T(8,128)S(1)} %bitcast.16, f32[4,4,128,512]{3,2,1,0:T(8,128)S(1)} %bitcast.17, bf16[512,512]{1,0:T(8,128)(2,1)S(1)} %get-tuple-element.60.wkt_ref, ...), custom_call_target="tpu_custom_call" | custom-call | tf_op jit(solution)/shard_map/reduce/pallas_call | solution.py:733
  69.2 1.0 %finish.1 = (bf16[128,512]{1,0:T(8,128)(2,1)}, bf16[128,512]{1,0:T(8,128)(2,1)}) custom-call(f32[512,128]{1,0:T(8,128)S(1)} %get-tuple-element.62.outputs_ref, bf16[512,128]{1,0:T(8,128)(2,1)S(1)} %get-tuple-element.63.queries_ref, f32[128,512]{1,0:T(8,128)S(1)} %get-tuple-element.64.nodes_ref, bf16[512,512]{1,0:T(8,128)(2,1)S(1)} %get-tuple-element.65.wq_ref), custom_call_target="tpu_custom_call" | custom-call | tf_op jit(solution)/shard_map/finish/pallas_call | solution.py:765

commit v6 on v5

--- a/solution.py
+++ b/solution.py
@@ -97,24 +97,21 @@
     def quarter(self, d1, q):
         return self.buf.at[self.me2, ahead(self.me1, d1), pl.ds(q * QUARTER, QUARTER)]
 
-    def spread(self, d1, src=None):
+    def spread(self, d1):
         ref = self.piece(d1, 0)
-        self.links.start(self.base + 4 + d1, ref if src is None else src, ref, self.up2)
-        self.links.start(self.base + 8 + d1, ref if src is None else src, ref, self.down2)
+        self.links.start(self.base + 4 + d1, ref, ref, self.up2)
+        self.links.start(self.base + 8 + d1, ref, ref, self.down2)
 
     def own(self):
         ref = self.piece(0, 0)
         self.links.start(self.base, self.source, ref, self.up1)
         self.links.start(self.base + 1, self.source, ref, self.down1)
-        self.spread(0, self.source)
 
     def near(self):
         self.links.arrive(self.base, self.piece(3, 0))
         self.links.start(self.base + 2, self.quarter(3, 0), self.quarter(3, 0), self.up1)
-        self.spread(3)
         self.links.arrive(self.base + 1, self.piece(1, 0))
         self.links.start(self.base + 3, self.quarter(1, 1), self.quarter(1, 1), self.down1)
-        self.spread(1)
 
     def far(self):
         self.links.arrive(self.base + 2, self.quarter(2, 0))
@@ -168,6 +165,8 @@
 
     for ring in rings:
         ring.own()
+    for ring in rings:
+        ring.spread(0)
     links.start(0, xb.at[z, core], xb.at[z, core], zp)
     links.start(2, xb.at[z, core], xb.at[z, core], zm)
     links.start(1, gn_ref.at[z, core], gn_ref.at[z, core], zp)
@@ -208,13 +207,16 @@
     for ring in rings:
         ring.near()
     for ring in rings:
-        ring.relay(0)
+        ring.spread(3)
+        ring.spread(1)
     arrive(0, xb, 3)
     pass_on(4, xb, 3, zp)
     for ring in rings:
         ring.far()
     for ring in rings:
+        ring.relay(0)
         ring.relay(3)
+    for ring in rings:
         ring.relay(1)
     pass_on(10, xb, 3, sib)
     arrive(2, xb, 1)
@@ -248,12 +250,12 @@
         if i == 10:
             arrive(5, gn_ref, 2)
             pass_on(15, gn_ref, 2, sib)
+    arrive(14, xb, 2, 1 - core)
+    arrive(15, gn_ref, 2, 1 - core)
+    prepare(2)
     for half, ring in enumerate(rings):
         ring.last()
         project(half, 2)
-    arrive(14, xb, 2, 1 - core)
-    arrive(15, gn_ref, 2, 1 - core)
-    prepare(2)
     links.arrive(6, coords_out)
     links.arrive(7, count_out)
     loads[7].wait()
@@ -317,6 +319,7 @@
 
 
 UNROLL = 4
+WIDE = 8
 LIST = 2 * 32 + UNROLL
 KEPT = 32
 
@@ -382,12 +385,15 @@
         run[qb, HEADS : 2 * HEADS] = run[qb, HEADS : 2 * HEADS] * old + total * new
         run[qb, 2 * HEADS :] = run[qb, 2 * HEADS :] * old + dots * new
 
-    def step(g, carry):
-        for found in [tile(g * UNROLL + u) for u in range(UNROLL)]:
+    def step(width, g, carry):
+        for found in [tile(g * width + u) for u in range(width)]:
             add(*found)
         return carry
 
-    lax.fori_loop(0, (count + UNROLL - 1) // UNROLL, step, 0)
+    wide = count // WIDE
+    lax.fori_loop(0, wide, functools.partial(step, WIDE), 0)
+    groups = (count + UNROLL - 1) // UNROLL
+    lax.fori_loop(wide * (WIDE // UNROLL), groups, functools.partial(step, UNROLL), 0)
     for b in range(nb):
         total = jnp.maximum(run[b, HEADS : 2 * HEADS], 1e-30)
         out_ref[b, :HEADS] = run[b, :HEADS] + jnp.log(total)
@@ -451,7 +457,7 @@
     wkt_ref[...] = wk_ref[...].T
     wvt_ref[...] = wv_ref[...].T
     pl.semaphore_wait(barrier, nb - 1)
-    for d in range(1, nb):
+    for d in (4, 3, 5, 2, 6, 1, 7):
         part(d).start()
     land[0] = st_ref[me]
     lax.fori_loop(0, 16, turn, 0)
@@ -468,7 +474,7 @@
         dots += land[d, HEADS:] * weight
     fin[0, :HEADS] = m + jnp.log(total)
     fin[0, HEADS:] = dots / total
-    for d in range(1, nb):
+    for d in (4, 3, 5, 2, 6, 1, 7):
         whole(d).start()
     out_ref[me] = fin[0]
     lax.fori_loop(0, 16, clear, 0)
@@ -608,22 +614,20 @@
         return self.land[channel].astype(F32)
 
     def first(self):
-        for d1 in range(4):
+        for d1 in (1, 2, 0, 3):
             self.send(d1, 2, 12 + d1, self.buf.at[self.at(d1, 2)], self.up2 if d1 < 2 else self.down2)
 
-    def second(self):
-        for d1 in range(4):
-            up = d1 >= 2
-            d2, channel = (1, 4 + d1) if up else (3, 8 + d1)
-            self.send(d1, d2, channel, self.buf.at[self.at(d1, d2)], self.up2 if up else self.down2)
-
-    def middle(self):
-        for d1 in (2, 0, 3, 1):
-            up = d1 < 2
-            d2, channel = (1, 4 + d1) if up else (3, 8 + d1)
-            total = self.buf[self.at(d1, d2)].astype(F32) + self.landed(12 + d1)
-            self.out[d1] = total.astype(BF16)
-            self.send(d1, d2, channel, self.out.at[d1], self.up2 if up else self.down2)
+    def direct(self, d1):
+        up = d1 >= 2
+        d2, channel = (1, 4 + d1) if up else (3, 8 + d1)
+        self.send(d1, d2, channel, self.buf.at[self.at(d1, d2)], self.up2 if up else self.down2)
+
+    def middle(self, d1):
+        up = d1 < 2
+        d2, channel = (1, 4 + d1) if up else (3, 8 + d1)
+        total = self.buf[self.at(d1, d2)].astype(F32) + self.landed(12 + d1)
+        self.out[d1] = total.astype(BF16)
+        self.send(d1, d2, channel, self.out.at[d1], self.up2 if up else self.down2)
 
     def row(self, d1):
         return self.buf[self.at(d1, 0)].astype(F32) + self.landed(4 + d1) + self.landed(8 + d1)
@@ -701,23 +705,32 @@
         links.arrive(channel, land.at[channel])
         return land[channel].astype(F32)
 
-    put(0, 0, 0, both(0, 0), zp)
-    put(1, 0, 1, both(0, 1), zm)
-    put(2, 1, 1, both(1, 1), zp)
-    put(3, 2, 0, both(2, 0), zm)
     for half, ring in enumerate(rings):
         weigh(half, 1)
         weigh(half, 3)
-        ring.second()
-    for ring in rings:
-        ring.middle()
+        ring.direct(2)
+    put(0, 0, 0, both(0, 0), zp)
+    put(1, 0, 1, both(0, 1), zm)
+    for ring in rings:
+        ring.middle(2)
+        ring.direct(1)
+    put(2, 1, 1, both(1, 1), zp)
+    put(3, 2, 0, both(2, 0), zm)
+    for ring in rings:
+        ring.middle(1)
+        ring.direct(3)
+    for ring in rings:
+        ring.middle(3)
     weigh(0, 0)
     weigh(1, 0)
+    for ring in rings:
+        ring.cross()
+    for ring in rings:
+        ring.middle(0)
+        ring.direct(0)
     up, down = both(1, 0), both(2, 1)
     put(4, 1, 0, up + landed(0), zp)
     put(5, 2, 1, down + landed(1), zm)
-    for ring in rings:
-        ring.cross()
     for ring in rings:
         ring.finals()
     outputs_ref[...] = both(3, 0) + landed(3) + landed(4)

time: 70.9 us -> 72.5 us (1.023)
  Pallas kernels: 68.9 us -> 70.9 us
    pallas_call x1, Pallas kernels: 21 us -> 27.2 us  [reduce(): pl.pallas_call(reduce_kernel, out_shape=[VMEM((D, BLOCK), F32), VMEM((D,...]
    pallas_call x1, Pallas kernels: 6.91 us -> 3.83 us  [grads(): pl.pallas_call(grad_kernel, out_shape=[VMEM(acc.shape, F32), VMEM(kacc.sh...]
    pallas_call x1, Pallas kernels: 8.87 us -> 11.5 us  [merge(): pl.pallas_call(merge_kernel, out_shape=[VMEM(partial.shape, F32), VMEM((n...]
    pallas_call x1, Pallas kernels: 5.98 us -> 3.7 us  [stats(): pl.pallas_call(stats_kernel, out_shape=[VMEM((nb, 2 * HEADS, BLOCK), F32)...]
    pallas_call x1, Pallas kernels: 25.1 us -> 23.6 us  [gather(): pl.pallas_call(gather_kernel, out_shape=[VMEM((4, 2, D, BLOCK), BF16), VM...]
where the time goes in v6:
time: 72.5 us; the launch traced here: 72.2 us
  Pallas kernels  70.9 us (98%)
  between operations  1.32 us (2%)
    pallas_call x1, Pallas kernels, reduce(): pl.pallas_call(reduce_kernel, out_shape=[VMEM((D, BLOCK), F32), VMEM((D,...  27.2 us
    pallas_call x1, Pallas kernels, gather(): pl.pallas_call(gather_kernel, out_shape=[VMEM((4, 2, D, BLOCK), BF16), VM...  23.6 us
    pallas_call x1, Pallas kernels, merge(): pl.pallas_call(merge_kernel, out_shape=[VMEM(partial.shape, F32), VMEM((n...  11.5 us
    pallas_call x1, Pallas kernels, grads(): pl.pallas_call(grad_kernel, out_shape=[VMEM(acc.shape, F32), VMEM(kacc.sh...  3.83 us
    pallas_call x1, Pallas kernels, stats(): pl.pallas_call(stats_kernel, out_shape=[VMEM((nb, 2 * HEADS, BLOCK), F32)...  3.7 us

profile of v6, /device:TPU:0, one launch (start us, length us, event | category | flops | bytes accessed | tf_op | source)
XLA Modules:
  0.0 72.2 jit_solution(12009046184858283951)
XLA Ops:
  1.3 23.6 %gather.1 = (bf16[4,2,512,128]{3,2,1,0:T(8,128)(2,1)S(1)}, bf16[4,2,512,128]{3,2,1,0:T(8,128)(2,1)S(1)}, bf16[4,2,128,512]{3,2,1,0:T(8,128)(2,1)S(1)}, bf16[4,2,...) custom-call(bf16[128,512]{1,0:T(8,128)(2,1)} %x_hbm.1, ...), custom_call_target="tpu_custom_call" | custom-call | tf_op jit(solution)/shard_map/gather/pallas_call | solution.py:269
  24.9 3.7 %stats.1 = (f32[8,16,128]{2,1,0:T(8,128)S(1)}, s32[69]{0:T(128)S(1)}, bf16[33,8,128,128]{3,2,1,0:T(8,128)(2,1)S(1)}, bf16[33,8,128,128]{3,2,1,0:T(8,128)(2,1)S(1)}, f32[33,8,128]{2,1,0:T(8,128)S(1)}) custom-call(s32[1,1]{1,0:T(1,128)S(6)} %copy.16.count_ref, s32[1,3,1,32]{3,2,1,0:T(1,128)S(1)} %get-tuple-element.34.coords_ref, ...), custom_call_target="tpu_custom_call" | custom-call | tf_op jit(solution)/shard_map/stats/pallas_call | solution.py:406
  28.6 11.5 %merge.1 = (f32[8,16,128]{2,1,0:T(8,128)S(1)}, f32[8,1024,128]{2,1,0:T(8,128)S(1)}, f32[16,128,512]{2,1,0:T(8,128)S(1)}, f32[16,128,512]{2,1,0:T(8,128)S(1)}, bf...) custom-call(f32[8,16,128]{2,1,0:T(8,128)S(1)} %get-tuple-element.45., ...), custom_call_target="tpu_custom_call" | custom-call | tf_op jit(solution)/shard_map/merge/pallas_call | solution.py:490
  40.1 3.8 %grads.1 = (f32[8,1024,128]{2,1,0:T(8,128)S(1)}, f32[16,128,512]{2,1,0:T(8,128)S(1)}, f32[16,128,512]{2,1,0:T(8,128)S(1)}) custom-call(s32[69]{0:T(128)S(1)} %get-tuple-element.42.list_ref, bf16[8,512,128]{2,1,0:T(8,128)(2,1)S(1)} %bitcast.19, bf16[8,512,128]{2,1,0:T(8,128)(2,1)S(1)} %bitcast.21, ...), custom_call_target="tpu_custom_call", output_to_operand_aliasing={{0}: (14, {}), {1}: (15, {}), {2}: (16, {})} | custom-call | tf_op jit(solution)/shard_map/grads/pallas_call | solution.py:584
  44.0 27.2 %reduce.1 = (f32[512,128]{1,0:T(8,128)S(1)}, bf16[512,128]{1,0:T(8,128)(2,1)S(1)}, f32[128,512]{1,0:T(8,128)S(1)}) custom-call(f32[8,1024,128]{2,1,0:T(8,128)S(1)} %get-tuple-element.57.p_ref, f32[4,4,128,512]{3,2,1,0:T(8,128)S(1)} %bitcast.16, f32[4,4,128,512]{3,2,1,0:T(8,128)S(1)} %bitcast.17, bf16[512,512]{1,0:T(8,128)(2,1)S(1)} %get-tuple-element.60.wkt_ref, ...), custom_call_target="tpu_custom_call" | custom-call | tf_op jit(solution)/shard_map/reduce/pallas_call | solution.py:746
  71.2 1.0 %finish.1 = (bf16[128,512]{1,0:T(8,128)(2,1)}, bf16[128,512]{1,0:T(8,128)(2,1)}) custom-call(f32[512,128]{1,0:T(8,128)S(1)} %get-tuple-element.62.outputs_ref, bf16[512,128]{1,0:T(8,128)(2,1)S(1)} %get-tuple-element.63.queries_ref, f32[128,512]{1,0:T(8,128)S(1)} %get-tuple-element.64.nodes_ref, bf16[512,512]{1,0:T(8,128)(2,1)S(1)} %get-tuple-element.65.wq_ref), custom_call_target="tpu_custom_call" | custom-call | tf_op jit(solution)/shard_map/finish/pallas_call | solution.py:778

commit v7 on v6

--- a/solution.py
+++ b/solution.py
@@ -638,12 +638,15 @@
             rows = pl.ds(q * QUARTER, QUARTER)
             self.links.start(self.base + 2 + q, self.out.at[4, rows], self.quarters.at[rows], to)
 
-    def finals(self):
-        up, down = self.row(1), self.row(3)
+    def final_up(self):
+        up = self.row(1)
         self.links.arrive(self.base + 2, self.quarters.at[pl.ds(0, QUARTER)])
         self.out[5, :QUARTER] = (up[:QUARTER] + self.quarters[:QUARTER].astype(F32)).astype(BF16)
         self.out[5, QUARTER:] = up[QUARTER:].astype(BF16)
         self.send(1, 0, 0, self.out.at[5], self.up1)
+
+    def final_down(self):
+        down = self.row(3)
         self.links.arrive(self.base + 3, self.quarters.at[pl.ds(QUARTER, QUARTER)])
         self.out[6, :QUARTER] = down[:QUARTER].astype(BF16)
         self.out[6, QUARTER:] = (down[QUARTER:] + self.quarters[QUARTER:].astype(F32)).astype(BF16)
@@ -654,7 +657,7 @@
 
 
 def reduce_kernel(
-    p_ref, kacc, vacc, wkt_ref, wvt_ref, outputs_ref, queries_ref, nodes_ref,
+    p_ref, kacc, vacc, wq_ref, wkt_ref, wvt_ref, attn_ref, grad_ref,
     low, high, to_sib, from_sib, sums, land, kland, quarters, ksums, send, recv,
 ):
     x, y, z, core, _ = place()
@@ -732,22 +735,26 @@
     put(4, 1, 0, up + landed(0), zp)
     put(5, 2, 1, down + landed(1), zm)
     for ring in rings:
-        ring.finals()
-    outputs_ref[...] = both(3, 0) + landed(3) + landed(4)
-    queries_ref[...] = ((both(3, 1) + landed(2) + landed(5)) * SCALE).astype(BF16)
+        ring.final_up()
+    for ring in rings:
+        ring.final_down()
+    attn_ref[...] = (both(3, 0) + landed(3) + landed(4)).T.astype(BF16)
+    queries = ((both(3, 1) + landed(2) + landed(5)) * SCALE).astype(BF16)
+    nodes = dot(wq_ref[...], queries).T
     for half, ring in enumerate(rings):
-        nodes_ref[half * HALF : (half + 1) * HALF] = ring.result()
+        rows = slice(half * HALF, (half + 1) * HALF)
+        grad_ref[rows] = (nodes[rows] + ring.result()).astype(BF16)
     links.finish()
 
 
-def reduce(parts, kacc, vacc, wkt, wvt):
+def reduce(parts, kacc, vacc, wq, wkt, wvt):
     vmem = pl.BlockSpec(memory_space=VMEM)
     block = (2, D, BLOCK)
     return pl.pallas_call(
         reduce_kernel,
-        out_shape=[VMEM((D, BLOCK), F32), VMEM((D, BLOCK), BF16), VMEM((BLOCK, D), F32)],
-        in_specs=[vmem] * 5,
-        out_specs=[vmem] * 3,
+        out_shape=[VMEM((BLOCK, D), BF16)] * 2,
+        in_specs=[vmem] * 6,
+        out_specs=[vmem] * 2,
         scratch_shapes=[
             VMEM((4, 4, HALF, D), BF16),
             VMEM((4, 4, HALF, D), BF16),
@@ -765,24 +772,31 @@
             collective_id=2, has_side_effects=True, vmem_limit_bytes=24 * 2**20
         ),
         name="reduce",
-    )(parts, kacc.reshape(4, 4, BLOCK, D), vacc.reshape(4, 4, BLOCK, D), wkt, wvt)
-
-
-def finish_kernel(outputs_ref, queries_ref, nodes_ref, wq_ref, attn_ref, grad_ref):
-    attn_ref[...] = outputs_ref[...].T.astype(BF16)
-    grad_ref[...] = (dot(wq_ref[...], queries_ref[...]).T + nodes_ref[...]).astype(BF16)
-
-
-def finish(outputs, queries, nodes, w_query):
-    vmem = pl.BlockSpec(memory_space=VMEM)
+    )(parts, kacc.reshape(4, 4, BLOCK, D), vacc.reshape(4, 4, BLOCK, D), wq, wkt, wvt)
+
+
+def finish_kernel(attn_ref, grad_ref, attn_out, grad_out, sems):
+    copies = [
+        pltpu.make_async_copy(attn_ref, attn_out, sems.at[0]),
+        pltpu.make_async_copy(grad_ref, grad_out, sems.at[1]),
+    ]
+    for copy in copies:
+        copy.start()
+    for copy in copies:
+        copy.wait()
+
+
+def finish(attn, grad):
+    vmem, hbm = pl.BlockSpec(memory_space=VMEM), pl.BlockSpec(memory_space=pltpu.HBM)
     return pl.pallas_call(
         finish_kernel,
         out_shape=[jax.ShapeDtypeStruct((BLOCK, D), BF16)] * 2,
-        in_specs=[vmem] * 4,
-        out_specs=[vmem] * 2,
-        compiler_params=pltpu.CompilerParams(vmem_limit_bytes=8 * 2**20),
+        in_specs=[vmem] * 2,
+        out_specs=[hbm] * 2,
+        scratch_shapes=[pltpu.SemaphoreType.DMA((2,))],
+        compiler_params=pltpu.CompilerParams(vmem_limit_bytes=4 * 2**20),
         name="finish",
-    )(outputs, queries, nodes, w_query)
+    )(attn, grad)
 
 
 def local(features, cotangent, w_query, w_key, w_value, tile_coords, tile_count, mask_table):
@@ -795,7 +809,7 @@
     fin, acc, kacc, vacc, keys_t, values_t, wkt, wvt = merge(partial, keys, values, wk, wv, *kept[:2])
     arrays = (qt, gt, qn, gn, keys, values, keys_t, values_t, masks, fin, *kept)
     parts, kacc, vacc = grads(tiles, arrays, acc, kacc, vacc)
-    return tuple(finish(*reduce(parts, kacc, vacc, wkt, wvt), wq))
+    return tuple(finish(*reduce(parts, kacc, vacc, wq, wkt, wvt)))
 
 
 def solution(mesh):

time: 72.5 us -> 70.8 us (0.977)
  Pallas kernels: 70.9 us -> 69.3 us
    pallas_call x1, Pallas kernels: 27.2 us -> 24 us  [reduce(): pl.pallas_call(reduce_kernel, out_shape=[VMEM((BLOCK, D), BF16)] * 2, in_...]
    pallas_call x1, Pallas kernels: 11.5 us -> 13.5 us  [merge(): pl.pallas_call(merge_kernel, out_shape=[VMEM(partial.shape, F32), VMEM((n...]
where the time goes in v7:
time: 70.8 us
  Pallas kernels  69.3 us (98%)
  between operations  1.48 us (2%)
    pallas_call x1, Pallas kernels, reduce(): pl.pallas_call(reduce_kernel, out_shape=[VMEM((BLOCK, D), BF16)] * 2, in_...  24 us
    pallas_call x1, Pallas kernels, gather(): pl.pallas_call(gather_kernel, out_shape=[VMEM((4, 2, D, BLOCK), BF16), VM...  23.6 us
    pallas_call x1, Pallas kernels, merge(): pl.pallas_call(merge_kernel, out_shape=[VMEM(partial.shape, F32), VMEM((n...  13.5 us
    pallas_call x1, Pallas kernels, grads(): pl.pallas_call(grad_kernel, out_shape=[VMEM(acc.shape, F32), VMEM(kacc.sh...  3.83 us
    pallas_call x1, Pallas kernels, stats(): pl.pallas_call(stats_kernel, out_shape=[VMEM((nb, 2 * HEADS, BLOCK), F32)...  3.62 us

profile of v7, /device:TPU:0, one launch (start us, length us, event | category | flops | bytes accessed | tf_op | source)
XLA Modules:
  0.0 70.8 jit_solution(17671274342844858568)
XLA Ops:
  1.3 23.6 %gather.1 = (bf16[4,2,512,128]{3,2,1,0:T(8,128)(2,1)S(1)}, bf16[4,2,512,128]{3,2,1,0:T(8,128)(2,1)S(1)}, bf16[4,2,128,512]{3,2,1,0:T(8,128)(2,1)S(1)}, bf16[4,2,...) custom-call(bf16[128,512]{1,0:T(8,128)(2,1)} %x_hbm.1, ...), custom_call_target="tpu_custom_call" | custom-call | tf_op jit(solution)/shard_map/gather/pallas_call | solution.py:269
  24.9 3.6 %stats.1 = (f32[8,16,128]{2,1,0:T(8,128)S(1)}, s32[69]{0:T(128)S(1)}, bf16[33,8,128,128]{3,2,1,0:T(8,128)(2,1)S(1)}, bf16[33,8,128,128]{3,2,1,0:T(8,128)(2,1)S(1)}, f32[33,8,128]{2,1,0:T(8,128)S(1)}) custom-call(s32[1,1]{1,0:T(1,128)S(6)} %copy.16.count_ref, s32[1,3,1,32]{3,2,1,0:T(1,128)S(1)} %get-tuple-element.33.coords_ref, ...), custom_call_target="tpu_custom_call" | custom-call | tf_op jit(solution)/shard_map/stats/pallas_call | solution.py:406
  28.5 13.5 %merge.1 = (f32[8,16,128]{2,1,0:T(8,128)S(1)}, f32[8,1024,128]{2,1,0:T(8,128)S(1)}, f32[16,128,512]{2,1,0:T(8,128)S(1)}, f32[16,128,512]{2,1,0:T(8,128)S(1)}, bf...) custom-call(f32[8,16,128]{2,1,0:T(8,128)S(1)} %get-tuple-element.44., ...), custom_call_target="tpu_custom_call" | custom-call | tf_op jit(solution)/shard_map/merge/pallas_call | solution.py:490
  42.1 3.8 %grads.1 = (f32[8,1024,128]{2,1,0:T(8,128)S(1)}, f32[16,128,512]{2,1,0:T(8,128)S(1)}, f32[16,128,512]{2,1,0:T(8,128)S(1)}) custom-call(s32[69]{0:T(128)S(1)} %get-tuple-element.41.list_ref, bf16[8,512,128]{2,1,0:T(8,128)(2,1)S(1)} %bitcast.19, bf16[8,512,128]{2,1,0:T(8,128)(2,1)S(1)} %bitcast.21, ...), custom_call_target="tpu_custom_call", output_to_operand_aliasing={{0}: (14, {}), {1}: (15, {}), {2}: (16, {})} | custom-call | tf_op jit(solution)/shard_map/grads/pallas_call | solution.py:584
  45.9 24.0 %reduce.1 = (bf16[128,512]{1,0:T(8,128)(2,1)S(1)}, bf16[128,512]{1,0:T(8,128)(2,1)S(1)}) custom-call(f32[8,1024,128]{2,1,0:T(8,128)S(1)} %get-tuple-element.56.p_ref, f32[4,4,128,512]{3,2,1,0:T(8,128)S(1)} %bitcast.16, f32[4,4,128,512]{3,2,1,0:T(8,128)S(1)} %bitcast.17, bf16[512,512]{1,0:T(8,128)(2,1)S(1)} %get-tuple-element.59.wq_ref, ...), custom_call_target="tpu_custom_call" | custom-call | tf_op jit(solution)/shard_map/reduce/pallas_call | solution.py:753
  69.9 0.7 %finish.1 = (bf16[128,512]{1,0:T(8,128)(2,1)}, bf16[128,512]{1,0:T(8,128)(2,1)}) custom-call(bf16[128,512]{1,0:T(8,128)(2,1)S(1)} %get-tuple-element.62.attn_ref, bf16[128,512]{1,0:T(8,128)(2,1)S(1)} %get-tuple-element.63.grad_ref), custom_call_target="tpu_custom_call" | custom-call | tf_op jit(solution)/shard_map/finish/pallas_call | solution.py:791
